TPU v7x, 128 devices: a whole 4x4x4 slice. The times are simulated.
128 devices in a mesh: dp: 64 (over z, y, x), tensor: 2 (over core).
Axes of the slice: x: 4, y: 4, z: 4, core: 2. Of those that a mesh axis runs over, the one named last changes fastest.
Arguments:
- acts: bfloat16 [32768, 8192], P(('dp', 'tensor')), may hold values from -6 to 6
- out_grad: bfloat16 [32768, 1024], P('dp', 'tensor'), may hold values from -6 to 6
- weight: bfloat16 [8192, 1024], P(None, 'tensor'), may hold values from -0.0625 to 0.0625
- error: bfloat16 [524288, 1024], P('dp', 'tensor'), may hold values from -4 to 4
- momentum: bfloat16 [8192, 1024], P('dp', 'tensor'), may hold values from -2 to 2
- q_init: float32 [1024, 32], P('tensor'), may hold values from -6 to 6
Outputs:
- new_error: bfloat16 [524288, 1024], P('dp', 'tensor')
- new_momentum: bfloat16 [8192, 1024], P('dp', 'tensor')
- input_grad: bfloat16 [32768, 8192], P(('dp', 'tensor'))
All inputs are finite; a program needn't handle non-finite values.
Results may differ from a plain program's by a relative error of at most 0.01.
Values may be sent and summed in bfloat16 or wider, within the bound.
No kernel may reach another device: no remote copies, remote signals or barrier semaphores. Data moves between devices by JAX's collectives and lax.ppermute only.
A program may use at most 192 MiB of HBM per device.

v0:
```python
import jax
import jax.numpy as jnp
from jax import lax
from jax.sharding import PartitionSpec as P


def orthonormal(block):
    width = block.shape[1]

    def step(k, current):
        column = lax.dynamic_slice_in_dim(current, k, 1, 1)[:, 0]
        keep = (jnp.arange(width) < k).astype(jnp.float32)
        coeff = jnp.dot(column, current, precision=lax.Precision.HIGHEST) * keep
        column = column - jnp.dot(current, coeff, precision=lax.Precision.HIGHEST)
        column = column * lax.rsqrt(jnp.sum(column * column) + 1e-06)
        return lax.dynamic_update_slice_in_dim(current, column[:, None], k, 1)

    return lax.fori_loop(0, width, step, block)


def per_device(acts, out_grad, weight, error, momentum, q_init):
    token_count = out_grad.shape[0]
    scale = 1.0 / token_count**0.5
    grads = out_grad
    grad = jnp.einsum(
        "td,tc->dc",
        lax.all_gather(acts, "tensor", axis=0, tiled=True),
        grads,
        preferred_element_type=jnp.float32,
    )
    merged = grad * scale + error.astype(jnp.float32)
    project = jnp.dot(merged, q_init, precision=lax.Precision.HIGHEST)
    summed = lax.psum(project, "dp")
    basis = orthonormal(summed)
    replicas = lax.axis_size("dp")
    right = lax.psum(jnp.dot(merged.T, basis, precision=lax.Precision.HIGHEST), "dp") / replicas
    approx = jnp.dot(basis, right.T, precision=lax.Precision.HIGHEST)
    new_error = (merged - approx).astype(jnp.bfloat16)
    mom_rows = momentum.shape[0]
    approx_share = lax.dynamic_slice_in_dim(approx, lax.axis_index("dp") * mom_rows, mom_rows, 0)
    new_momentum = (0.9 * momentum.astype(jnp.float32) + approx_share).astype(jnp.bfloat16)
    grads = out_grad
    input_sum = lax.psum_scatter(
        lax.dot_general(
            grads, weight, (((1,), (1,)), ((), ())), preferred_element_type=jnp.float32
        ).astype(jnp.bfloat16),
        "tensor",
        scatter_dimension=0,
        tiled=True,
    )
    return (new_error, new_momentum, input_sum)


def solution(mesh):
    return jax.shard_map(
        per_device,
        mesh=mesh,
        in_specs=(
            P(("dp", "tensor"), None),
            P("dp", "tensor"),
            P(None, "tensor"),
            P("dp", "tensor"),
            P("dp", "tensor"),
            P("tensor", None),
        ),
        out_specs=(P("dp", "tensor"), P("dp", "tensor"), P(("dp", "tensor"), None)),
        check_vma=False,
    )
```

profile of v0, /device:TPU:0, one launch (start us, length us, event | category | flops | bytes accessed | tf_op | source)
XLA Modules:
  0.0 661.7 jit_solution(18221307158783074263)
XLA Ops:
  8.0 26.7 %all-gather.2.cloned.1.call-done = bf16[512,8192]{1,0:T(8,128)(2,1)} async-done(((bf16[256,8192]{1,0:T(8,128)(2,1)}), bf16[512,8192]{1,0:T(8,128)(2,1)}) %all-gather.2.cloned.1.call-update) | async-done | bytes 8388624 | tf_op jit(solution)/shard_map/all_gather | solution.py:27
  34.7 31.0 %convert_add_fusion = f32[8192,512]{1,0:T(8,128)S(1)} fusion(bf16[8192,512]{1,0:T(8,128)(2,1)} %param.11, bf16[512,8192]{1,0:T(8,128)(2,1)} %all-gather.2.cloned.1.call-done, bf16[512,512]{1,0:T(8,128)(2,1)S(1)} %copy-done), kind=kOutput, calls=%fused_computation.7 | convolution fusion | flops 4307550208 | bytes 34078720 | tf_op jit(solution)/shard_map/td,tc->dc/dot_general | solution.py:25
  65.7 5.7 copy-done.1
  71.4 16.3 %fusion.7 = f32[8192,32]{0,1:T(8,128)} fusion(f32[8192,512]{1,0:T(8,128)S(1)} %convert_add_fusion, f32[512,32]{0,1:T(8,128)S(1)} %copy-done.4), kind=kOutput, calls=%fused_computation.15 | convolution fusion | flops 1610612736 | bytes 17891328 | tf_op jit(solution)/shard_map/dot_general | solution.py:32
  88.0 131.0 %all-reduce.3.cloned.1.call-done = f32[8192,32]{0,1:T(8,128)} async-done(((f32[8192,32]{0,1:T(8,128)}), f32[8192,32]{0,1:T(8,128)}) %all-reduce.3.cloned.1.call-update) | async-done | bytes 1048592 | tf_op jit(solution)/shard_map/psum | solution.py:33
  219.0 260.8 %while.13 = (s32[]{:T(128)}, f32[8192,32]{0,1:T(8,128)}, s32[]{:T(128)}, f32[]{:T(128)}, s32[]{:T(128)}) while((s32[]{:T(128)}, f32[8192,32]{0,1:T(8,128)}, s32[]{:T(128)}, f32[]{:T(128)}, s32[]{:T(128)}) %tuple.37), condition=%wide.region_3.0_spmd, body=%wide.region_1.0_spmd.sunk | while | flops 6324290 | bytes 2458977 | solution.py:18
  219.0 2.2 fusion.29
  227.1 2.2 fusion.29
  235.3 2.2 fusion.29
  243.4 2.2 fusion.29
  251.6 2.2 fusion.29
  259.7 2.2 fusion.29
  267.8 2.2 fusion.29
  276.0 2.2 fusion.29
  284.1 2.2 fusion.29
  292.3 2.2 fusion.29
  300.4 2.2 fusion.29
  308.6 2.2 fusion.29
  316.8 2.2 fusion.29
  324.9 2.2 fusion.29
  333.1 2.2 fusion.29
  341.3 2.2 fusion.29
  349.4 2.2 fusion.29
  357.6 2.2 fusion.29
  365.7 2.2 fusion.29
  373.9 2.2 fusion.29
  382.0 2.2 fusion.29
  455.3 2.2 fusion.29
  479.8 29.6 %fusion.8 = f32[512,32]{1,0:T(8,128)} fusion(f32[8192,512]{1,0:T(8,128)} %copy-done.1, f32[8192,32]{0,1:T(8,128)} %get-tuple-element.52), kind=kOutput, calls=%fused_computation.16 | convolution fusion | flops 1610612736 | bytes 17891328 | tf_op jit(solution)/shard_map/dot_general | solution.py:36
  509.4 10.4 %convolution_convert_fusion = bf16[512,8192]{1,0:T(8,128)(2,1)} fusion(bf16[512,512]{1,0:T(8,128)(2,1)S(1)} %copy-done, bf16[8192,512]{1,0:T(8,128)(2,1)} %param.10), kind=kOutput, calls=%fused_computation.8 | convolution fusion | flops 4299161600 | bytes 17301504 | tf_op jit(solution)/shard_map/dot_general | solution.py:44
  519.8 112.5 %all-reduce.5.cloned.1.call-done = f32[512,32]{1,0:T(8,128)} async-done(((f32[512,32]{1,0:T(8,128)}), f32[512,32]{1,0:T(8,128)}) %all-reduce.5.cloned.1.call-update) | async-done | bytes 65552 | tf_op jit(solution)/shard_map/psum | solution.py:36
  632.3 21.2 %subtract_convert_fusion = (bf16[8192,512]{1,0:T(8,128)(2,1)}, f32[8192,512]{1,0:T(8,128)}) fusion(f32[8192,512]{1,0:T(8,128)} %copy-done.1, f32[8192,32]{0,1:T(8,128)S(1)} %copy-done.2, f32[512,32]{1,0:T(8,128)} %all-reduce.5.cloned.1.call-done), kind=kOutput, calls=%fused_computation.6 | convolution fusion | flops 1619017728 | bytes 43057152 | tf_op jit(solution)/shard_map/dot_general | solution.py:37
  (189 shorter events, 191.8 us)
Async XLA Ops:
  7.2 27.5 %copy-start = (bf16[512,512]{1,0:T(8,128)(2,1)S(1)}, bf16[512,512]{1,0:T(8,128)(2,1)}, u32[]{:S(2)}) copy-start(bf16[512,512]{1,0:T(8,128)(2,1)} %param.9) | copy-start | bytes 1572868
  7.2 27.5 %all-gather.2.cloned.1.call-start = ((), (), s32[]{:S(2)}) async-start(), calls=%async_computation.1 | async-start | bytes 12582912 | tf_op jit(solution)/shard_map/all_gather | solution.py:27
  7.9 63.5 %copy-start.4 = (f32[512,32]{0,1:T(8,128)S(1)}, f32[512,32]{0,1:T(8,128)}, u32[]{:S(2)}) copy-start(f32[512,32]{0,1:T(8,128)} %param.13) | copy-start | bytes 196612
  7.9 211.1 %all-reduce.3.cloned.1.call-start = ((), (), s32[]{:S(2)}) async-start(), calls=%async_computation.2 | async-start | bytes 2097152 | tf_op jit(solution)/shard_map/psum | solution.py:33
  65.7 5.7 copy-start.1
  87.8 544.6 %all-reduce.5.cloned.1.call-start = ((), (), s32[]{:S(2)}) async-start(), calls=%async_computation.3 | async-start | bytes 524288 | tf_op jit(solution)/shard_map/psum | solution.py:36
  509.3 123.0 %copy-start.2 = (f32[8192,32]{0,1:T(8,128)S(1)}, f32[8192,32]{0,1:T(8,128)}, u32[]{:S(2)}) copy-start(f32[8192,32]{0,1:T(8,128)} %get-tuple-element.52) | copy-start | bytes 3145732
  509.4 145.8 %reduce-scatter.2.cloned.1.call-start = ((), (), s32[]{:S(2)}) async-start(), calls=%async_computation.4 | async-start | bytes 12582912 | tf_op jit(solution)/shard_map/reduce_scatter | solution.py:43
  519.8 133.7 %copy-start.3 = (bf16[128,512]{1,0:T(8,128)(2,1)S(1)}, bf16[128,512]{1,0:T(8,128)(2,1)}, u32[]{:S(2)}) copy-start(bf16[128,512]{1,0:T(8,128)(2,1)} %param.12) | copy-start | bytes 393220
Sparse Core Ops, SparseCore 0:
  9.7 24.9 all-gather.1
  87.9 131.0 all-reduce.2
  509.5 122.7 all-reduce.4
  635.3 16.9 reduce-scatter.1
where the time goes:
time: 666 us; the launch traced here: 662 us
  waiting for transfers between devices  271 us (41%)
  matrix products  239 us (36%)
  local copies, waits for them, and re-layouts  93.9 us (14%)
  loops' own time  22.8 us (3%)
  other arithmetic  21.3 us (3%)
  between operations  13.8 us (2%)
    psum x1, waiting for transfers between devices, per_device(): summed = lax.psum(project, 'dp')  131 us
    psum x1, waiting for transfers between devices, per_device(): lax.psum(jnp.dot(merged.T, basis, precision=lax.Precision.HIGHEST), 'dp')  112 us
    dot_general x32, matrix products, step(): coeff = jnp.dot(column, current, precision=lax.Precision.HIGHEST) * keep  71.2 us
    dot_general x32, matrix products, step(): column = column - jnp.dot(current, coeff, precision=lax.Precision.HIGHEST)  59 us
    dynamic_update_slice x32, local copies, waits for them, and re-layouts, step(): return lax.dynamic_update_slice_in_dim(current, column[:, None], k, 1)  56.7 us
    dynamic_slice x32, local copies, waits for them, and re-layouts, step(): column = lax.dynamic_slice_in_dim(current, k, 1, 1)[:, 0]  31.4 us
    dot_general x1, matrix products, per_device(): jnp.einsum('td,tc->dc', lax.all_gather(acts, 'tensor', axis=0, tiled=True...  31 us
    dot_general x1, matrix products, per_device(): jnp.dot(merged.T, basis, precision=lax.Precision.HIGHEST)  29.6 us
  transfers between devices with their start and end apart: 4, of which 3 were waited for; matrix products, arithmetic and copies ran while one was open for 5% of the time, Pallas kernels for 0%

commit v1 on v0

v1 whole, which is shorter than its diff:
```python
import functools

import jax
import jax.numpy as jnp
from jax import lax
from jax.experimental import pallas as pl
from jax.experimental.pallas import tpu as pltpu
from jax.sharding import PartitionSpec as P

F32 = jnp.float32
BF16 = jnp.bfloat16
MIB = 1024 * 1024
BLOCK = 512
CHUNK = 128
GROUP = 8

NT = (((1,), (1,)), ((), ()))
TN = (((0,), (0,)), ((), ()))


def dot(a, b, dims=(((1,), (0,)), ((), ()))):
    return lax.dot_general(a, b, dims, preferred_element_type=F32)


def split3(x):
    high = x.astype(BF16)
    rest = x - high.astype(F32)
    middle = rest.astype(BF16)
    low = (rest - middle.astype(F32)).astype(BF16)
    return jnp.concatenate([high, middle, low], axis=0)


def sum3(x):
    rows = x.shape[0] // 3
    return x[:rows] + x[rows : 2 * rows] + x[2 * rows :]


def call(kernel, place, grid, in_specs, out_specs, out_shape, args, flops, moved, scratch=(), vmem=48):
    return pl.pallas_call(
        kernel,
        grid_spec=pltpu.PrefetchScalarGridSpec(
            num_scalar_prefetch=1,
            grid=grid,
            in_specs=in_specs,
            out_specs=out_specs,
            scratch_shapes=list(scratch),
        ),
        out_shape=out_shape,
        compiler_params=pltpu.CompilerParams(vmem_limit_bytes=vmem * MIB),
        cost_estimate=pl.CostEstimate(flops=flops, bytes_accessed=moved, transcendentals=0),
    )(place, *args)


def whole(*shape):
    return pl.BlockSpec(shape, lambda *_: (0,) * len(shape))


def left_own_kernel(scale, place, q_ref, og_own, og_oth, acts, error, part, pq_oth, q3, pq3):
    @pl.when(pl.program_id(0) == 0)
    def _():
        q3[...] = split3(q_ref[...])
        pq3[...] = split3(sum3(dot(q3[...], og_own[...], NT)) * scale)
        pq_oth[...] = split3(sum3(dot(q3[...], og_oth[...], NT)) * scale)

    part[...] = sum3(dot(q3[...], error[...], NT)) + sum3(dot(pq3[...], acts[...]))


def left_kernel(place, pq3, acts, part, left):
    total = part[...] + sum3(dot(pq3[...], acts[...]))
    for i in range(left.shape[0]):
        left[i] = total[:, i * CHUNK : (i + 1) * CHUNK].astype(BF16)


def input_kernel(place, og_own, og_oth, weight, own, oth):
    own[...] = dot(og_own[...], weight[...], NT).astype(BF16)
    oth[...] = dot(og_oth[...], weight[...], NT).astype(BF16)


def merged_kernel(scale, place, og_own, og_oth, acts_own, acts_oth, error, merged):
    grad = dot(acts_own[...], og_own[...], TN) + dot(acts_oth[...], og_oth[...], TN)
    merged[...] = grad * scale + error[...].astype(F32)


def add_kernel(place, own, other, out):
    out[...] = (own[...].astype(F32) + other[...].astype(F32)).astype(BF16)


def left_sum_kernel(place, parts, out):
    total = jnp.sum(parts[...].astype(F32), axis=0).astype(BF16)
    out[...] = jnp.broadcast_to(total[None], out.shape)


def join(left):
    return jnp.concatenate([left[i] for i in range(left.shape[0])], axis=1)


def right_kernel(scale, place, og_own, og_oth, left, acts_own, acts_oth, error, right, gram, r_acc, own_acc, oth_acc):
    step = pl.program_id(0)

    @pl.when(step == 0)
    def _():
        r_acc[...] = jnp.zeros_like(r_acc)
        own_acc[...] = jnp.zeros_like(own_acc)
        oth_acc[...] = jnp.zeros_like(oth_acc)
        gram[...] = jnp.zeros_like(gram)

    block = join(left)
    r_acc[...] += dot(block, error[...])
    own_acc[...] += dot(block, acts_own[...], NT)
    oth_acc[...] += dot(block, acts_oth[...], NT)
    gram[...] += dot(block, block, NT)

    @pl.when(step == pl.num_programs(0) - 1)
    def _():
        total = r_acc[...]
        total += sum3(dot(split3(own_acc[...] * scale), og_own[...]))
        total += sum3(dot(split3(oth_acc[...] * scale), og_oth[...]))
        for i in range(right.shape[0]):
            right[i] = total


def gram_schmidt_kernel(place, gram, out):
    width = gram.shape[0]
    g = gram[...]
    rows = lax.broadcasted_iota(jnp.int32, (width, width), 0)
    columns = lax.broadcasted_iota(jnp.int32, (width, width), 1)
    coeffs = jnp.zeros((width, width), F32)
    products = jnp.zeros((width, width), F32)
    for k in range(width):
        along = jnp.sum(jnp.where(columns == k, products, 0.0), axis=1, keepdims=True)
        unit = (columns[:1] == k).astype(F32)
        v = unit - jnp.sum(along * coeffs, axis=0, keepdims=True)
        inner = g[k : k + 1] - jnp.sum(along * products, axis=0, keepdims=True)
        square = jnp.maximum(jnp.sum(v * inner, axis=1, keepdims=True), 0.0)
        inverse = lax.rsqrt(square + 1e-06)
        coeffs = jnp.where(rows == k, v * inverse, coeffs)
        products = jnp.where(rows == k, inner * inverse, products)
    out[...] = lax.dot_general(
        coeffs, coeffs, TN, precision=lax.Precision.HIGHEST, preferred_element_type=F32
    )


def right_sum_kernel(place, parts, out):
    total = jnp.sum(parts[...], axis=0)
    out[...] = jnp.broadcast_to(total[None], out.shape)


def final_kernel(inverse_replicas, place, parts, metric, left_mine, momentum, left, merged, new_error, new_momentum, w3):
    @pl.when(pl.program_id(0) == 0)
    def _():
        total = jnp.sum(parts[...], axis=0) * inverse_replicas
        w3[...] = split3(
            jnp.dot(metric[...], total, precision=lax.Precision.HIGHEST, preferred_element_type=F32)
        )
        mine = jnp.concatenate([left_mine[0]] * 3, axis=0)
        approx = dot(mine, w3[...], TN)
        new_momentum[...] = (0.9 * momentum[...].astype(F32) + approx).astype(BF16)

    block = jnp.concatenate([join(left)] * 3, axis=0)
    new_error[...] = (merged[...] - dot(block, w3[...], TN)).astype(BF16)


def per_device(acts, out_grad, weight, error, momentum, q_init):
    tokens, cols = out_grad.shape
    half, width = acts.shape
    rank = q_init.shape[1]
    replicas = lax.axis_size("dp")
    scale = 1.0 / tokens**0.5
    steps = width // BLOCK
    per_step = BLOCK // CHUNK
    core = lax.axis_index("tensor")
    place = jnp.stack([core, 1 - core, lax.axis_index("dp")]).astype(jnp.int32)
    swap = [(0, 1), (1, 0)]
    shape = jax.ShapeDtypeStruct

    og_own = pl.BlockSpec((half, cols), lambda i, p: (p[0], 0))
    og_oth = pl.BlockSpec((half, cols), lambda i, p: (p[1], 0))
    over_lanes = lambda rows: pl.BlockSpec((rows, BLOCK), lambda i, p: (0, i))
    over_rows = pl.BlockSpec((BLOCK, cols), lambda i, p: (i, 0))
    chunks = pl.BlockSpec((per_step, rank, CHUNK), lambda i, p: (i, 0, 0))

    acts_oth = lax.ppermute(acts, "tensor", swap)

    part, pq_oth = call(
        functools.partial(left_own_kernel, scale),
        place,
        (steps,),
        [whole(rank, cols), og_own, og_oth, over_lanes(half), over_rows],
        [over_lanes(rank), whole(3 * rank, half)],
        [shape((rank, width), F32), shape((3 * rank, half), BF16)],
        (q_init.T, out_grad, out_grad, acts, error),
        flops=2 * 96 * width * 768,
        moved=13 * MIB,
        scratch=[pltpu.VMEM((3 * rank, cols), BF16), pltpu.VMEM((3 * rank, half), BF16)],
    )
    left_parts = call(
        left_kernel,
        place,
        (steps,),
        [whole(3 * rank, half), over_lanes(half), over_lanes(rank)],
        chunks,
        shape((replicas, rank, CHUNK), BF16),
        (pq_oth, acts_oth, part),
        flops=2 * 96 * width * 256,
        moved=6 * MIB,
    )
    gathered = lax.all_to_all(left_parts, "dp", 0, 0, tiled=True)

    own_input, oth_input = call(
        input_kernel,
        place,
        (steps,),
        [og_own, og_oth, over_rows],
        [over_lanes(half)] * 2,
        [shape((half, width), BF16)] * 2,
        (out_grad, out_grad, weight),
        flops=2 * tokens * cols * width,
        moved=17 * MIB,
    )
    received = lax.ppermute(oth_input, "tensor", swap)
    merged = call(
        functools.partial(merged_kernel, scale),
        place,
        (steps,),
        [og_own, og_oth, over_lanes(half), over_lanes(half), over_rows],
        over_rows,
        shape((width, cols), F32),
        (out_grad, out_grad, acts, acts_oth, error),
        flops=2 * tokens * cols * width,
        moved=33 * MIB,
    )

    left_copies = call(
        left_sum_kernel,
        place,
        (1,),
        [whole(replicas, rank, CHUNK)],
        whole(replicas, rank, CHUNK),
        shape((replicas, rank, CHUNK), BF16),
        (gathered,),
        flops=replicas * rank * CHUNK,
        moved=MIB,
    )
    left = lax.all_to_all(left_copies, "dp", 0, 0, tiled=True)
    input_grad = call(
        add_kernel,
        place,
        (8,),
        [pl.BlockSpec((half // 8, width), lambda i, p: (i, 0))] * 2,
        pl.BlockSpec((half // 8, width), lambda i, p: (i, 0)),
        shape((half, width), BF16),
        (own_input, received),
        flops=half * width,
        moved=12 * MIB,
    )

    right_copies, gram = call(
        functools.partial(right_kernel, scale),
        place,
        (steps,),
        [og_own, og_oth, chunks, over_lanes(half), over_lanes(half), over_rows],
        [whole(GROUP, rank, cols), whole(rank, rank)],
        [shape((GROUP, rank, cols), F32), shape((rank, rank), F32)],
        (out_grad, out_grad, left, acts, acts_oth, error),
        flops=2 * rank * width * 1024,
        moved=17 * MIB,
        scratch=[pltpu.VMEM((rank, cols), F32), pltpu.VMEM((rank, half), F32), pltpu.VMEM((rank, half), F32)],
    )
    metric = call(
        gram_schmidt_kernel,
        place,
        (1,),
        [whole(rank, rank)],
        whole(rank, rank),
        shape((rank, rank), F32),
        (gram,),
        flops=rank**3,
        moved=8192,
    )
    near = [[g * GROUP + i for i in range(GROUP)] for g in range(replicas // GROUP)]
    far = [[i * (replicas // GROUP) + g for i in range(GROUP)] for g in range(replicas // GROUP)]
    first = lax.all_to_all(right_copies, "dp", 0, 0, tiled=True, axis_index_groups=near)
    second_copies = call(
        right_sum_kernel,
        place,
        (1,),
        [whole(GROUP, rank, cols)],
        whole(GROUP, rank, cols),
        shape((GROUP, rank, cols), F32),
        (first,),
        flops=GROUP * rank * cols,
        moved=MIB,
    )
    second = lax.all_to_all(second_copies, "dp", 0, 0, tiled=True, axis_index_groups=far)
    new_error, new_momentum = call(
        functools.partial(final_kernel, 1.0 / replicas),
        place,
        (steps,),
        [
            whole(GROUP, rank, cols),
            whole(rank, rank),
            pl.BlockSpec((1, rank, CHUNK), lambda i, p: (p[2], 0, 0)),
            whole(CHUNK, cols),
            chunks,
            over_rows,
        ],
        [over_rows, whole(CHUNK, cols)],
        [shape((width, cols), BF16), shape((CHUNK, cols), BF16)],
        (second, metric, left, momentum, left, merged),
        flops=2 * 96 * width * cols,
        moved=25 * MIB,
        scratch=[pltpu.VMEM((3 * rank, cols), BF16)],
    )
    return (new_error, new_momentum, input_grad)


def solution(mesh):
    return jax.shard_map(
        per_device,
        mesh=mesh,
        in_specs=(
            P(("dp", "tensor"), None),
            P("dp", "tensor"),
            P(None, "tensor"),
            P("dp", "tensor"),
            P("dp", "tensor"),
            P("tensor", None),
        ),
        out_specs=(P("dp", "tensor"), P("dp", "tensor"), P(("dp", "tensor"), None)),
        check_vma=False,
    )
```

time: 666 us -> 168 us (0.25)
  waiting for transfers between devices: 271 us -> 0.01 us
  matrix products: 239 us -> 0 us
  Pallas kernels: 0 us -> 104 us
  local copies, waits for them, and re-layouts: 93.9 us -> 3.26 us
  blocking collectives: 0 us -> 52.6 us
  loops' own time: 22.8 us -> 0 us
  other arithmetic: 21.3 us -> 0.08 us
  between operations: 13.8 us -> 0.72 us
    psum x2 -> x0, waiting for transfers between devices: 243 us -> none  [the longest x1 131 us: per_device(): summed = lax.psum(project, 'dp')]
    dot_general x69 -> x0, matrix products: 239 us -> none  [the longest x32 71.2 us: step(): coeff = jnp.dot(column, current, precision=lax.Precision.HIGHEST) * keep]
    pallas_call x0 -> x10, Pallas kernels: none -> 104 us  [call(): pl.pallas_call(kernel, grid_spec=pltpu.PrefetchScalarGridSpec(num_scalar_...]
    dynamic_update_slice x32 -> x0, local copies, waits for them, and re-layouts: 56.7 us -> none  [step(): return lax.dynamic_update_slice_in_dim(current, column[:, None], k, 1)]
    all_to_all x0 -> x3, blocking collectives: none -> 52.6 us  [the longest x1 24.9 us: per_device(): gathered = lax.all_to_all(left_parts, 'dp', 0, 0, tiled=True)]
    dynamic_slice x32 -> x0, local copies, waits for them, and re-layouts: 31.4 us -> none  [step(): column = lax.dynamic_slice_in_dim(current, k, 1, 1)[:, 0]]
    all_gather x1 -> x0, waiting for transfers between devices: 26.7 us -> none  [per_device(): lax.all_gather(acts, 'tensor', axis=0, tiled=True)]
    another operation x1 -> x0, loops' own time: 22.8 us -> none  [orthonormal(): return lax.fori_loop(0, width, step, block)]
  transfers between devices with their start and end apart: 4 -> 3, of which waited for: 3 -> 0; matrix products, arithmetic and copies ran while one was open for 5% -> 0% of each run, Pallas kernels for 0% -> 53%
where the time goes in v1:
time: 168 us; the launch traced here: 165 us
  Pallas kernels  104 us (62%)
  blocking collectives  52.6 us (31%)
  starting transfers between devices  4.2 us (2%)
  local copies, waits for them, and re-layouts  3.26 us (2%)
    pallas_call x10, Pallas kernels, call(): pl.pallas_call(kernel, grid_spec=pltpu.PrefetchScalarGridSpec(num_scalar_...  104 us
    all_to_all x1, blocking collectives, per_device(): gathered = lax.all_to_all(left_parts, 'dp', 0, 0, tiled=True)  24.9 us
    all_to_all x1, blocking collectives, per_device(): left = lax.all_to_all(left_copies, 'dp', 0, 0, tiled=True)  16.6 us
    all_to_all x1, blocking collectives, per_device(): lax.all_to_all(right_copies, 'dp', 0, 0, tiled=True, axis_index_groups=near)  11.1 us
    all_to_all x1, starting transfers between devices, per_device(): lax.all_to_all(second_copies, 'dp', 0, 0, tiled=True, axis_index_groups=far)  3.62 us
  transfers between devices with their start and end apart: 3, of which 0 were waited for; matrix products, arithmetic and copies ran while one was open for 0% of the time, Pallas kernels for 53%

profile of v1, /device:TPU:0, one launch (start us, length us, event | category | flops | bytes accessed | tf_op | source)
XLA Modules:
  0.0 165.3 jit_solution(4575954534086642453)
XLA Ops:
  0.6 0.1 collective-permute-start
  0.7 0.1 pad_add_fusion.place
  0.8 0.0 copy-start.2
  0.8 1.0 copy-done.2
  1.9 0.0 copy-start
  1.9 0.0 copy-start.3
  1.9 15.3 %shard_map.93 = (bf16[256,8192]{1,0:T(8,128)(2,1)S(1)}, bf16[256,8192]{1,0:T(8,128)(2,1)}) custom-call(s32[3]{0:T(128)S(1)} %pad_add_fusion.place, bf16[512,512]{1,0:T(8,128)(2,1)S(1)} %copy-done.2, bf16[512,512]{1,0:T(8,128)(2,1)S(1)} %copy-done.2, bf16[8192,512]{1,0:T(8,128)(2,1)} %weight.1), custom_call_target="tpu_custom_call" | custom-call | flops 4294967296 | bytes 17825792 | tf_op jit(solution)/shard_map/pallas_call | solution.py:39
  17.2 0.5 collective-permute-start.1
  17.7 0.0 copy-done
  17.7 0.0 copy-done.3
  17.7 0.0 copy-done.7
  17.7 13.1 %shard_map.85 = (f32[32,8192]{1,0:T(8,128)S(1)}, bf16[96,256]{1,0:T(8,128)(2,1)S(1)}) custom-call(s32[3]{0:T(128)S(1)} %pad_add_fusion.place, f32[32,512]{1,0:T(8,128)S(1)} %bitcast.4, bf16[512,512]{1,0:T(8,128)(2,1)S(1)} %copy-done.3, bf16[512,512]{1,0:T(8,128)(2,1)S(1)} %copy-done.3, bf16[256,8192]{1,0:T(8,128)(2,1)S(1)} %copy-done, bf16[8192,512]{1,0:T(8,128)(2,1)} %error.5), custom_call_target="tpu_custom_call" | custom-call | flops 1207959552 | bytes 13631488 | tf_op jit(solution)/shard_map/pallas_call | solution.py:39
  30.8 0.0 copy-done.4
  30.8 0.0 collective-permute-done.acts.acts_oth
  30.8 9.9 %shard_map.86 = bf16[64,32,128]{2,1,0:T(8,128)(2,1)S(1)} custom-call(s32[3]{0:T(128)S(1)} %pad_add_fusion.place, bf16[96,256]{1,0:T(8,128)(2,1)S(1)} %get-tuple-element.11.pq3, bf16[256,8192]{1,0:T(8,128)(2,1)} %collective-permute-done.acts.acts_oth, f32[32,8192]{1,0:T(8,128)S(1)} %get-tuple-element.12.part), custom_call_target="tpu_custom_call" | custom-call | flops 402653184 | bytes 6291456 | tf_op jit(solution)/shard_map/pallas_call | solution.py:39
  40.8 24.9 %all_to_all.20.parts = bf16[64,32,128]{2,1,0:T(8,128)(2,1)S(1)} all-to-all(bf16[64,32,128]{2,1,0:T(8,128)(2,1)S(1)} %shard_map.86), channel_id=1, replica_groups=mesh['dp'=64,'tensor'=2] {'dp'}, dimensions={0} | all-to-all | bytes 1048576 | tf_op jit(solution)/shard_map/all_to_all | solution.py:207
  65.7 0.7 shard_map.87
  66.3 16.6 %all_to_all.21.left.left_mine = bf16[64,32,128]{2,1,0:T(8,128)(2,1)S(1)} all-to-all(bf16[64,32,128]{2,1,0:T(8,128)(2,1)S(1)} %shard_map.87), channel_id=1, replica_groups=mesh['dp'=64,'tensor'=2] {'dp'}, dimensions={0} | all-to-all | bytes 1048576 | tf_op jit(solution)/shard_map/all_to_all | solution.py:244
  82.9 13.8 %shard_map.88 = (f32[8,32,512]{2,1,0:T(8,128)S(1)}, f32[32,32]{1,0:T(8,128)S(1)}) custom-call(s32[3]{0:T(128)S(1)} %pad_add_fusion.place, bf16[512,512]{1,0:T(8,128)(2,1)S(1)} %copy-done.3, bf16[512,512]{1,0:T(8,128)(2,1)S(1)} %copy-done.3, bf16[64,32,128]{2,1,0:T(8,128)(2,1)S(1)} %all_to_all.21.left.left_mine, bf16[256,8192]{1,0:T(8,128)(2,1)S(1)} %copy-done, ...), custom_call_target="tpu_custom_call" | custom-call | flops 536870912 | bytes 17825792 | tf_op jit(solution)/shard_map/pallas_call | solution.py:39
  96.7 11.1 %all_to_all.22.parts = f32[8,32,512]{2,1,0:T(8,128)S(1)} all-to-all(f32[8,32,512]{2,1,0:T(8,128)S(1)} %get-tuple-element.13), channel_id=1, replica_groups={{0,2,4,6,8,10,12,14},{16,18,20,22,24,26,28,30},{32,34,36,38,40,42,44,46..., dimensions={0} | all-to-all | bytes 1048576 | tf_op jit(solution)/shard_map/all_to_all | solution.py:282
  107.8 1.4 shard_map.89
  109.2 3.6 %all-to-all-start.3 = ((f32[8,32,512]{2,1,0:T(8,128)}), f32[8,32,512]{2,1,0:T(8,128)S(1)}, u32[]{:S(2)}, u32[]{:S(2)}) async-start(f32[8,32,512]{2,1,0:T(8,128)} %shard_map.89), calls=%async_computation.3 | async-start | bytes 1048576 | tf_op jit(solution)/shard_map/all_to_all | solution.py:294
  112.8 0.0 collective-permute-done.1.other
  112.8 0.0 copy-start.5
  112.8 2.2 %copy-done.5 = bf16[256,8192]{1,0:T(8,128)(2,1)S(1)} copy-done((bf16[256,8192]{1,0:T(8,128)(2,1)S(1)}, bf16[256,8192]{1,0:T(8,128)(2,1)}, u32[]{:S(2)}) %copy-start.5) | copy-done | bytes 4194328
  115.0 7.9 %shard_map.94 = bf16[256,8192]{1,0:T(8,128)(2,1)} custom-call(s32[3]{0:T(128)S(1)} %pad_add_fusion.place, bf16[256,8192]{1,0:T(8,128)(2,1)S(1)} %copy-done.5, bf16[256,8192]{1,0:T(8,128)(2,1)} %collective-permute-done.1.other), custom_call_target="tpu_custom_call" | custom-call | flops 2097152 | bytes 12582912 | tf_op jit(solution)/shard_map/pallas_call | solution.py:39
  122.9 0.0 copy-done.1
  122.9 19.3 %shard_map.91.merged = f32[8192,512]{1,0:T(8,128)} custom-call(s32[3]{0:T(128)S(1)} %pad_add_fusion.place, bf16[512,512]{1,0:T(8,128)(2,1)S(1)} %copy-done.3, bf16[512,512]{1,0:T(8,128)(2,1)S(1)} %copy-done.3, bf16[256,8192]{1,0:T(8,128)(2,1)S(1)} %copy-done.1, bf16[256,8192]{1,0:T(8,128)(2,1)} %collective-permute-done.acts.acts_oth, bf16[8192,512]{1,0:T(8,128)(2,1)} %error.5), custom_call_target="tpu_custom_call" | custom-call | flops 4294967296 | bytes 34603008 | tf_op jit(solution)/shard_map/pallas_call | solution.py:39
  142.2 6.3 %shard_map.90.metric = f32[32,32]{1,0:T(8,128)S(1)} custom-call(s32[3]{0:T(128)S(1)} %pad_add_fusion.place, f32[32,32]{1,0:T(8,128)S(1)} %get-tuple-element.14.gram), custom_call_target="tpu_custom_call" | custom-call | flops 32768 | bytes 8192 | tf_op jit(solution)/shard_map/pallas_call | solution.py:39
  148.5 0.0 all-to-all-done.3.parts
  148.5 0.0 copy-done.6
  148.6 16.7 %shard_map.92 = (bf16[8192,512]{1,0:T(8,128)(2,1)}, bf16[128,512]{1,0:T(8,128)(2,1)}) custom-call(s32[3]{0:T(128)S(1)} %pad_add_fusion.place, f32[8,32,512]{2,1,0:T(8,128)S(1)} %all-to-all-done.3.parts, f32[32,32]{1,0:T(8,128)S(1)} %shard_map.90.metric, bf16[64,32,128]{2,1,0:T(8,128)(2,1)S(1)} %all_to_all.21.left.left_mine, bf16[128,512]{1,0:T(8,128)(2,1)S(1)} %copy-done.6, ...), custom_call_target="tpu_custom_call" | custom-call | flops 805306368 | bytes 26214400 | tf_op jit(solution)/shard_map/pallas_call | solution.py:39
  (4 shorter events, 0.0 us)
Async XLA Ops:
  0.6 30.2 %collective-permute-start = (bf16[256,8192]{1,0:T(8,128)(2,1)}, bf16[256,8192]{1,0:T(8,128)(2,1)}, u32[]{:S(2)}, u32[]{:S(2)}) collective-permute-start(bf16[256,8192]{1,0:T(8,128)(2,1)} %acts_own.3), channel_id=1, source_target_pairs={{0,1},{1,0},{2,3},{3,2},{4,5},{5,4},{6,7},{7,6},{8,9},{9,8},{10,11... | collective-permute-start | bytes 12582920 | tf_op jit(solution)/shard_map/ppermute | solution.py:182
  0.8 1.0 copy-start.2
  1.9 15.8 %copy-start = (bf16[256,8192]{1,0:T(8,128)(2,1)S(1)}, bf16[256,8192]{1,0:T(8,128)(2,1)}, u32[]{:S(2)}) copy-start(bf16[256,8192]{1,0:T(8,128)(2,1)} %acts_own.3) | copy-start | bytes 12582916
  1.9 15.8 %copy-start.3 = (bf16[512,512]{1,0:T(8,128)(2,1)S(1)}, bf16[512,512]{1,0:T(8,128)(2,1)}, u32[]{:S(2)}) copy-start(bf16[512,512]{1,0:T(8,128)(2,1)} %og_oth.7) | copy-start | bytes 1572868
  1.9 15.8 %copy-start.7 = (f32[512,32]{0,1:T(8,128)S(1)}, f32[512,32]{0,1:T(8,128)}, u32[]{:S(2)}) copy-start(f32[512,32]{0,1:T(8,128)} %param.11) | copy-start | bytes 196612
  17.2 13.6 %copy-start.4 = (bf16[256,8192]{1,0:T(8,128)(2,1)}, bf16[256,8192]{1,0:T(8,128)(2,1)S(1)}, u32[]{:S(2)}) copy-start(bf16[256,8192]{1,0:T(8,128)(2,1)S(1)} %get-tuple-element.17.own) | copy-start | bytes 12582916
  17.2 95.7 %collective-permute-start.1 = (bf16[256,8192]{1,0:T(8,128)(2,1)}, bf16[256,8192]{1,0:T(8,128)(2,1)}, u32[]{:S(2)}, u32[]{:S(2)}) collective-permute-start(bf16[256,8192]{1,0:T(8,128)(2,1)} %get-tuple-element.18), channel_id=1, source_target_pairs={{0,1},{1,0},{2,3},{3,2},{4,5},{5,4},{6,7},{7,6},{8,9},{9,8},{10,11... | collective-permute-start | bytes 12582920 | tf_op jit(solution)/shard_map/ppermute | solution.py:220
  109.2 39.3 %all-to-all-start.3 = ((f32[8,32,512]{2,1,0:T(8,128)}), f32[8,32,512]{2,1,0:T(8,128)S(1)}, u32[]{:S(2)}, u32[]{:S(2)}) async-start(f32[8,32,512]{2,1,0:T(8,128)} %shard_map.89), calls=%async_computation.3 | async-start | bytes 1048576 | tf_op jit(solution)/shard_map/all_to_all | solution.py:294
  112.8 2.2 %copy-start.5 = (bf16[256,8192]{1,0:T(8,128)(2,1)S(1)}, bf16[256,8192]{1,0:T(8,128)(2,1)}, u32[]{:S(2)}) copy-start(bf16[256,8192]{1,0:T(8,128)(2,1)} %copy-done.4) | copy-start | bytes 12582916
  115.0 7.9 %copy-start.1 = (bf16[256,8192]{1,0:T(8,128)(2,1)S(1)}, bf16[256,8192]{1,0:T(8,128)(2,1)}, u32[]{:S(2)}) copy-start(bf16[256,8192]{1,0:T(8,128)(2,1)} %acts_own.3) | copy-start | bytes 12582916
  122.9 25.6 %copy-start.6 = (bf16[128,512]{1,0:T(8,128)(2,1)S(1)}, bf16[128,512]{1,0:T(8,128)(2,1)}, u32[]{:S(2)}) copy-start(bf16[128,512]{1,0:T(8,128)(2,1)} %momentum.1) | copy-start | bytes 393220

commit v2 on v0

v2 whole, which is shorter than its diff:
```python
import functools

import jax
import jax.numpy as jnp
from jax import lax
from jax.experimental import pallas as pl
from jax.experimental.pallas import tpu as pltpu
from jax.sharding import PartitionSpec as P

F32 = jnp.float32
BF16 = jnp.bfloat16
MIB = 1024 * 1024
BLOCK = 1024
CHUNK = 128
GROUP = 8

NN = (((1,), (0,)), ((), ()))
NT = (((1,), (1,)), ((), ()))
TN = (((0,), (0,)), ((), ()))

VMEM = pl.BlockSpec(memory_space=pltpu.VMEM)
SMEM = pl.BlockSpec(memory_space=pltpu.SMEM)
HBM = pl.BlockSpec(memory_space=pltpu.HBM)
TOKEN = jax.ShapeDtypeStruct((8, 128), jnp.float32)


def in_hbm(x):
    return pltpu.with_memory_space_constraint(x, pltpu.HBM)


def dot(a, b, dims=NN):
    return lax.dot_general(a, b, dims, preferred_element_type=F32)


def exact_dot(a, b, dims=NN):
    return lax.dot_general(a, b, dims, precision=lax.Precision.HIGHEST, preferred_element_type=F32)


def split3(x, axis=0):
    high = x.astype(BF16)
    rest = x - high.astype(F32)
    middle = rest.astype(BF16)
    low = (rest - middle.astype(F32)).astype(BF16)
    return jnp.concatenate([high, middle, low], axis=axis)


def sum3(x):
    rows = x.shape[0] // 3
    return x[:rows] + x[rows : 2 * rows] + x[2 * rows :]


def call(kernel, in_specs, out_specs, out_shape, args, flops, moved, scratch=(), aliases={}):
    args = [in_hbm(x) if spec is HBM else x for spec, x in zip(in_specs, args)]
    return pl.pallas_call(
        kernel,
        in_specs=in_specs,
        out_specs=out_specs,
        out_shape=out_shape,
        scratch_shapes=list(scratch),
        input_output_aliases=aliases,
        compiler_params=pltpu.CompilerParams(vmem_limit_bytes=48 * MIB),
        cost_estimate=pl.CostEstimate(flops=flops, bytes_accessed=moved, transcendentals=0),
    )(*args)


def halves(place, og, half):
    own = pl.multiple_of(place[0] * half, half)
    oth = pl.multiple_of(place[1] * half, half)
    return og[pl.ds(own, half), :], og[pl.ds(oth, half), :]


def blocks(width):
    return [slice(i, i + BLOCK) for i in range(0, width, BLOCK)]


class Reader:
    ahead = 3

    def __init__(self, pairs, sems):
        self.copies = [
            [pltpu.make_async_copy(source, target, sems.at[i, j]) for j, (source, target) in enumerate(block)]
            for i, block in enumerate(pairs)
        ]
        for block in self.copies[: self.ahead]:
            for copy in block:
                copy.start()

    def wait(self, i):
        if i + self.ahead < len(self.copies):
            for copy in self.copies[i + self.ahead]:
                copy.start()
        for copy in self.copies[i]:
            copy.wait()


class Writer:
    def __init__(self, slots, sems):
        self.slots, self.sems, self.copies = slots, sems, []

    def put(self, value, target):
        at = len(self.copies)
        slot = at % self.slots.shape[0]
        if at >= self.slots.shape[0]:
            self.copies[at - self.slots.shape[0]].wait()
        self.slots[slot] = value
        copy = pltpu.make_async_copy(self.slots.at[slot], target, self.sems.at[slot])
        copy.start()
        self.copies.append(copy)

    def finish(self):
        for copy in self.copies[-self.slots.shape[0] :]:
            copy.wait()


def left_own_kernel(
    scale, place, q_hbm, og_hbm, acts, error, part, pq_oth, q, og, acts_here, error_here, sems, small_sems
):
    half, width = acts.shape
    rows = blocks(width)
    q_copy = pltpu.make_async_copy(q_hbm, q, small_sems.at[0])
    og_copy = pltpu.make_async_copy(og_hbm, og, small_sems.at[1])
    q_copy.start()
    og_copy.start()
    reader = Reader([[(error.at[at, :], error_here.at[at, :]), (acts.at[:, at], acts_here.at[:, at])] for at in rows], sems)
    q_copy.wait()
    og_copy.wait()
    q3 = split3(q[...])
    og_own, og_oth = halves(place, og, half)
    pq3 = split3(sum3(dot(q3, og_own, NT)) * scale)
    pq_oth[...] = split3(sum3(dot(q3, og_oth, NT)) * scale)
    for i, at in enumerate(rows):
        reader.wait(i)
        by_error = dot(error_here[at, :], q3, NT)
        part[:, at] = sum3(by_error.T) + sum3(dot(pq3, acts_here[:, at]))


def left_kernel(pq3, acts, part, left, token):
    token[...] = jnp.zeros_like(token)
    for at in blocks(acts.shape[1]):
        total = part[:, at] + sum3(dot(pq3[...], acts[:, at]))
        for i in range(BLOCK // CHUNK):
            left[at.start // CHUNK + i] = total[:, i * CHUNK : (i + 1) * CHUNK].astype(BF16)


def merged_kernel(
    scale, place, og, acts, acts_oth, error, after, merged, token,
    acts_here, oth_here, error_here, slots, sems, out_sems,
):
    token[...] = jnp.zeros_like(token)
    half, width = acts.shape
    rows = blocks(width)
    reader = Reader(
        [
            [
                (acts.at[:, at], acts_here.at[:, at]),
                (acts_oth.at[:, at], oth_here.at[:, at]),
                (error.at[at, :], error_here.at[at, :]),
            ]
            for at in rows
        ],
        sems,
    )
    own, oth = halves(place, og, half)
    writer = Writer(slots, out_sems)
    for i, at in enumerate(rows):
        reader.wait(i)
        grad = dot(acts_here[:, at], own, TN) + dot(oth_here[:, at], oth, TN)
        writer.put(grad * scale + error_here[at, :].astype(F32), merged.at[at, :])
    writer.finish()


def input_kernel(place, og, weight, after, own_part, oth_part, token, weight_here, own_slots, oth_slots, sems, own_sems, oth_sems):
    token[...] = jnp.zeros_like(token)
    half, width = own_part.shape
    rows = blocks(width)
    reader = Reader([[(weight.at[at, :], weight_here.at[at, :])] for at in rows], sems)
    own, oth = halves(place, og, half)
    both = jnp.concatenate([own, oth], axis=0)
    own_out = Writer(own_slots, own_sems)
    oth_out = Writer(oth_slots, oth_sems)
    for i, at in enumerate(rows):
        reader.wait(i)
        product = dot(both, weight_here[at, :], NT).astype(BF16)
        oth_out.put(product[half:], oth_part.at[:, at])
        own_out.put(product[:half], own_part.at[:, at])
    own_out.finish()
    oth_out.finish()


def pass_kernel(part, left, after, out, token):
    token[...] = left[0, :8].astype(F32)


def add_kernel(own, other, after, out, token, own_here, other_here, slots, sems, out_sems):
    token[...] = jnp.zeros_like(token)
    rows = blocks(own.shape[1])
    reader = Reader([[(own.at[:, at], own_here.at[:, at]), (other.at[:, at], other_here.at[:, at])] for at in rows], sems)
    writer = Writer(slots, out_sems)
    for i, at in enumerate(rows):
        reader.wait(i)
        writer.put((own_here[:, at].astype(F32) + other_here[:, at].astype(F32)).astype(BF16), out.at[:, at])
    writer.finish()


def left_sum_kernel(parts, after, out, token):
    token[...] = jnp.zeros_like(token)
    total = jnp.sum(parts[...].astype(F32), axis=0).astype(BF16)
    out[...] = jnp.broadcast_to(total[None], out.shape)


def right_kernel(
    scale, place, og, left, acts, acts_oth, error, after, right, gram, left_rows, stack, error_here, sems
):
    tokens, cols = og.shape
    half, width = acts.shape
    rows = blocks(width)
    reader = Reader(
        [
            [
                (acts.at[:, at], stack.at[:half, at]),
                (acts_oth.at[:, at], stack.at[half:tokens, at]),
                (error.at[at, :], error_here.at[at, :]),
            ]
            for at in rows
        ],
        sems,
    )
    for i in range(left.shape[0]):
        stack[tokens:, i * CHUNK : (i + 1) * CHUNK] = left[i]
    left_rows[...] = stack[tokens:, :]
    by_stack, result = None, None
    for i, at in enumerate(rows):
        reader.wait(i)
        here = stack[tokens:, at]
        stack_term = dot(stack[:, at], here, NT)
        error_term = dot(here, error_here[at, :])
        by_stack = stack_term if by_stack is None else by_stack + stack_term
        result = error_term if result is None else result + error_term
    gram[...] = by_stack[tokens:]
    own, oth = halves(place, og, half)
    by_acts = split3(by_stack[:tokens] * scale, axis=1)
    result += sum3(dot(by_acts[:half], own, TN) + dot(by_acts[half:], oth, TN))
    for i in range(right.shape[0]):
        right[i] = result


def gram_schmidt_kernel(gram, left_rows, out, left_columns):
    width = gram.shape[0]
    g = gram[...]
    rows = lax.broadcasted_iota(jnp.int32, (width, width), 0)
    columns = lax.broadcasted_iota(jnp.int32, (width, width), 1)
    coeffs = jnp.zeros((width, width), F32)
    products = jnp.zeros((width, width), F32)
    for k in range(width):
        along = jnp.sum(jnp.where(columns == k, products, 0.0), axis=1, keepdims=True)
        unit = (columns[:1] == k).astype(F32)
        v = unit - jnp.sum(along * coeffs, axis=0, keepdims=True)
        inner = g[k : k + 1] - jnp.sum(along * products, axis=0, keepdims=True)
        square = jnp.maximum(jnp.sum(v * inner, axis=1, keepdims=True), 0.0)
        inverse = lax.rsqrt(square + 1e-06)
        coeffs = jnp.where(rows == k, v * inverse, coeffs)
        products = jnp.where(rows == k, inner * inverse, products)
    out[...] = exact_dot(coeffs, coeffs, TN)
    for at in blocks(left_rows.shape[1]):
        left_columns[at, :] = jnp.concatenate([left_rows[:, at]] * 3, axis=0).T


def right_sum_kernel(parts, after, out, token):
    token[...] = jnp.zeros_like(token)
    total = jnp.sum(parts[...], axis=0)
    out[...] = jnp.broadcast_to(total[None], out.shape)


def final_kernel(
    inverse_replicas, place, parts, metric, left, momentum, merged, after, new_error, new_momentum,
    merged_here, slots, sems, out_sems,
):
    all_rows = blocks(merged.shape[0])
    reader = Reader([[(merged.at[at, :], merged_here.at[at, :])] for at in all_rows], sems)
    total = jnp.sum(parts[...], axis=0) * inverse_replicas
    w3 = split3(exact_dot(metric[...], total))
    writer = Writer(slots, out_sems)
    for i, at in enumerate(all_rows):
        reader.wait(i)
        writer.put((merged_here[at, :] - dot(left[at, :], w3)).astype(BF16), new_error.at[at, :])
    rows = momentum.shape[0]
    mine = pl.ds(pl.multiple_of(place[2] * rows, rows), rows)
    new_momentum[...] = (0.9 * momentum[...].astype(F32) + dot(left[mine, :], w3)).astype(BF16)
    writer.finish()


def per_device(acts, out_grad, weight, error, momentum, q_init):
    tokens, cols = out_grad.shape
    half, width = acts.shape
    rank = q_init.shape[1]
    replicas = lax.axis_size("dp")
    scale = 1.0 / tokens**0.5
    core = lax.axis_index("tensor")
    place = jnp.stack([core, 1 - core, lax.axis_index("dp")]).astype(jnp.int32)
    swap = [(0, 1), (1, 0)]
    shape = jax.ShapeDtypeStruct
    near = [[g * GROUP + i for i in range(GROUP)] for g in range(replicas // GROUP)]
    far = [[i * (replicas // GROUP) + g for i in range(GROUP)] for g in range(replicas // GROUP)]
    dma = pltpu.SemaphoreType.DMA
    n_blocks = width // BLOCK

    acts_oth = lax.ppermute(acts, "tensor", swap)

    part, pq_oth = call(
        functools.partial(left_own_kernel, scale),
        [SMEM, HBM, HBM, HBM, HBM],
        [VMEM] * 2,
        [shape((rank, width), F32), shape((3 * rank, half), BF16)],
        (place, q_init.T, out_grad, acts, error),
        flops=2 * 96 * width * 768,
        moved=13 * MIB,
        scratch=[
            pltpu.VMEM((rank, cols), F32),
            pltpu.VMEM((tokens, cols), BF16),
            pltpu.VMEM((half, width), BF16),
            pltpu.VMEM((width, cols), BF16),
            dma((n_blocks, 2)),
            dma((2,)),
        ],
    )
    left_parts, left_done = call(
        left_kernel,
        [VMEM] * 3,
        [VMEM] * 2,
        [shape((replicas, rank, CHUNK), BF16), TOKEN],
        (pq_oth, acts_oth, part),
        flops=2 * 96 * width * 256,
        moved=6 * MIB,
    )
    gathered = lax.all_to_all(left_parts, "dp", 0, 0, tiled=True)
    merged, merged_done = call(
        functools.partial(merged_kernel, scale),
        [SMEM, VMEM, HBM, HBM, HBM, VMEM],
        [HBM, VMEM],
        [pltpu.HBM((width, cols), F32), TOKEN],
        (place, out_grad, acts, acts_oth, error, left_done),
        flops=2 * tokens * cols * width,
        moved=32 * MIB,
        scratch=[
            pltpu.VMEM((half, width), BF16),
            pltpu.VMEM((half, width), BF16),
            pltpu.VMEM((width, cols), BF16),
            pltpu.VMEM((4, BLOCK, cols), F32),
            dma((n_blocks, 3)),
            dma((4,)),
        ],
    )

    left_copies, sum_done = call(
        left_sum_kernel,
        [VMEM, VMEM],
        [VMEM, VMEM],
        [shape((replicas, rank, CHUNK), BF16), TOKEN],
        (gathered, merged_done),
        flops=replicas * rank * CHUNK,
        moved=MIB,
    )
    left = lax.all_to_all(left_copies, "dp", 0, 0, tiled=True)
    own_input, oth_input, input_done = call(
        input_kernel,
        [SMEM, VMEM, HBM, VMEM],
        [HBM, HBM, VMEM],
        [pltpu.HBM((half, width), BF16), pltpu.HBM((half, width), BF16), TOKEN],
        (place, out_grad, weight, sum_done),
        flops=2 * tokens * cols * width,
        moved=17 * MIB,
        scratch=[
            pltpu.VMEM((width, cols), BF16),
            pltpu.VMEM((4, half, BLOCK), BF16),
            pltpu.VMEM((4, half, BLOCK), BF16),
            dma((n_blocks, 1)),
            dma((4,)),
            dma((4,)),
        ],
    )
    oth_input, passed = call(
        pass_kernel,
        [HBM, VMEM, VMEM],
        [HBM, VMEM],
        [pltpu.HBM((half, width), BF16), TOKEN],
        (oth_input, left, input_done),
        flops=1,
        moved=4096,
        aliases={0: 0},
    )
    received = lax.ppermute(oth_input, "tensor", swap)

    right_copies, gram, left_rows = call(
        functools.partial(right_kernel, scale),
        [SMEM, VMEM, VMEM, HBM, HBM, HBM, VMEM],
        [VMEM] * 3,
        [shape((GROUP, rank, cols), F32), shape((rank, rank), F32), shape((rank, width), BF16)],
        (place, out_grad, left, acts, acts_oth, error, passed),
        flops=2 * rank * width * 1024,
        moved=17 * MIB,
        scratch=[pltpu.VMEM((tokens + rank, width), BF16), pltpu.VMEM((width, cols), BF16), dma((n_blocks, 3))],
    )
    first = lax.all_to_all(right_copies, "dp", 0, 0, tiled=True, axis_index_groups=near)
    metric, left_columns = call(
        gram_schmidt_kernel,
        [VMEM] * 2,
        [VMEM] * 2,
        [shape((rank, rank), F32), shape((width, 3 * rank), BF16)],
        (gram, left_rows),
        flops=MIB * 1024,
        moved=3 * MIB,
    )
    second_copies, second_done = call(
        right_sum_kernel,
        [VMEM, VMEM],
        [VMEM, VMEM],
        [shape((GROUP, rank, cols), F32), TOKEN],
        (first, metric),
        flops=GROUP * rank * cols,
        moved=MIB,
    )
    second = lax.all_to_all(second_copies, "dp", 0, 0, tiled=True, axis_index_groups=far)
    input_grad, add_done = call(
        add_kernel,
        [HBM, HBM, VMEM],
        [HBM, VMEM],
        [pltpu.HBM((half, width), BF16), TOKEN],
        (own_input, received, second_done),
        flops=half * width,
        moved=12 * MIB,
        scratch=[
            pltpu.VMEM((half, width), BF16),
            pltpu.VMEM((half, width), BF16),
            pltpu.VMEM((4, half, BLOCK), BF16),
            dma((n_blocks, 2)),
            dma((4,)),
        ],
    )
    new_error, new_momentum = call(
        functools.partial(final_kernel, 1.0 / replicas),
        [SMEM, VMEM, VMEM, VMEM, VMEM, HBM, VMEM],
        [HBM, VMEM],
        [pltpu.HBM((width, cols), BF16), shape(momentum.shape, BF16)],
        (place, second, metric, left_columns, momentum, merged, add_done),
        flops=2 * 96 * width * cols,
        moved=25 * MIB,
        scratch=[pltpu.VMEM((width, cols), F32), pltpu.VMEM((4, BLOCK, cols), BF16), dma((n_blocks, 1)), dma((4,))],
    )
    return (new_error, new_momentum, input_grad)


def solution(mesh):
    return jax.shard_map(
        per_device,
        mesh=mesh,
        in_specs=(
            P(("dp", "tensor"), None),
            P("dp", "tensor"),
            P(None, "tensor"),
            P("dp", "tensor"),
            P("dp", "tensor"),
            P("tensor", None),
        ),
        out_specs=(P("dp", "tensor"), P("dp", "tensor"), P(("dp", "tensor"), None)),
        check_vma=False,
    )
```

time: 666 us -> 115 us (0.17)
  waiting for transfers between devices: 271 us -> 16.7 us
  matrix products: 239 us -> 0 us
  local copies, waits for them, and re-layouts: 93.9 us -> 0.01 us
  Pallas kernels: 0 us -> 68.4 us
  starting transfers between devices: 0.38 us -> 28 us
  loops' own time: 22.8 us -> 0 us
  other arithmetic: 21.3 us -> 0.08 us
  between operations: 13.8 us -> 0.93 us
    psum x2 -> x0, waiting for transfers between devices: 243 us -> none  [the longest x1 131 us: per_device(): summed = lax.psum(project, 'dp')]
    dot_general x69 -> x0, matrix products: 239 us -> none  [the longest x32 71.2 us: step(): coeff = jnp.dot(column, current, precision=lax.Precision.HIGHEST) * keep]
    pallas_call x0 -> x11, Pallas kernels: none -> 68.4 us  [call(): pl.pallas_call(kernel, in_specs=in_specs, out_specs=out_specs, out_shape=...]
    dynamic_update_slice x32 -> x0, local copies, waits for them, and re-layouts: 56.7 us -> none  [step(): return lax.dynamic_update_slice_in_dim(current, column[:, None], k, 1)]
    dynamic_slice x32 -> x0, local copies, waits for them, and re-layouts: 31.4 us -> none  [step(): column = lax.dynamic_slice_in_dim(current, k, 1, 1)[:, 0]]
    all_to_all x0 -> x4, starting transfers between devices: none -> 27.9 us  [the longest x1 11.5 us: per_device(): gathered = lax.all_to_all(left_parts, 'dp', 0, 0, tiled=True)]
    all_gather x1 -> x0, waiting for transfers between devices: 26.7 us -> none  [per_device(): lax.all_gather(acts, 'tensor', axis=0, tiled=True)]
    another operation x1 -> x0, loops' own time: 22.8 us -> none  [orthonormal(): return lax.fori_loop(0, width, step, block)]
  transfers between devices with their start and end apart: 4 -> 6, of which waited for: 3 -> 4; matrix products, arithmetic and copies ran while one was open for 5% -> 0% of each run, Pallas kernels for 0% -> 46%
where the time goes in v2:
time: 115 us; the launch traced here: 114 us
  Pallas kernels  68.4 us (59%)
  starting transfers between devices  28 us (24%)
  waiting for transfers between devices  16.7 us (15%)
    pallas_call x11, Pallas kernels, call(): pl.pallas_call(kernel, in_specs=in_specs, out_specs=out_specs, out_shape=...  68.4 us
    all_to_all x1, starting transfers between devices, per_device(): gathered = lax.all_to_all(left_parts, 'dp', 0, 0, tiled=True)  11.5 us
    all_to_all x1, starting transfers between devices, per_device(): left = lax.all_to_all(left_copies, 'dp', 0, 0, tiled=True)  9.01 us
    all_to_all x1, waiting for transfers between devices, per_device(): lax.all_to_all(second_copies, 'dp', 0, 0, tiled=True, axis_index_groups=far)  5.95 us
    all_to_all x1, waiting for transfers between devices, per_device(): lax.all_to_all(right_copies, 'dp', 0, 0, tiled=True, axis_index_groups=near)  5.13 us
    all_to_all x1, waiting for transfers between devices, per_device(): left = lax.all_to_all(left_copies, 'dp', 0, 0, tiled=True)  4.26 us
    all_to_all x1, starting transfers between devices, per_device(): lax.all_to_all(second_copies, 'dp', 0, 0, tiled=True, axis_index_groups=far)  3.92 us
    all_to_all x1, starting transfers between devices, per_device(): lax.all_to_all(right_copies, 'dp', 0, 0, tiled=True, axis_index_groups=near)  3.5 us
  transfers between devices with their start and end apart: 6, of which 4 were waited for; matrix products, arithmetic and copies ran while one was open for 0% of the time, Pallas kernels for 46%

profile of v2, /device:TPU:0, one launch (start us, length us, event | category | flops | bytes accessed | tf_op | source)
XLA Modules:
  0.0 114.1 jit_solution(4299770886668346319)
XLA Ops:
  0.6 0.1 collective-permute-start
  0.7 0.1 pad_add_fusion.place
  0.8 9.3 %shard_map.85 = (f32[32,8192]{1,0:T(8,128)S(1)}, bf16[96,256]{1,0:T(8,128)(2,1)S(1)}) custom-call(s32[3]{0:T(128)S(1)} %pad_add_fusion.place, f32[32,512]{1,0:T(8,128)} %bitcast.4, bf16[512,512]{1,0:T(8,128)(2,1)} %og.5, bf16[256,8192]{1,0:T(8,128)(2,1)} %acts.5, bf16[8192,512]{1,0:T(8,128)(2,1)} %error.5), custom_call_target="tpu_custom_call" | custom-call | flops 1207959552 | bytes 13631488 | tf_op jit(solution)/shard_map/pallas_call | solution.py:54
  10.1 0.0 copy-start
  10.1 0.0 collective-permute-done.acts.acts_oth
  10.1 3.9 %shard_map.86 = (bf16[64,32,128]{2,1,0:T(8,128)(2,1)}, f32[8,128]{1,0:T(8,128)S(1)}) custom-call(bf16[96,256]{1,0:T(8,128)(2,1)S(1)} %get-tuple-element.27.pq3, bf16[256,8192]{1,0:T(8,128)(2,1)} %collective-permute-done.acts.acts_oth, f32[32,8192]{1,0:T(8,128)S(1)} %get-tuple-element.28.part), custom_call_target="tpu_custom_call" | custom-call | flops 402653184 | bytes 6291456 | tf_op jit(solution)/shard_map/pallas_call | solution.py:54
  14.0 11.5 %all-to-all-start = ((bf16[64,32,128]{2,1,0:T(8,128)(2,1)}), bf16[64,32,128]{2,1,0:T(8,128)(2,1)S(1)}, u32[]{:S(2)}, u32[]{:S(2)}) async-start(bf16[64,32,128]{2,1,0:T(8,128)(2,1)} %get-tuple-element.29), calls=%async_computation | async-start | bytes 1048576 | tf_op jit(solution)/shard_map/all_to_all | solution.py:335
  25.5 0.0 copy-done
  25.5 12.7 %shard_map.87 = (f32[8192,512]{1,0:T(8,128)}, f32[8,128]{1,0:T(8,128)S(1)}) custom-call(s32[3]{0:T(128)S(1)} %pad_add_fusion.place, bf16[512,512]{1,0:T(8,128)(2,1)S(1)} %copy-done, bf16[256,8192]{1,0:T(8,128)(2,1)} %acts.5, bf16[256,8192]{1,0:T(8,128)(2,1)} %collective-permute-done.acts.acts_oth, bf16[8192,512]{1,0:T(8,128)(2,1)} %error.5, ...), custom_call_target="tpu_custom_call" | custom-call | flops 4294967296 | bytes 33554432 | tf_op jit(solution)/shard_map/pallas_call | solution.py:54
  38.2 1.3 %all-to-all-done.parts = bf16[64,32,128]{2,1,0:T(8,128)(2,1)S(1)} async-done(((bf16[64,32,128]{2,1,0:T(8,128)(2,1)}), bf16[64,32,128]{2,1,0:T(8,128)(2,1)S(1)}, u32[]{:S(2)}, u32[]{:S(2)}) %all-to-all-start) | async-done | bytes 524320 | tf_op jit(solution)/shard_map/all_to_all | solution.py:335
  39.5 0.9 shard_map.88
  40.4 9.0 %all-to-all-start.1 = ((bf16[64,32,128]{2,1,0:T(8,128)(2,1)}), bf16[64,32,128]{2,1,0:T(8,128)(2,1)S(1)}, u32[]{:S(2)}, u32[]{:S(2)}) async-start(bf16[64,32,128]{2,1,0:T(8,128)(2,1)} %get-tuple-element.32), calls=%async_computation.1 | async-start | bytes 1048576 | tf_op jit(solution)/shard_map/all_to_all | solution.py:363
  49.5 9.2 %shard_map.89 = (bf16[256,8192]{1,0:T(8,128)(2,1)}, bf16[256,8192]{1,0:T(8,128)(2,1)}, f32[8,128]{1,0:T(8,128)S(1)}) custom-call(s32[3]{0:T(128)S(1)} %pad_add_fusion.place, bf16[512,512]{1,0:T(8,128)(2,1)S(1)} %copy-done, bf16[8192,512]{1,0:T(8,128)(2,1)} %weight.1, f32[8,128]{1,0:T(8,128)S(1)} %get-tuple-element.33.after), custom_call_target="tpu_custom_call" | custom-call | flops 4294967296 | bytes 17825792 | tf_op jit(solution)/shard_map/pallas_call | solution.py:54
  58.6 4.3 %all-to-all-done.1.left = bf16[64,32,128]{2,1,0:T(8,128)(2,1)S(1)} async-done(((bf16[64,32,128]{2,1,0:T(8,128)(2,1)}), bf16[64,32,128]{2,1,0:T(8,128)(2,1)S(1)}, u32[]{:S(2)}, u32[]{:S(2)}) %all-to-all-start.1) | async-done | bytes 524320 | tf_op jit(solution)/shard_map/all_to_all | solution.py:363
  62.9 0.0 collective-permute-start.1
  62.9 9.5 %shard_map.91 = (f32[8,32,512]{2,1,0:T(8,128)}, f32[32,32]{1,0:T(8,128)S(1)}, bf16[32,8192]{1,0:T(8,128)(2,1)S(1)}) custom-call(s32[3]{0:T(128)S(1)} %pad_add_fusion.place, bf16[512,512]{1,0:T(8,128)(2,1)S(1)} %copy-done, bf16[64,32,128]{2,1,0:T(8,128)(2,1)S(1)} %all-to-all-done.1.left, bf16[256,8192]{1,0:T(8,128)(2,1)} %acts.5, ...), custom_call_target="tpu_custom_call" | custom-call | flops 536870912 | bytes 17825792 | tf_op jit(solution)/shard_map/pallas_call | solution.py:54
  72.4 3.5 %all-to-all-start.2 = ((f32[8,32,512]{2,1,0:T(8,128)}), f32[8,32,512]{2,1,0:T(8,128)S(1)}, u32[]{:S(2)}, u32[]{:S(2)}) async-start(f32[8,32,512]{2,1,0:T(8,128)} %get-tuple-element.37), calls=%async_computation.2 | async-start | bytes 1048576 | tf_op jit(solution)/shard_map/all_to_all | solution.py:403
  75.9 5.8 %shard_map.92 = (f32[32,32]{1,0:T(8,128)S(1)}, bf16[8192,96]{1,0:T(8,128)(2,1)S(1)}) custom-call(f32[32,32]{1,0:T(8,128)S(1)} %get-tuple-element.38.gram, bf16[32,8192]{1,0:T(8,128)(2,1)S(1)} %get-tuple-element.39.left_rows), custom_call_target="tpu_custom_call" | custom-call | flops 1073741824 | bytes 3145728 | tf_op jit(solution)/shard_map/pallas_call | solution.py:54
  81.7 5.1 %all-to-all-done.2.parts = f32[8,32,512]{2,1,0:T(8,128)S(1)} async-done(((f32[8,32,512]{2,1,0:T(8,128)}), f32[8,32,512]{2,1,0:T(8,128)S(1)}, u32[]{:S(2)}, u32[]{:S(2)}) %all-to-all-start.2) | async-done | bytes 524320 | tf_op jit(solution)/shard_map/all_to_all | solution.py:403
  86.9 0.9 shard_map.93
  87.7 3.9 %all-to-all-start.3 = ((f32[8,32,512]{2,1,0:T(8,128)}), f32[8,32,512]{2,1,0:T(8,128)S(1)}, u32[]{:S(2)}, u32[]{:S(2)}) async-start(f32[8,32,512]{2,1,0:T(8,128)} %get-tuple-element.41), calls=%async_computation.3 | async-start | bytes 1048576 | tf_op jit(solution)/shard_map/all_to_all | solution.py:422
  91.6 0.0 collective-permute-done.1.other
  91.7 0.0 copy-start.1
  91.7 5.5 %shard_map.94 = (bf16[256,8192]{1,0:T(8,128)(2,1)}, f32[8,128]{1,0:T(8,128)S(1)}) custom-call(bf16[256,8192]{1,0:T(8,128)(2,1)} %get-tuple-element.44.own, bf16[256,8192]{1,0:T(8,128)(2,1)} %collective-permute-done.1.other, f32[8,128]{1,0:T(8,128)S(1)} %get-tuple-element.46.after), custom_call_target="tpu_custom_call" | custom-call | flops 2097152 | bytes 12582912 | tf_op jit(solution)/shard_map/pallas_call | solution.py:54
  97.2 5.9 %all-to-all-done.3.parts = f32[8,32,512]{2,1,0:T(8,128)S(1)} async-done(((f32[8,32,512]{2,1,0:T(8,128)}), f32[8,32,512]{2,1,0:T(8,128)S(1)}, u32[]{:S(2)}, u32[]{:S(2)}) %all-to-all-start.3) | async-done | bytes 524320 | tf_op jit(solution)/shard_map/all_to_all | solution.py:422
  103.2 0.0 copy-done.1
  103.2 10.8 %shard_map.95 = (bf16[8192,512]{1,0:T(8,128)(2,1)}, bf16[128,512]{1,0:T(8,128)(2,1)}) custom-call(s32[3]{0:T(128)S(1)} %pad_add_fusion.place, f32[8,32,512]{2,1,0:T(8,128)S(1)} %all-to-all-done.3.parts, f32[32,32]{1,0:T(8,128)S(1)} %get-tuple-element.40.after.metric, bf16[8192,96]{1,0:T(8,128)(2,1)S(1)} %get-tuple-element.42.left, ...), custom_call_target="tpu_custom_call" | custom-call | flops 805306368 | bytes 26214400 | tf_op jit(solution)/shard_map/pallas_call | solution.py:54
  (1 shorter events, 0.0 us)
Async XLA Ops:
  0.6 9.5 %collective-permute-start = (bf16[256,8192]{1,0:T(8,128)(2,1)}, bf16[256,8192]{1,0:T(8,128)(2,1)}, u32[]{:S(2)}, u32[]{:S(2)}) collective-permute-start(bf16[256,8192]{1,0:T(8,128)(2,1)} %acts.5), channel_id=1, source_target_pairs={{0,1},{1,0},{2,3},{3,2},{4,5},{5,4},{6,7},{7,6},{8,9},{9,8},{10,11... | collective-permute-start | bytes 12582920 | tf_op jit(solution)/shard_map/ppermute | solution.py:307
  10.1 15.4 %copy-start = (bf16[512,512]{1,0:T(8,128)(2,1)S(1)}, bf16[512,512]{1,0:T(8,128)(2,1)}, u32[]{:S(2)}) copy-start(bf16[512,512]{1,0:T(8,128)(2,1)} %og.5) | copy-start | bytes 1572868
  14.0 25.5 %all-to-all-start = ((bf16[64,32,128]{2,1,0:T(8,128)(2,1)}), bf16[64,32,128]{2,1,0:T(8,128)(2,1)S(1)}, u32[]{:S(2)}, u32[]{:S(2)}) async-start(bf16[64,32,128]{2,1,0:T(8,128)(2,1)} %get-tuple-element.29), calls=%async_computation | async-start | bytes 1048576 | tf_op jit(solution)/shard_map/all_to_all | solution.py:335
  40.4 22.5 %all-to-all-start.1 = ((bf16[64,32,128]{2,1,0:T(8,128)(2,1)}), bf16[64,32,128]{2,1,0:T(8,128)(2,1)S(1)}, u32[]{:S(2)}, u32[]{:S(2)}) async-start(bf16[64,32,128]{2,1,0:T(8,128)(2,1)} %get-tuple-element.32), calls=%async_computation.1 | async-start | bytes 1048576 | tf_op jit(solution)/shard_map/all_to_all | solution.py:363
  62.9 28.7 %collective-permute-start.1 = (bf16[256,8192]{1,0:T(8,128)(2,1)}, bf16[256,8192]{1,0:T(8,128)(2,1)}, u32[]{:S(2)}, u32[]{:S(2)}) collective-permute-start(bf16[256,8192]{1,0:T(8,128)(2,1)} %get-tuple-element.45), channel_id=1, source_target_pairs={{0,1},{1,0},{2,3},{3,2},{4,5},{5,4},{6,7},{7,6},{8,9},{9,8},{10,11... | collective-permute-start | bytes 12582920 | tf_op jit(solution)/shard_map/ppermute | solution.py:391
  72.4 14.5 %all-to-all-start.2 = ((f32[8,32,512]{2,1,0:T(8,128)}), f32[8,32,512]{2,1,0:T(8,128)S(1)}, u32[]{:S(2)}, u32[]{:S(2)}) async-start(f32[8,32,512]{2,1,0:T(8,128)} %get-tuple-element.37), calls=%async_computation.2 | async-start | bytes 1048576 | tf_op jit(solution)/shard_map/all_to_all | solution.py:403
  87.7 15.4 %all-to-all-start.3 = ((f32[8,32,512]{2,1,0:T(8,128)}), f32[8,32,512]{2,1,0:T(8,128)S(1)}, u32[]{:S(2)}, u32[]{:S(2)}) async-start(f32[8,32,512]{2,1,0:T(8,128)} %get-tuple-element.41), calls=%async_computation.3 | async-start | bytes 1048576 | tf_op jit(solution)/shard_map/all_to_all | solution.py:422
  91.7 11.5 %copy-start.1 = (bf16[128,512]{1,0:T(8,128)(2,1)S(1)}, bf16[128,512]{1,0:T(8,128)(2,1)}, u32[]{:S(2)}) copy-start(bf16[128,512]{1,0:T(8,128)(2,1)} %momentum.1) | copy-start | bytes 393220

commit v3 on v2

v3 whole, which is shorter than its diff:
```python
import functools

import jax
import jax.numpy as jnp
from jax import lax
from jax.experimental import pallas as pl
from jax.experimental.pallas import tpu as pltpu
from jax.sharding import PartitionSpec as P

F32 = jnp.float32
BF16 = jnp.bfloat16
MIB = 1024 * 1024
BLOCK = 1024
CHUNK = 128
GROUP = 8

NN = (((1,), (0,)), ((), ()))
NT = (((1,), (1,)), ((), ()))
TN = (((0,), (0,)), ((), ()))

VMEM = pl.BlockSpec(memory_space=pltpu.VMEM)
SMEM = pl.BlockSpec(memory_space=pltpu.SMEM)
HBM = pl.BlockSpec(memory_space=pltpu.HBM)
TOKEN = jax.ShapeDtypeStruct((8, 128), jnp.float32)


def in_hbm(x):
    return pltpu.with_memory_space_constraint(x, pltpu.HBM)


def dot(a, b, dims=NN):
    return lax.dot_general(a, b, dims, preferred_element_type=F32)


def exact_dot(a, b, dims=NN):
    return lax.dot_general(a, b, dims, precision=lax.Precision.HIGHEST, preferred_element_type=F32)


def split3(x, axis=0):
    high = x.astype(BF16)
    rest = x - high.astype(F32)
    middle = rest.astype(BF16)
    low = (rest - middle.astype(F32)).astype(BF16)
    return jnp.concatenate([high, middle, low], axis=axis)


def sum3(x):
    rows = x.shape[0] // 3
    return x[:rows] + x[rows : 2 * rows] + x[2 * rows :]


def call(kernel, in_specs, out_specs, out_shape, args, flops, moved, scratch=(), aliases={}):
    args = [in_hbm(x) if spec is HBM else x for spec, x in zip(in_specs, args)]
    return pl.pallas_call(
        kernel,
        in_specs=in_specs,
        out_specs=out_specs,
        out_shape=out_shape,
        scratch_shapes=list(scratch),
        input_output_aliases=aliases,
        compiler_params=pltpu.CompilerParams(vmem_limit_bytes=48 * MIB),
        cost_estimate=pl.CostEstimate(flops=flops, bytes_accessed=moved, transcendentals=0),
    )(*args)


def halves(place, og, half):
    own = pl.multiple_of(place[0] * half, half)
    oth = pl.multiple_of(place[1] * half, half)
    return og[pl.ds(own, half), :], og[pl.ds(oth, half), :]


def blocks(width, size=BLOCK):
    return [slice(i, i + size) for i in range(0, width, size)]


class Reader:
    def __init__(self, pairs, sems, ahead=3):
        self.ahead = ahead
        self.copies = [
            [pltpu.make_async_copy(source, target, sems.at[i, j]) for j, (source, target) in enumerate(block)]
            for i, block in enumerate(pairs)
        ]
        for block in self.copies[: self.ahead]:
            for copy in block:
                copy.start()

    def wait(self, i):
        if i + self.ahead < len(self.copies):
            for copy in self.copies[i + self.ahead]:
                copy.start()
        for copy in self.copies[i]:
            copy.wait()


class Writer:
    def __init__(self, slots, sems):
        self.slots, self.sems, self.copies = slots, sems, []

    def put(self, value, target):
        at = len(self.copies)
        slot = at % self.slots.shape[0]
        if at >= self.slots.shape[0]:
            self.copies[at - self.slots.shape[0]].wait()
        self.slots[slot] = value
        copy = pltpu.make_async_copy(self.slots.at[slot], target, self.sems.at[slot])
        copy.start()
        self.copies.append(copy)

    def finish(self):
        for copy in self.copies[-self.slots.shape[0] :]:
            copy.wait()


def left_own_kernel(
    scale, place, q_hbm, og_hbm, acts, error, part, pq_oth, q, og, acts_here, error_here, sems, small_sems
):
    half, width = acts.shape
    rows = blocks(width)
    q_copy = pltpu.make_async_copy(q_hbm, q, small_sems.at[0])
    og_copy = pltpu.make_async_copy(og_hbm, og, small_sems.at[1])
    q_copy.start()
    reads = [[(error.at[at, :], error_here.at[at, :]), (acts.at[:, at], acts_here.at[:, at])] for at in rows]
    reader = Reader(reads, sems, ahead=2)
    og_copy.start()
    q_copy.wait()
    q3 = split3(q[...])
    for i, at in enumerate(rows):
        reader.wait(i)
        by_error = sum3(dot(error_here[at, :], q3, NT).T)
        if i == 0:
            og_copy.wait()
            og_own, og_oth = halves(place, og, half)
            pq3 = split3(sum3(dot(q3, og_own, NT)) * scale)
            pq_oth[...] = split3(sum3(dot(q3, og_oth, NT)) * scale)
        part[:, at] = by_error + sum3(dot(pq3, acts_here[:, at]))


def left_kernel(pq3, acts, part, left, token):
    token[...] = jnp.zeros_like(token)
    for at in blocks(acts.shape[1]):
        total = part[:, at] + sum3(dot(pq3[...], acts[:, at]))
        for i in range(BLOCK // CHUNK):
            left[at.start // CHUNK + i] = total[:, i * CHUNK : (i + 1) * CHUNK].astype(BF16)


def input_oth_kernel(place, og, weight, after, part, token, weight_here, slots, sems, out_sems):
    token[...] = jnp.zeros_like(token)
    half, width = part.shape
    rows = blocks(width)
    reader = Reader([[(weight.at[at, :], weight_here.at[at, :])] for at in rows], sems)
    _, oth = halves(place, og, half)
    writer = Writer(slots, out_sems)
    for i, at in enumerate(rows):
        reader.wait(i)
        writer.put(dot(oth, weight_here[at, :], NT).astype(BF16), part.at[:, at])
    writer.finish()


def pass_kernel(part, after, out):
    pass


def input_own_kernel(
    place, og, weight, received, gram, out, metric, token, weight_here, received_here, slots, sems, out_sems
):
    token[...] = jnp.zeros_like(token)
    half, width = received.shape
    rank = gram.shape[0]
    rows = blocks(width)
    reader = Reader(
        [[(weight.at[at, :], weight_here.at[at, :]), (received.at[:, at], received_here.at[:, at])] for at in rows],
        sems,
    )
    own, _ = halves(place, og, half)
    writer = Writer(slots, out_sems)
    steps = gram_schmidt(gram[...])
    for i, at in enumerate(rows):
        reader.wait(i)
        product = dot(own, weight_here[at, :], NT).astype(BF16)
        for _ in range(rank * i // len(rows), rank * (i + 1) // len(rows)):
            coeffs = next(steps)
        writer.put((product.astype(F32) + received_here[:, at].astype(F32)).astype(BF16), out.at[:, at])
    metric[...] = exact_dot(coeffs, coeffs, NT)
    writer.finish()


def left_sum_kernel(parts, after, out, token):
    token[...] = jnp.zeros_like(token)
    total = jnp.sum(parts[...].astype(F32), axis=0).astype(BF16)
    out[...] = jnp.broadcast_to(total[None], out.shape)


def right_kernel(
    scale, place, og, left, acts, acts_oth, error, right, gram, left_rows, stack, error_here, sems
):
    tokens, cols = og.shape
    half, width = acts.shape
    rows = blocks(width, BLOCK // 2)
    reader = Reader(
        [
            [
                (acts.at[:, at], stack.at[:half, at]),
                (acts_oth.at[:, at], stack.at[half:tokens, at]),
                (error.at[at, :], error_here.at[at, :]),
            ]
            for at in rows
        ],
        sems,
        ahead=8,
    )
    for i in range(left.shape[0]):
        stack[tokens:, i * CHUNK : (i + 1) * CHUNK] = left[i]
    left_rows[...] = stack[tokens:, :]
    by_stack, result = None, None
    for i, at in enumerate(rows):
        reader.wait(i)
        here = stack[tokens:, at]
        stack_term = dot(stack[:, at], here, NT)
        error_term = dot(here, error_here[at, :])
        by_stack = stack_term if by_stack is None else by_stack + stack_term
        result = error_term if result is None else result + error_term
    gram[...] = by_stack[tokens:]
    own, oth = halves(place, og, half)
    by_acts = split3(by_stack[:tokens] * scale, axis=1)
    result += sum3(dot(by_acts[:half], own, TN) + dot(by_acts[half:], oth, TN))
    for i in range(right.shape[0]):
        right[i] = result


def gram_schmidt(g):
    width = g.shape[0]
    rows = lax.broadcasted_iota(jnp.int32, (width, width), 0)
    columns = lax.broadcasted_iota(jnp.int32, (width, width), 1)
    coeffs = jnp.zeros((width, width), F32)
    products = jnp.zeros((width, width), F32)
    for k in range(width):
        along = products[k : k + 1]
        unit = (rows[:, :1] == k).astype(F32)
        v = unit - jnp.sum(along * coeffs, axis=1, keepdims=True)
        inner = g[:, k : k + 1] - jnp.sum(along * products, axis=1, keepdims=True)
        square = jnp.maximum(jnp.sum(v * inner, axis=0, keepdims=True), 0.0)
        inverse = lax.rsqrt(square + 1e-06)
        coeffs = jnp.where(columns == k, v * inverse, coeffs)
        products = jnp.where(columns == k, inner * inverse, products)
        yield coeffs


def right_sum_kernel(parts, after, out):
    total = jnp.sum(parts[...], axis=0)
    out[...] = jnp.broadcast_to(total[None], out.shape)


def final_kernel(
    scale, inverse_replicas, place, parts, metric, og, left_rows, momentum, acts, acts_oth, error,
    new_error, new_momentum, stack, rest, error_here, slots, sems, out_sems,
):
    tokens, cols = og.shape
    half, width = acts.shape
    rank = left_rows.shape[0]
    rows = blocks(width)
    reader = Reader(
        [
            [
                (acts.at[:, at], stack.at[:half, at]),
                (acts_oth.at[:, at], stack.at[half:tokens, at]),
                (error.at[at, :], error_here.at[at, :]),
            ]
            for at in rows
        ],
        sems,
    )
    for i in range(3):
        stack[tokens + i * rank : tokens + (i + 1) * rank, :] = left_rows[...]
    total = jnp.sum(parts[...], axis=0) * (-inverse_replicas / scale)
    own, oth = halves(place, og, half)
    rest[:half] = own
    rest[half:tokens] = oth
    rest[tokens:] = split3(exact_dot(metric[...], total))
    writer = Writer(slots, out_sems)
    for i, at in enumerate(rows):
        reader.wait(i)
        product = dot(stack[:, at], rest[...], TN)
        writer.put((product * scale + error_here[at, :].astype(F32)).astype(BF16), new_error.at[at, :])
    count = momentum.shape[0]
    mine = pl.ds(pl.multiple_of(place[2] * count, count), count)
    approx = dot(stack[tokens:, mine], rest[tokens:], TN) * -scale
    new_momentum[...] = (0.9 * momentum[...].astype(F32) + approx).astype(BF16)
    writer.finish()


def per_device(acts, out_grad, weight, error, momentum, q_init):
    tokens, cols = out_grad.shape
    half, width = acts.shape
    rank = q_init.shape[1]
    replicas = lax.axis_size("dp")
    scale = 1.0 / tokens**0.5
    core = lax.axis_index("tensor")
    place = jnp.stack([core, 1 - core, lax.axis_index("dp")]).astype(jnp.int32)
    swap = [(0, 1), (1, 0)]
    shape = jax.ShapeDtypeStruct
    near = [[g * GROUP + i for i in range(GROUP)] for g in range(replicas // GROUP)]
    far = [[i * (replicas // GROUP) + g for i in range(GROUP)] for g in range(replicas // GROUP)]
    dma = pltpu.SemaphoreType.DMA
    n_blocks = width // BLOCK

    acts_oth = lax.ppermute(acts, "tensor", swap)

    part, pq_oth = call(
        functools.partial(left_own_kernel, scale),
        [SMEM, HBM, HBM, HBM, HBM],
        [VMEM] * 2,
        [shape((rank, width), F32), shape((3 * rank, half), BF16)],
        (place, q_init.T, out_grad, acts, error),
        flops=2 * 96 * width * 768,
        moved=13 * MIB,
        scratch=[
            pltpu.VMEM((rank, cols), F32),
            pltpu.VMEM((tokens, cols), BF16),
            pltpu.VMEM((half, width), BF16),
            pltpu.VMEM((width, cols), BF16),
            dma((n_blocks, 2)),
            dma((2,)),
        ],
    )
    left_parts, left_done = call(
        left_kernel,
        [VMEM] * 3,
        [VMEM] * 2,
        [shape((replicas, rank, CHUNK), BF16), TOKEN],
        (pq_oth, acts_oth, part),
        flops=2 * 96 * width * 256,
        moved=6 * MIB,
    )
    gathered = lax.all_to_all(left_parts, "dp", 0, 0, tiled=True)
    oth_input, oth_done = call(
        input_oth_kernel,
        [SMEM, VMEM, HBM, VMEM],
        [HBM, VMEM],
        [pltpu.HBM((half, width), BF16), TOKEN],
        (place, out_grad, weight, left_done),
        flops=tokens * cols * width,
        moved=13 * MIB,
        scratch=[
            pltpu.VMEM((width, cols), BF16),
            pltpu.VMEM((4, half, BLOCK), BF16),
            dma((n_blocks, 1)),
            dma((4,)),
        ],
    )

    left_copies, sum_done = call(
        left_sum_kernel,
        [VMEM, VMEM],
        [VMEM, VMEM],
        [shape((replicas, rank, CHUNK), BF16), TOKEN],
        (gathered, oth_done),
        flops=replicas * rank * CHUNK,
        moved=MIB,
    )
    left = lax.all_to_all(left_copies, "dp", 0, 0, tiled=True)
    oth_input = call(
        pass_kernel,
        [HBM, VMEM],
        HBM,
        pltpu.HBM((half, width), BF16),
        (oth_input, sum_done),
        flops=1,
        moved=4096,
        aliases={0: 0},
    )
    received = lax.ppermute(oth_input, "tensor", swap)

    right_copies, gram, left_rows = call(
        functools.partial(right_kernel, scale),
        [SMEM, VMEM, VMEM, HBM, HBM, HBM],
        [VMEM] * 3,
        [shape((GROUP, rank, cols), F32), shape((rank, rank), F32), shape((rank, width), BF16)],
        (place, out_grad, left, acts, acts_oth, error),
        flops=2 * rank * width * 1024,
        moved=17 * MIB,
        scratch=[pltpu.VMEM((tokens + rank, width), BF16), pltpu.VMEM((width, cols), BF16), dma((2 * n_blocks, 3))],
    )
    first = lax.all_to_all(right_copies, "dp", 0, 0, tiled=True, axis_index_groups=near)
    input_grad, metric, input_done = call(
        input_own_kernel,
        [SMEM, VMEM, HBM, HBM, VMEM],
        [HBM, VMEM, VMEM],
        [pltpu.HBM((half, width), BF16), shape((rank, rank), F32), TOKEN],
        (place, out_grad, weight, received, gram),
        flops=tokens * cols * width,
        moved=17 * MIB,
        scratch=[
            pltpu.VMEM((width, cols), BF16),
            pltpu.VMEM((half, width), BF16),
            pltpu.VMEM((4, half, BLOCK), BF16),
            dma((n_blocks, 2)),
            dma((4,)),
        ],
    )
    second_copies = call(
        right_sum_kernel,
        [VMEM, VMEM],
        VMEM,
        shape((GROUP, rank, cols), F32),
        (first, input_done),
        flops=GROUP * rank * cols,
        moved=MIB,
    )
    second = lax.all_to_all(second_copies, "dp", 0, 0, tiled=True, axis_index_groups=far)
    new_error, new_momentum = call(
        functools.partial(final_kernel, scale, 1.0 / replicas),
        [SMEM, VMEM, VMEM, VMEM, VMEM, VMEM, HBM, HBM, HBM],
        [HBM, VMEM],
        [pltpu.HBM((width, cols), BF16), shape(momentum.shape, BF16)],
        (place, second, metric, out_grad, left_rows, momentum, acts, acts_oth, error),
        flops=2 * (tokens + 3 * rank) * width * cols,
        moved=25 * MIB,
        scratch=[
            pltpu.VMEM((tokens + 3 * rank, width), BF16),
            pltpu.VMEM((tokens + 3 * rank, cols), BF16),
            pltpu.VMEM((width, cols), BF16),
            pltpu.VMEM((4, BLOCK, cols), BF16),
            dma((n_blocks, 3)),
            dma((4,)),
        ],
    )
    return (new_error, new_momentum, input_grad)


def solution(mesh):
    return jax.shard_map(
        per_device,
        mesh=mesh,
        in_specs=(
            P(("dp", "tensor"), None),
            P("dp", "tensor"),
            P(None, "tensor"),
            P("dp", "tensor"),
            P("dp", "tensor"),
            P("tensor", None),
        ),
        out_specs=(P("dp", "tensor"), P("dp", "tensor"), P(("dp", "tensor"), None)),
        check_vma=False,
    )
```

time: 115 us -> 107 us (0.930)
  blocking collectives: 0 us -> 32.5 us
  Pallas kernels: 68.4 us -> 50 us
  starting transfers between devices: 28 us -> 15.2 us
  waiting for transfers between devices: 16.7 us -> 7.62 us
    all_to_all x0 -> x2, blocking collectives: none -> 32.5 us  [the longest x1 18.5 us: per_device(): left = lax.all_to_all(left_copies, 'dp', 0, 0, tiled=True)]
    pallas_call x11 -> x9, Pallas kernels: 68.4 us -> 50 us  [call(): pl.pallas_call(kernel, in_specs=in_specs, out_specs=out_specs, out_shape=...]
    all_to_all x2 -> x0, starting transfers between devices: 12.9 us -> none  [the longest x1 9.01 us: per_device(): left = lax.all_to_all(left_copies, 'dp', 0, 0, tiled=True)]
    all_to_all x2 -> x0, waiting for transfers between devices: 10.2 us -> none  [the longest x1 5.95 us: per_device(): lax.all_to_all(second_copies, 'dp', 0, 0, tiled=True, axis_index_groups=far)]
    all_to_all x1, waiting for transfers between devices: 1.34 us -> 7.38 us  [per_device(): gathered = lax.all_to_all(left_parts, 'dp', 0, 0, tiled=True)]
    all_to_all x1, waiting for transfers between devices: 5.13 us -> 0.24 us  [per_device(): lax.all_to_all(right_copies, 'dp', 0, 0, tiled=True, axis_index_groups=near)]
  transfers between devices with their start and end apart: 6 -> 4, of which waited for: 4 -> 2; matrix products, arithmetic and copies ran while one was open for 0% -> 0% of each run, Pallas kernels for 46% -> 31%
where the time goes in v3:
time: 107 us; the launch traced here: 106 us
  Pallas kernels  50 us (47%)
  blocking collectives  32.5 us (30%)
  starting transfers between devices  15.2 us (14%)
  waiting for transfers between devices  7.62 us (7%)
    pallas_call x9, Pallas kernels, call(): pl.pallas_call(kernel, in_specs=in_specs, out_specs=out_specs, out_shape=...  50 us
    all_to_all x1, blocking collectives, per_device(): left = lax.all_to_all(left_copies, 'dp', 0, 0, tiled=True)  18.5 us
    all_to_all x1, blocking collectives, per_device(): lax.all_to_all(second_copies, 'dp', 0, 0, tiled=True, axis_index_groups=far)  13.9 us
    all_to_all x1, starting transfers between devices, per_device(): gathered = lax.all_to_all(left_parts, 'dp', 0, 0, tiled=True)  11.5 us
    all_to_all x1, waiting for transfers between devices, per_device(): gathered = lax.all_to_all(left_parts, 'dp', 0, 0, tiled=True)  7.38 us
    all_to_all x1, starting transfers between devices, per_device(): lax.all_to_all(right_copies, 'dp', 0, 0, tiled=True, axis_index_groups=near)  3.51 us
  transfers between devices with their start and end apart: 4, of which 2 were waited for; matrix products, arithmetic and copies ran while one was open for 0% of the time, Pallas kernels for 31%

profile of v3, /device:TPU:0, one launch (start us, length us, event | category | flops | bytes accessed | tf_op | source)
XLA Modules:
  0.0 106.3 jit_solution(8531964280949446009)
XLA Ops:
  0.6 0.1 collective-permute-start
  0.7 0.1 pad_add_fusion.place
  0.8 8.5 %shard_map.85 = (f32[32,8192]{1,0:T(8,128)S(1)}, bf16[96,256]{1,0:T(8,128)(2,1)S(1)}) custom-call(s32[3]{0:T(128)S(1)} %pad_add_fusion.place, f32[32,512]{1,0:T(8,128)} %bitcast.4, bf16[512,512]{1,0:T(8,128)(2,1)} %og.7, bf16[256,8192]{1,0:T(8,128)(2,1)} %acts.5, bf16[8192,512]{1,0:T(8,128)(2,1)} %error.5), custom_call_target="tpu_custom_call" | custom-call | flops 1207959552 | bytes 13631488 | tf_op jit(solution)/shard_map/pallas_call | solution.py:54
  9.3 0.0 copy-start
  9.3 0.0 collective-permute-done.acts.acts_oth
  9.3 3.9 %shard_map.86 = (bf16[64,32,128]{2,1,0:T(8,128)(2,1)}, f32[8,128]{1,0:T(8,128)S(1)}) custom-call(bf16[96,256]{1,0:T(8,128)(2,1)S(1)} %get-tuple-element.19.pq3, bf16[256,8192]{1,0:T(8,128)(2,1)} %collective-permute-done.acts.acts_oth, f32[32,8192]{1,0:T(8,128)S(1)} %get-tuple-element.20.part), custom_call_target="tpu_custom_call" | custom-call | flops 402653184 | bytes 6291456 | tf_op jit(solution)/shard_map/pallas_call | solution.py:54
  13.2 11.5 %all-to-all-start = ((bf16[64,32,128]{2,1,0:T(8,128)(2,1)}), bf16[64,32,128]{2,1,0:T(8,128)(2,1)S(1)}, u32[]{:S(2)}, u32[]{:S(2)}) async-start(bf16[64,32,128]{2,1,0:T(8,128)(2,1)} %get-tuple-element.21), calls=%async_computation | async-start | bytes 1048576 | tf_op jit(solution)/shard_map/all_to_all | solution.py:334
  24.7 0.0 copy-done
  24.7 6.6 %shard_map.87 = (bf16[256,8192]{1,0:T(8,128)(2,1)}, f32[8,128]{1,0:T(8,128)S(1)}) custom-call(s32[3]{0:T(128)S(1)} %pad_add_fusion.place, bf16[512,512]{1,0:T(8,128)(2,1)S(1)} %copy-done, bf16[8192,512]{1,0:T(8,128)(2,1)} %weight.3, f32[8,128]{1,0:T(8,128)S(1)} %get-tuple-element.22.after), custom_call_target="tpu_custom_call" | custom-call | flops 2147483648 | bytes 13631488 | tf_op jit(solution)/shard_map/pallas_call | solution.py:54
  31.3 7.4 %all-to-all-done.parts = bf16[64,32,128]{2,1,0:T(8,128)(2,1)S(1)} async-done(((bf16[64,32,128]{2,1,0:T(8,128)(2,1)}), bf16[64,32,128]{2,1,0:T(8,128)(2,1)S(1)}, u32[]{:S(2)}, u32[]{:S(2)}) %all-to-all-start) | async-done | bytes 524320 | tf_op jit(solution)/shard_map/all_to_all | solution.py:334
  38.7 0.1 shard_map.88
  38.8 0.1 collective-permute-start.1
  38.9 18.5 %all_to_all.20.left = bf16[64,32,128]{2,1,0:T(8,128)(2,1)S(1)} all-to-all(bf16[64,32,128]{2,1,0:T(8,128)(2,1)S(1)} %get-tuple-element.24), channel_id=1, replica_groups=mesh['dp'=64,'tensor'=2] {'dp'}, dimensions={0} | all-to-all | bytes 1048576 | tf_op jit(solution)/shard_map/all_to_all | solution.py:360
  57.5 8.9 %shard_map.89 = (f32[8,32,512]{2,1,0:T(8,128)}, f32[32,32]{1,0:T(8,128)S(1)}, bf16[32,8192]{1,0:T(8,128)(2,1)S(1)}) custom-call(s32[3]{0:T(128)S(1)} %pad_add_fusion.place, bf16[512,512]{1,0:T(8,128)(2,1)S(1)} %copy-done, bf16[64,32,128]{2,1,0:T(8,128)(2,1)S(1)} %all_to_all.20.left, bf16[256,8192]{1,0:T(8,128)(2,1)} %acts.5, ...), custom_call_target="tpu_custom_call" | custom-call | flops 536870912 | bytes 17825792 | tf_op jit(solution)/shard_map/pallas_call | solution.py:54
  66.4 3.5 %all-to-all-start.2 = ((f32[8,32,512]{2,1,0:T(8,128)}), f32[8,32,512]{2,1,0:T(8,128)S(1)}, u32[]{:S(2)}, u32[]{:S(2)}) async-start(f32[8,32,512]{2,1,0:T(8,128)} %get-tuple-element.25), calls=%async_computation.2 | async-start | bytes 1048576 | tf_op jit(solution)/shard_map/all_to_all | solution.py:383
  69.9 0.0 collective-permute-done.1.received
  69.9 0.0 copy-start.1
  70.0 9.2 %shard_map.91 = (bf16[256,8192]{1,0:T(8,128)(2,1)}, f32[32,32]{1,0:T(8,128)S(1)}, f32[8,128]{1,0:T(8,128)S(1)}) custom-call(s32[3]{0:T(128)S(1)} %pad_add_fusion.place, bf16[512,512]{1,0:T(8,128)(2,1)S(1)} %copy-done, bf16[8192,512]{1,0:T(8,128)(2,1)} %weight.3, bf16[256,8192]{1,0:T(8,128)(2,1)} %collective-permute-done.1.received, ...), custom_call_target="tpu_custom_call" | custom-call | flops 2147483648 | bytes 17825792 | tf_op jit(solution)/shard_map/pallas_call | solution.py:54
  79.2 0.2 all-to-all-done.2.parts
  79.4 13.9 %all_to_all.21.parts = f32[8,32,512]{2,1,0:T(8,128)S(1)} all-to-all(f32[8,32,512]{2,1,0:T(8,128)S(1)} %shard_map.92), channel_id=1, replica_groups={{0,16,32,48,64,80,96,112},{2,18,34,50,66,82,98,114},{4,20,36,52,68,84,1..., dimensions={0} | all-to-all | bytes 1048576 | tf_op jit(solution)/shard_map/all_to_all | solution.py:409
  93.4 0.0 copy-done.1
  93.4 12.7 %shard_map.93 = (bf16[8192,512]{1,0:T(8,128)(2,1)}, bf16[128,512]{1,0:T(8,128)(2,1)}) custom-call(s32[3]{0:T(128)S(1)} %pad_add_fusion.place, f32[8,32,512]{2,1,0:T(8,128)S(1)} %all_to_all.21.parts, f32[32,32]{1,0:T(8,128)S(1)} %get-tuple-element.30.metric, bf16[512,512]{1,0:T(8,128)(2,1)S(1)} %copy-done, bf16[32,8192]{1,0:T(8,128)(2,1)S(1)} %get-tuple-element.31.left_rows, ...), custom_call_target="tpu_custom_call" | custom-call | flops 5100273664 | bytes 26214400 | tf_op jit(solution)/shard_map/pallas_call | solution.py:54
  (2 shorter events, 0.0 us)
Async XLA Ops:
  0.6 8.7 %collective-permute-start = (bf16[256,8192]{1,0:T(8,128)(2,1)}, bf16[256,8192]{1,0:T(8,128)(2,1)}, u32[]{:S(2)}, u32[]{:S(2)}) collective-permute-start(bf16[256,8192]{1,0:T(8,128)(2,1)} %acts.5), channel_id=1, source_target_pairs={{0,1},{1,0},{2,3},{3,2},{4,5},{5,4},{6,7},{7,6},{8,9},{9,8},{10,11... | collective-permute-start | bytes 12582920 | tf_op jit(solution)/shard_map/ppermute | solution.py:306
  9.3 15.4 %copy-start = (bf16[512,512]{1,0:T(8,128)(2,1)S(1)}, bf16[512,512]{1,0:T(8,128)(2,1)}, u32[]{:S(2)}) copy-start(bf16[512,512]{1,0:T(8,128)(2,1)} %og.7) | copy-start | bytes 1572868
  13.2 25.5 %all-to-all-start = ((bf16[64,32,128]{2,1,0:T(8,128)(2,1)}), bf16[64,32,128]{2,1,0:T(8,128)(2,1)S(1)}, u32[]{:S(2)}, u32[]{:S(2)}) async-start(bf16[64,32,128]{2,1,0:T(8,128)(2,1)} %get-tuple-element.21), calls=%async_computation | async-start | bytes 1048576 | tf_op jit(solution)/shard_map/all_to_all | solution.py:334
  38.8 31.1 %collective-permute-start.1 = (bf16[256,8192]{1,0:T(8,128)(2,1)}, bf16[256,8192]{1,0:T(8,128)(2,1)}, u32[]{:S(2)}, u32[]{:S(2)}) collective-permute-start(bf16[256,8192]{1,0:T(8,128)(2,1)} %shard_map.90), channel_id=1, source_target_pairs={{0,1},{1,0},{2,3},{3,2},{4,5},{5,4},{6,7},{7,6},{8,9},{9,8},{10,11... | collective-permute-start | bytes 12582920 | tf_op jit(solution)/shard_map/ppermute | solution.py:371
  66.4 13.0 %all-to-all-start.2 = ((f32[8,32,512]{2,1,0:T(8,128)}), f32[8,32,512]{2,1,0:T(8,128)S(1)}, u32[]{:S(2)}, u32[]{:S(2)}) async-start(f32[8,32,512]{2,1,0:T(8,128)} %get-tuple-element.25), calls=%async_computation.2 | async-start | bytes 1048576 | tf_op jit(solution)/shard_map/all_to_all | solution.py:383
  69.9 23.4 %copy-start.1 = (bf16[128,512]{1,0:T(8,128)(2,1)S(1)}, bf16[128,512]{1,0:T(8,128)(2,1)}, u32[]{:S(2)}) copy-start(bf16[128,512]{1,0:T(8,128)(2,1)} %momentum.1) | copy-start | bytes 393220

commit v4 on v3

--- a/solution.py
+++ b/solution.py
@@ -19,7 +19,6 @@
 TN = (((0,), (0,)), ((), ()))
 
 VMEM = pl.BlockSpec(memory_space=pltpu.VMEM)
-SMEM = pl.BlockSpec(memory_space=pltpu.SMEM)
 HBM = pl.BlockSpec(memory_space=pltpu.HBM)
 TOKEN = jax.ShapeDtypeStruct((8, 128), jnp.float32)
 
@@ -63,9 +62,10 @@
     )(*args)
 
 
-def halves(place, og, half):
-    own = pl.multiple_of(place[0] * half, half)
-    oth = pl.multiple_of(place[1] * half, half)
+def halves(og, half):
+    core = lax.axis_index("tensor")
+    own = pl.multiple_of(core * half, half)
+    oth = pl.multiple_of((1 - core) * half, half)
     return og[pl.ds(own, half), :], og[pl.ds(oth, half), :]
 
 
@@ -101,8 +101,9 @@
         slot = at % self.slots.shape[0]
         if at >= self.slots.shape[0]:
             self.copies[at - self.slots.shape[0]].wait()
-        self.slots[slot] = value
-        copy = pltpu.make_async_copy(self.slots.at[slot], target, self.sems.at[slot])
+        rows = value.shape[0]
+        self.slots[slot, :rows] = value
+        copy = pltpu.make_async_copy(self.slots.at[slot, :rows], target, self.sems.at[slot])
         copy.start()
         self.copies.append(copy)
 
@@ -112,7 +113,7 @@
 
 
 def left_own_kernel(
-    scale, place, q_hbm, og_hbm, acts, error, part, pq_oth, q, og, acts_here, error_here, sems, small_sems
+    scale, q_hbm, og_hbm, acts, error, part, pq_oth, q, og, acts_here, error_here, sems, small_sems
 ):
     half, width = acts.shape
     rows = blocks(width)
@@ -129,26 +130,35 @@
         by_error = sum3(dot(error_here[at, :], q3, NT).T)
         if i == 0:
             og_copy.wait()
-            og_own, og_oth = halves(place, og, half)
+            og_own, og_oth = halves(og, half)
             pq3 = split3(sum3(dot(q3, og_own, NT)) * scale)
             pq_oth[...] = split3(sum3(dot(q3, og_oth, NT)) * scale)
         part[:, at] = by_error + sum3(dot(pq3, acts_here[:, at]))
 
 
-def left_kernel(pq3, acts, part, left, token):
+def left_kernel(pq3, acts, part, left, acts_kept, token, here, sems):
     token[...] = jnp.zeros_like(token)
-    for at in blocks(acts.shape[1]):
+    rows = blocks(acts.shape[1])
+    copies = [pltpu.make_async_copy(acts, acts_kept, sems.at[len(rows)])]
+    copies[0].start()
+    for i, at in enumerate(rows):
         total = part[:, at] + sum3(dot(pq3[...], acts[:, at]))
-        for i in range(BLOCK // CHUNK):
-            left[at.start // CHUNK + i] = total[:, i * CHUNK : (i + 1) * CHUNK].astype(BF16)
-
-
-def input_oth_kernel(place, og, weight, after, part, token, weight_here, slots, sems, out_sems):
+        count = BLOCK // CHUNK
+        chunks = slice(i * count, (i + 1) * count)
+        for j in range(count):
+            here[i * count + j] = total[:, j * CHUNK : (j + 1) * CHUNK].astype(BF16)
+        copies.append(pltpu.make_async_copy(here.at[chunks], left.at[chunks], sems.at[i]))
+        copies[-1].start()
+    for copy in copies:
+        copy.wait()
+
+
+def input_oth_kernel(og, weight, after, part, token, weight_here, slots, sems, out_sems):
     token[...] = jnp.zeros_like(token)
     half, width = part.shape
     rows = blocks(width)
     reader = Reader([[(weight.at[at, :], weight_here.at[at, :])] for at in rows], sems)
-    _, oth = halves(place, og, half)
+    _, oth = halves(og, half)
     writer = Writer(slots, out_sems)
     for i, at in enumerate(rows):
         reader.wait(i)
@@ -161,7 +171,7 @@
 
 
 def input_own_kernel(
-    place, og, weight, received, gram, out, metric, token, weight_here, received_here, slots, sems, out_sems
+    og, weight, received, gram, out, metric, token, weight_here, received_here, slots, sems, out_sems
 ):
     token[...] = jnp.zeros_like(token)
     half, width = received.shape
@@ -171,13 +181,16 @@
         [[(weight.at[at, :], weight_here.at[at, :]), (received.at[:, at], received_here.at[:, at])] for at in rows],
         sems,
     )
-    own, _ = halves(place, og, half)
+    own, _ = halves(og, half)
     writer = Writer(slots, out_sems)
     steps = gram_schmidt(gram[...])
+    first = rank // 4
+    for _ in range(first):
+        coeffs = next(steps)
     for i, at in enumerate(rows):
         reader.wait(i)
         product = dot(own, weight_here[at, :], NT).astype(BF16)
-        for _ in range(rank * i // len(rows), rank * (i + 1) // len(rows)):
+        for _ in range((rank - first) * i // len(rows), (rank - first) * (i + 1) // len(rows)):
             coeffs = next(steps)
         writer.put((product.astype(F32) + received_here[:, at].astype(F32)).astype(BF16), out.at[:, at])
     metric[...] = exact_dot(coeffs, coeffs, NT)
@@ -191,7 +204,7 @@
 
 
 def right_kernel(
-    scale, place, og, left, acts, acts_oth, error, right, gram, left_rows, stack, error_here, sems
+    scale, og, left, acts, acts_oth, error, right, gram, left_rows, stack, error_here, right_here, sems, out_sems
 ):
     tokens, cols = og.shape
     half, width = acts.shape
@@ -210,7 +223,8 @@
     )
     for i in range(left.shape[0]):
         stack[tokens:, i * CHUNK : (i + 1) * CHUNK] = left[i]
-    left_rows[...] = stack[tokens:, :]
+    left_copy = pltpu.make_async_copy(stack.at[tokens:, :], left_rows, out_sems.at[0])
+    left_copy.start()
     by_stack, result = None, None
     for i, at in enumerate(rows):
         reader.wait(i)
@@ -220,11 +234,18 @@
         by_stack = stack_term if by_stack is None else by_stack + stack_term
         result = error_term if result is None else result + error_term
     gram[...] = by_stack[tokens:]
-    own, oth = halves(place, og, half)
+    own, oth = halves(og, half)
     by_acts = split3(by_stack[:tokens] * scale, axis=1)
     result += sum3(dot(by_acts[:half], own, TN) + dot(by_acts[half:], oth, TN))
-    for i in range(right.shape[0]):
-        right[i] = result
+    right_here[...] = result
+    copies = [
+        pltpu.make_async_copy(right_here, right.at[i], out_sems.at[1 + i]) for i in range(right.shape[0])
+    ]
+    for copy in copies:
+        copy.start()
+    for copy in copies:
+        copy.wait()
+    left_copy.wait()
 
 
 def gram_schmidt(g):
@@ -251,7 +272,7 @@
 
 
 def final_kernel(
-    scale, inverse_replicas, place, parts, metric, og, left_rows, momentum, acts, acts_oth, error,
+    scale, inverse_replicas, parts, metric, og, left_rows, momentum, acts, acts_oth, error,
     new_error, new_momentum, stack, rest, error_here, slots, sems, out_sems,
 ):
     tokens, cols = og.shape
@@ -272,7 +293,7 @@
     for i in range(3):
         stack[tokens + i * rank : tokens + (i + 1) * rank, :] = left_rows[...]
     total = jnp.sum(parts[...], axis=0) * (-inverse_replicas / scale)
-    own, oth = halves(place, og, half)
+    own, oth = halves(og, half)
     rest[:half] = own
     rest[half:tokens] = oth
     rest[tokens:] = split3(exact_dot(metric[...], total))
@@ -282,7 +303,7 @@
         product = dot(stack[:, at], rest[...], TN)
         writer.put((product * scale + error_here[at, :].astype(F32)).astype(BF16), new_error.at[at, :])
     count = momentum.shape[0]
-    mine = pl.ds(pl.multiple_of(place[2] * count, count), count)
+    mine = pl.ds(pl.multiple_of(lax.axis_index("dp") * count, count), count)
     approx = dot(stack[tokens:, mine], rest[tokens:], TN) * -scale
     new_momentum[...] = (0.9 * momentum[...].astype(F32) + approx).astype(BF16)
     writer.finish()
@@ -294,8 +315,6 @@
     rank = q_init.shape[1]
     replicas = lax.axis_size("dp")
     scale = 1.0 / tokens**0.5
-    core = lax.axis_index("tensor")
-    place = jnp.stack([core, 1 - core, lax.axis_index("dp")]).astype(jnp.int32)
     swap = [(0, 1), (1, 0)]
     shape = jax.ShapeDtypeStruct
     near = [[g * GROUP + i for i in range(GROUP)] for g in range(replicas // GROUP)]
@@ -307,10 +326,10 @@
 
     part, pq_oth = call(
         functools.partial(left_own_kernel, scale),
-        [SMEM, HBM, HBM, HBM, HBM],
+        [HBM, HBM, HBM, HBM],
         [VMEM] * 2,
         [shape((rank, width), F32), shape((3 * rank, half), BF16)],
-        (place, q_init.T, out_grad, acts, error),
+        (q_init.T, out_grad, acts, error),
         flops=2 * 96 * width * 768,
         moved=13 * MIB,
         scratch=[
@@ -322,22 +341,23 @@
             dma((2,)),
         ],
     )
-    left_parts, left_done = call(
+    left_parts, acts_oth, left_done = call(
         left_kernel,
         [VMEM] * 3,
-        [VMEM] * 2,
-        [shape((replicas, rank, CHUNK), BF16), TOKEN],
+        [HBM, HBM, VMEM],
+        [pltpu.HBM((replicas, rank, CHUNK), BF16), pltpu.HBM((half, width), BF16), TOKEN],
         (pq_oth, acts_oth, part),
         flops=2 * 96 * width * 256,
         moved=6 * MIB,
+        scratch=[pltpu.VMEM((replicas, rank, CHUNK), BF16), dma((n_blocks + 1,))],
     )
     gathered = lax.all_to_all(left_parts, "dp", 0, 0, tiled=True)
     oth_input, oth_done = call(
         input_oth_kernel,
-        [SMEM, VMEM, HBM, VMEM],
+        [VMEM, HBM, VMEM],
         [HBM, VMEM],
         [pltpu.HBM((half, width), BF16), TOKEN],
-        (place, out_grad, weight, left_done),
+        (out_grad, weight, left_done),
         flops=tokens * cols * width,
         moved=13 * MIB,
         scratch=[
@@ -372,21 +392,21 @@
 
     right_copies, gram, left_rows = call(
         functools.partial(right_kernel, scale),
-        [SMEM, VMEM, VMEM, HBM, HBM, HBM],
-        [VMEM] * 3,
-        [shape((GROUP, rank, cols), F32), shape((rank, rank), F32), shape((rank, width), BF16)],
-        (place, out_grad, left, acts, acts_oth, error),
+        [VMEM, VMEM, HBM, HBM, HBM],
+        [HBM, VMEM, HBM],
+        [pltpu.HBM((GROUP, rank, cols), F32), shape((rank, rank), F32), pltpu.HBM((rank, width), BF16)],
+        (out_grad, left, acts, acts_oth, error),
         flops=2 * rank * width * 1024,
         moved=17 * MIB,
-        scratch=[pltpu.VMEM((tokens + rank, width), BF16), pltpu.VMEM((width, cols), BF16), dma((2 * n_blocks, 3))],
+        scratch=[pltpu.VMEM((tokens + rank, width), BF16), pltpu.VMEM((width, cols), BF16), pltpu.VMEM((rank, cols), F32), dma((2 * n_blocks, 3)), dma((1 + GROUP,))],
     )
     first = lax.all_to_all(right_copies, "dp", 0, 0, tiled=True, axis_index_groups=near)
     input_grad, metric, input_done = call(
         input_own_kernel,
-        [SMEM, VMEM, HBM, HBM, VMEM],
+        [VMEM, HBM, HBM, VMEM],
         [HBM, VMEM, VMEM],
         [pltpu.HBM((half, width), BF16), shape((rank, rank), F32), TOKEN],
-        (place, out_grad, weight, received, gram),
+        (out_grad, weight, received, gram),
         flops=tokens * cols * width,
         moved=17 * MIB,
         scratch=[
@@ -409,10 +429,10 @@
     second = lax.all_to_all(second_copies, "dp", 0, 0, tiled=True, axis_index_groups=far)
     new_error, new_momentum = call(
         functools.partial(final_kernel, scale, 1.0 / replicas),
-        [SMEM, VMEM, VMEM, VMEM, VMEM, VMEM, HBM, HBM, HBM],
+        [VMEM, VMEM, VMEM, VMEM, VMEM, HBM, HBM, HBM],
         [HBM, VMEM],
         [pltpu.HBM((width, cols), BF16), shape(momentum.shape, BF16)],
-        (place, second, metric, out_grad, left_rows, momentum, acts, acts_oth, error),
+        (second, metric, out_grad, left_rows, momentum, acts, acts_oth, error),
         flops=2 * (tokens + 3 * rank) * width * cols,
         moved=25 * MIB,
         scratch=[

time: 107 us -> 104 us (0.972)
  Pallas kernels: 50 us -> 44.8 us
  waiting for transfers between devices: 7.62 us -> 9.81 us
    pallas_call x9, Pallas kernels: 50 us -> 44.8 us  [call(): pl.pallas_call(kernel, in_specs=in_specs, out_specs=out_specs, out_shape=...]
    all_to_all x1, waiting for transfers between devices: 0.24 us -> 1.89 us  [per_device(): lax.all_to_all(right_copies, 'dp', 0, 0, tiled=True, axis_index_groups=near)]
  transfers between devices with their start and end apart: 4 -> 4, of which waited for: 2 -> 2; matrix products, arithmetic and copies ran while one was open for 0% -> 0% of each run, Pallas kernels for 31% -> 29%
where the time goes in v4:
time: 104 us; the launch traced here: 103 us
  Pallas kernels  44.8 us (43%)
  blocking collectives  32.5 us (31%)
  starting transfers between devices  15.2 us (15%)
  waiting for transfers between devices  9.81 us (9%)
    pallas_call x9, Pallas kernels, call(): pl.pallas_call(kernel, in_specs=in_specs, out_specs=out_specs, out_shape=...  44.8 us
    all_to_all x1, blocking collectives, per_device(): left = lax.all_to_all(left_copies, 'dp', 0, 0, tiled=True)  18.5 us
    all_to_all x1, blocking collectives, per_device(): lax.all_to_all(second_copies, 'dp', 0, 0, tiled=True, axis_index_groups=far)  13.9 us
    all_to_all x1, starting transfers between devices, per_device(): gathered = lax.all_to_all(left_parts, 'dp', 0, 0, tiled=True)  11.5 us
    all_to_all x1, waiting for transfers between devices, per_device(): gathered = lax.all_to_all(left_parts, 'dp', 0, 0, tiled=True)  7.92 us
    all_to_all x1, starting transfers between devices, per_device(): lax.all_to_all(right_copies, 'dp', 0, 0, tiled=True, axis_index_groups=near)  3.51 us
  transfers between devices with their start and end apart: 4, of which 2 were waited for; matrix products, arithmetic and copies ran while one was open for 0% of the time, Pallas kernels for 29%

profile of v4, /device:TPU:0, one launch (start us, length us, event | category | flops | bytes accessed | tf_op | source)
XLA Modules:
  0.0 103.2 jit_solution(1912032276143785966)
XLA Ops:
  0.6 0.1 collective-permute-start
  0.7 7.9 %shard_map.85 = (f32[32,8192]{1,0:T(8,128)S(1)}, bf16[96,256]{1,0:T(8,128)(2,1)S(1)}) custom-call(f32[32,512]{1,0:T(8,128)} %bitcast.1, bf16[512,512]{1,0:T(8,128)(2,1)} %og.7, bf16[256,8192]{1,0:T(8,128)(2,1)} %acts.5, bf16[8192,512]{1,0:T(8,128)(2,1)} %error.5), custom_call_target="tpu_custom_call" | custom-call | flops 1207959552 | bytes 13631488 | tf_op jit(solution)/shard_map/pallas_call | solution.py:53
  8.7 0.0 copy-start
  8.7 0.0 collective-permute-done.acts
  8.7 2.2 %shard_map.86 = (bf16[64,32,128]{2,1,0:T(8,128)(2,1)}, bf16[256,8192]{1,0:T(8,128)(2,1)}, f32[8,128]{1,0:T(8,128)S(1)}) custom-call(bf16[96,256]{1,0:T(8,128)(2,1)S(1)} %get-tuple-element.20.pq3, bf16[256,8192]{1,0:T(8,128)(2,1)S(1)} %collective-permute-done.acts, f32[32,8192]{1,0:T(8,128)S(1)} %get-tuple-element.21.part), custom_call_target="tpu_custom_call" | custom-call | flops 402653184 | bytes 6291456 | tf_op jit(solution)/shard_map/pallas_call | solution.py:53
  10.9 11.5 %all-to-all-start = ((bf16[64,32,128]{2,1,0:T(8,128)(2,1)}), bf16[64,32,128]{2,1,0:T(8,128)(2,1)S(1)}, u32[]{:S(2)}, u32[]{:S(2)}) async-start(bf16[64,32,128]{2,1,0:T(8,128)(2,1)} %get-tuple-element.22), calls=%async_computation | async-start | bytes 1048576 | tf_op jit(solution)/shard_map/all_to_all | solution.py:354
  22.4 0.0 copy-done
  22.5 6.1 %shard_map.87 = (bf16[256,8192]{1,0:T(8,128)(2,1)}, f32[8,128]{1,0:T(8,128)S(1)}) custom-call(bf16[512,512]{1,0:T(8,128)(2,1)S(1)} %copy-done, bf16[8192,512]{1,0:T(8,128)(2,1)} %weight.3, f32[8,128]{1,0:T(8,128)S(1)} %get-tuple-element.23.after), custom_call_target="tpu_custom_call" | custom-call | flops 2147483648 | bytes 13631488 | tf_op jit(solution)/shard_map/pallas_call | solution.py:53
  28.5 7.9 %all-to-all-done.parts = bf16[64,32,128]{2,1,0:T(8,128)(2,1)S(1)} async-done(((bf16[64,32,128]{2,1,0:T(8,128)(2,1)}), bf16[64,32,128]{2,1,0:T(8,128)(2,1)S(1)}, u32[]{:S(2)}, u32[]{:S(2)}) %all-to-all-start) | async-done | bytes 524320 | tf_op jit(solution)/shard_map/all_to_all | solution.py:354
  36.5 0.1 shard_map.88
  36.6 0.1 collective-permute-start.1
  36.7 18.5 %all_to_all.20.left = bf16[64,32,128]{2,1,0:T(8,128)(2,1)S(1)} all-to-all(bf16[64,32,128]{2,1,0:T(8,128)(2,1)S(1)} %get-tuple-element.25), channel_id=1, replica_groups=mesh['dp'=64,'tensor'=2] {'dp'}, dimensions={0} | all-to-all | bytes 1048576 | tf_op jit(solution)/shard_map/all_to_all | solution.py:380
  55.2 8.6 %shard_map.89 = (f32[8,32,512]{2,1,0:T(8,128)}, f32[32,32]{1,0:T(8,128)S(1)}, bf16[32,8192]{1,0:T(8,128)(2,1)}) custom-call(bf16[512,512]{1,0:T(8,128)(2,1)S(1)} %copy-done, bf16[64,32,128]{2,1,0:T(8,128)(2,1)S(1)} %all_to_all.20.left, bf16[256,8192]{1,0:T(8,128)(2,1)} %acts.5, bf16[256,8192]{1,0:T(8,128)(2,1)} %get-tuple-element.26.acts_oth, ...), custom_call_target="tpu_custom_call" | custom-call | flops 536870912 | bytes 17825792 | tf_op jit(solution)/shard_map/pallas_call | solution.py:53
  63.9 3.5 %all-to-all-start.2 = ((f32[8,32,512]{2,1,0:T(8,128)}), f32[8,32,512]{2,1,0:T(8,128)S(1)}, u32[]{:S(2)}, u32[]{:S(2)}) async-start(f32[8,32,512]{2,1,0:T(8,128)} %get-tuple-element.27), calls=%async_computation.2 | async-start | bytes 1048576 | tf_op jit(solution)/shard_map/all_to_all | solution.py:403
  67.4 0.0 collective-permute-done.1.received
  67.4 0.0 copy-start.1
  67.4 0.0 copy-start.2
  67.4 7.5 %shard_map.91 = (bf16[256,8192]{1,0:T(8,128)(2,1)}, f32[32,32]{1,0:T(8,128)S(1)}, f32[8,128]{1,0:T(8,128)S(1)}) custom-call(bf16[512,512]{1,0:T(8,128)(2,1)S(1)} %copy-done, bf16[8192,512]{1,0:T(8,128)(2,1)} %weight.3, bf16[256,8192]{1,0:T(8,128)(2,1)} %collective-permute-done.1.received, f32[32,32]{1,0:T(8,128)S(1)} %get-tuple-element.30.gram), custom_call_target="tpu_custom_call" | custom-call | flops 2147483648 | bytes 17825792 | tf_op jit(solution)/shard_map/pallas_call | solution.py:53
  75.0 1.9 %all-to-all-done.2.parts = f32[8,32,512]{2,1,0:T(8,128)S(1)} async-done(((f32[8,32,512]{2,1,0:T(8,128)}), f32[8,32,512]{2,1,0:T(8,128)S(1)}, u32[]{:S(2)}, u32[]{:S(2)}) %all-to-all-start.2) | async-done | bytes 524320 | tf_op jit(solution)/shard_map/all_to_all | solution.py:403
  76.9 13.9 %all_to_all.21.parts = f32[8,32,512]{2,1,0:T(8,128)S(1)} all-to-all(f32[8,32,512]{2,1,0:T(8,128)S(1)} %shard_map.92), channel_id=1, replica_groups={{0,16,32,48,64,80,96,112},{2,18,34,50,66,82,98,114},{4,20,36,52,68,84,1..., dimensions={0} | all-to-all | bytes 1048576 | tf_op jit(solution)/shard_map/all_to_all | solution.py:429
  90.8 0.0 copy-done.1
  90.8 0.0 copy-done.2
  90.8 12.2 %shard_map.93 = (bf16[8192,512]{1,0:T(8,128)(2,1)}, bf16[128,512]{1,0:T(8,128)(2,1)}) custom-call(f32[8,32,512]{2,1,0:T(8,128)S(1)} %all_to_all.21.parts, f32[32,32]{1,0:T(8,128)S(1)} %get-tuple-element.32.metric, bf16[512,512]{1,0:T(8,128)(2,1)S(1)} %copy-done, bf16[32,8192]{1,0:T(8,128)(2,1)S(1)} %copy-done.1, bf16[128,512]{1,0:T(8,128)(2,1)S(1)} %copy-done.2, ...), custom_call_target="tpu_custom_call" | custom-call | flops 5100273664 | bytes 26214400 | tf_op jit(solution)/shard_map/pallas_call | solution.py:53
  (2 shorter events, 0.0 us)
Async XLA Ops:
  0.6 8.1 %collective-permute-start = (bf16[256,8192]{1,0:T(8,128)(2,1)}, bf16[256,8192]{1,0:T(8,128)(2,1)S(1)}, u32[]{:S(2)}, u32[]{:S(2)}) collective-permute-start(bf16[256,8192]{1,0:T(8,128)(2,1)} %acts.5), channel_id=1, source_target_pairs={{0,1},{1,0},{2,3},{3,2},{4,5},{5,4},{6,7},{7,6},{8,9},{9,8},{10,11... | collective-permute-start | bytes 12582920 | tf_op jit(solution)/shard_map/ppermute | solution.py:325
  8.7 13.8 %copy-start = (bf16[512,512]{1,0:T(8,128)(2,1)S(1)}, bf16[512,512]{1,0:T(8,128)(2,1)}, u32[]{:S(2)}) copy-start(bf16[512,512]{1,0:T(8,128)(2,1)} %og.7) | copy-start | bytes 1572868
  10.9 25.5 %all-to-all-start = ((bf16[64,32,128]{2,1,0:T(8,128)(2,1)}), bf16[64,32,128]{2,1,0:T(8,128)(2,1)S(1)}, u32[]{:S(2)}, u32[]{:S(2)}) async-start(bf16[64,32,128]{2,1,0:T(8,128)(2,1)} %get-tuple-element.22), calls=%async_computation | async-start | bytes 1048576 | tf_op jit(solution)/shard_map/all_to_all | solution.py:354
  36.6 30.8 %collective-permute-start.1 = (bf16[256,8192]{1,0:T(8,128)(2,1)}, bf16[256,8192]{1,0:T(8,128)(2,1)}, u32[]{:S(2)}, u32[]{:S(2)}) collective-permute-start(bf16[256,8192]{1,0:T(8,128)(2,1)} %shard_map.90), channel_id=1, source_target_pairs={{0,1},{1,0},{2,3},{3,2},{4,5},{5,4},{6,7},{7,6},{8,9},{9,8},{10,11... | collective-permute-start | bytes 12582920 | tf_op jit(solution)/shard_map/ppermute | solution.py:391
  63.9 13.0 %all-to-all-start.2 = ((f32[8,32,512]{2,1,0:T(8,128)}), f32[8,32,512]{2,1,0:T(8,128)S(1)}, u32[]{:S(2)}, u32[]{:S(2)}) async-start(f32[8,32,512]{2,1,0:T(8,128)} %get-tuple-element.27), calls=%async_computation.2 | async-start | bytes 1048576 | tf_op jit(solution)/shard_map/all_to_all | solution.py:403
  67.4 23.4 %copy-start.1 = (bf16[32,8192]{1,0:T(8,128)(2,1)S(1)}, bf16[32,8192]{1,0:T(8,128)(2,1)}, u32[]{:S(2)}) copy-start(bf16[32,8192]{1,0:T(8,128)(2,1)} %get-tuple-element.33.left_rows) | copy-start | bytes 1572868
  67.4 23.4 %copy-start.2 = (bf16[128,512]{1,0:T(8,128)(2,1)S(1)}, bf16[128,512]{1,0:T(8,128)(2,1)}, u32[]{:S(2)}) copy-start(bf16[128,512]{1,0:T(8,128)(2,1)} %momentum.1) | copy-start | bytes 393220

commit v5 on v4

--- a/solution.py
+++ b/solution.py
@@ -12,7 +12,6 @@
 MIB = 1024 * 1024
 BLOCK = 1024
 CHUNK = 128
-GROUP = 8
 
 NN = (((1,), (0,)), ((), ()))
 NT = (((1,), (1,)), ((), ()))
@@ -170,41 +169,35 @@
     pass
 
 
-def input_own_kernel(
-    og, weight, received, gram, out, metric, token, weight_here, received_here, slots, sems, out_sems
-):
+def input_own_kernel(part, og, weight, received, after, *refs):
+    out, token, weight_here, slots, sems, out_sems = refs[part:]
     token[...] = jnp.zeros_like(token)
     half, width = received.shape
-    rank = gram.shape[0]
     rows = blocks(width)
-    reader = Reader(
-        [[(weight.at[at, :], weight_here.at[at, :]), (received.at[:, at], received_here.at[:, at])] for at in rows],
-        sems,
-    )
+    rows = rows[: len(rows) // 2] if part == 0 else rows[len(rows) // 2 :]
+    reader = Reader([[(weight.at[at, :], weight_here.at[at, :])] for at in rows], sems)
     own, _ = halves(og, half)
     writer = Writer(slots, out_sems)
-    steps = gram_schmidt(gram[...])
-    first = rank // 4
-    for _ in range(first):
-        coeffs = next(steps)
     for i, at in enumerate(rows):
         reader.wait(i)
         product = dot(own, weight_here[at, :], NT).astype(BF16)
-        for _ in range((rank - first) * i // len(rows), (rank - first) * (i + 1) // len(rows)):
-            coeffs = next(steps)
-        writer.put((product.astype(F32) + received_here[:, at].astype(F32)).astype(BF16), out.at[:, at])
+        writer.put((product.astype(F32) + received[:, at].astype(F32)).astype(BF16), out.at[:, at])
+    writer.finish()
+
+
+def gram_schmidt_kernel(gram, metric):
+    for coeffs in gram_schmidt(gram[...]):
+        pass
     metric[...] = exact_dot(coeffs, coeffs, NT)
-    writer.finish()
-
-
-def left_sum_kernel(parts, after, out, token):
-    token[...] = jnp.zeros_like(token)
+
+
+def left_sum_kernel(parts, after, out):
     total = jnp.sum(parts[...].astype(F32), axis=0).astype(BF16)
     out[...] = jnp.broadcast_to(total[None], out.shape)
 
 
 def right_kernel(
-    scale, og, left, acts, acts_oth, error, right, gram, left_rows, stack, error_here, right_here, sems, out_sems
+    scale, og, left, acts, acts_oth, error, right, gram, left_rows, stack, error_here, sems, out_sems
 ):
     tokens, cols = og.shape
     half, width = acts.shape
@@ -237,14 +230,7 @@
     own, oth = halves(og, half)
     by_acts = split3(by_stack[:tokens] * scale, axis=1)
     result += sum3(dot(by_acts[:half], own, TN) + dot(by_acts[half:], oth, TN))
-    right_here[...] = result
-    copies = [
-        pltpu.make_async_copy(right_here, right.at[i], out_sems.at[1 + i]) for i in range(right.shape[0])
-    ]
-    for copy in copies:
-        copy.start()
-    for copy in copies:
-        copy.wait()
+    right[...] = result
     left_copy.wait()
 
 
@@ -266,13 +252,13 @@
         yield coeffs
 
 
-def right_sum_kernel(parts, after, out):
-    total = jnp.sum(parts[...], axis=0)
-    out[...] = jnp.broadcast_to(total[None], out.shape)
+def right_sum_kernel(first, second, third, fourth, after, out, token):
+    token[...] = jnp.zeros_like(token)
+    out[...] = (first[...] + third[...]) + (second[...] + fourth[...])
 
 
 def final_kernel(
-    scale, inverse_replicas, parts, metric, og, left_rows, momentum, acts, acts_oth, error,
+    scale, inverse_replicas, first, second, third, fourth, metric, og, left_rows, momentum, after, acts, acts_oth, error,
     new_error, new_momentum, stack, rest, error_here, slots, sems, out_sems,
 ):
     tokens, cols = og.shape
@@ -292,7 +278,7 @@
     )
     for i in range(3):
         stack[tokens + i * rank : tokens + (i + 1) * rank, :] = left_rows[...]
-    total = jnp.sum(parts[...], axis=0) * (-inverse_replicas / scale)
+    total = ((first[...] + third[...]) + (second[...] + fourth[...])) * (-inverse_replicas / scale)
     own, oth = halves(og, half)
     rest[:half] = own
     rest[half:tokens] = oth
@@ -317,8 +303,44 @@
     scale = 1.0 / tokens**0.5
     swap = [(0, 1), (1, 0)]
     shape = jax.ShapeDtypeStruct
-    near = [[g * GROUP + i for i in range(GROUP)] for g in range(replicas // GROUP)]
-    far = [[i * (replicas // GROUP) + g for i in range(GROUP)] for g in range(replicas // GROUP)]
+    side = 4
+
+    def exchange(value, stride):
+        def to(step):
+            moved = lambda i: i + ((i // stride + step) % side - i // stride % side) * stride
+            return [(i, moved(i)) for i in range(replicas)]
+
+        return [value] + [lax.ppermute(value, "dp", to(step)) for step in range(1, side)]
+
+    def right_sum(values, after):
+        return call(
+            right_sum_kernel,
+            [VMEM] * (side + 1),
+            [VMEM] * 2,
+            [shape((rank, cols), F32), TOKEN],
+            (*values, after),
+            flops=side * rank * cols,
+            moved=MIB // 4,
+        )
+
+    def input_own(part, after, *first_part):
+        return call(
+            functools.partial(input_own_kernel, part),
+            [VMEM, HBM, VMEM, VMEM] + [HBM] * part,
+            [HBM, VMEM],
+            [pltpu.HBM((half, width), BF16), TOKEN],
+            (out_grad, weight, received, after, *first_part),
+            flops=tokens * cols * width // 2,
+            moved=8 * MIB,
+            scratch=[
+                pltpu.VMEM((width, cols), BF16),
+                pltpu.VMEM((4, half, BLOCK), BF16),
+                dma((n_blocks, 1)),
+                dma((4,)),
+            ],
+            aliases={4: 0} if part else {},
+        )
+
     dma = pltpu.SemaphoreType.DMA
     n_blocks = width // BLOCK
 
@@ -368,11 +390,11 @@
         ],
     )
 
-    left_copies, sum_done = call(
+    left_copies = call(
         left_sum_kernel,
         [VMEM, VMEM],
-        [VMEM, VMEM],
-        [shape((replicas, rank, CHUNK), BF16), TOKEN],
+        VMEM,
+        shape((replicas, rank, CHUNK), BF16),
         (gathered, oth_done),
         flops=replicas * rank * CHUNK,
         moved=MIB,
@@ -383,56 +405,39 @@
         [HBM, VMEM],
         HBM,
         pltpu.HBM((half, width), BF16),
-        (oth_input, sum_done),
+        (oth_input, left),
         flops=1,
         moved=4096,
         aliases={0: 0},
     )
     received = lax.ppermute(oth_input, "tensor", swap)
 
-    right_copies, gram, left_rows = call(
+    right, gram, left_rows = call(
         functools.partial(right_kernel, scale),
         [VMEM, VMEM, HBM, HBM, HBM],
-        [HBM, VMEM, HBM],
-        [pltpu.HBM((GROUP, rank, cols), F32), shape((rank, rank), F32), pltpu.HBM((rank, width), BF16)],
+        [VMEM, VMEM, HBM],
+        [shape((rank, cols), F32), shape((rank, rank), F32), pltpu.HBM((rank, width), BF16)],
         (out_grad, left, acts, acts_oth, error),
         flops=2 * rank * width * 1024,
         moved=17 * MIB,
-        scratch=[pltpu.VMEM((tokens + rank, width), BF16), pltpu.VMEM((width, cols), BF16), pltpu.VMEM((rank, cols), F32), dma((2 * n_blocks, 3)), dma((1 + GROUP,))],
-    )
-    first = lax.all_to_all(right_copies, "dp", 0, 0, tiled=True, axis_index_groups=near)
-    input_grad, metric, input_done = call(
-        input_own_kernel,
-        [VMEM, HBM, HBM, VMEM],
-        [HBM, VMEM, VMEM],
-        [pltpu.HBM((half, width), BF16), shape((rank, rank), F32), TOKEN],
-        (out_grad, weight, received, gram),
-        flops=tokens * cols * width,
-        moved=17 * MIB,
-        scratch=[
-            pltpu.VMEM((width, cols), BF16),
-            pltpu.VMEM((half, width), BF16),
-            pltpu.VMEM((4, half, BLOCK), BF16),
-            dma((n_blocks, 2)),
-            dma((4,)),
-        ],
-    )
-    second_copies = call(
-        right_sum_kernel,
-        [VMEM, VMEM],
-        VMEM,
-        shape((GROUP, rank, cols), F32),
-        (first, input_done),
-        flops=GROUP * rank * cols,
-        moved=MIB,
-    )
-    second = lax.all_to_all(second_copies, "dp", 0, 0, tiled=True, axis_index_groups=far)
+        scratch=[pltpu.VMEM((tokens + rank, width), BF16), pltpu.VMEM((width, cols), BF16), dma((2 * n_blocks, 3)), dma((1,))],
+    )
+    rows = exchange(right, 1)
+    metric = call(
+        gram_schmidt_kernel, [VMEM], VMEM, shape((rank, rank), F32), (gram,), flops=MIB * 1024, moved=8192
+    )
+    right, right_done = right_sum(rows, metric)
+    rows = exchange(right, side)
+    input_grad, input_done = input_own(0, right_done)
+    right, right_done = right_sum(rows, input_done)
+    rows = exchange(right, side * side)
+    input_grad, input_done = input_own(1, right_done, input_grad)
     new_error, new_momentum = call(
         functools.partial(final_kernel, scale, 1.0 / replicas),
-        [VMEM, VMEM, VMEM, VMEM, VMEM, HBM, HBM, HBM],
+        [VMEM] * (side + 5) + [HBM] * 3,
         [HBM, VMEM],
         [pltpu.HBM((width, cols), BF16), shape(momentum.shape, BF16)],
-        (second, metric, out_grad, left_rows, momentum, acts, acts_oth, error),
+        (*rows, metric, out_grad, left_rows, momentum, input_done, acts, acts_oth, error),
         flops=2 * (tokens + 3 * rank) * width * cols,
         moved=25 * MIB,
         scratch=[

time: 104 us -> 99 us (0.952)
  blocking collectives: 32.5 us -> 17.1 us
  Pallas kernels: 44.8 us -> 50.5 us
  starting transfers between devices: 15.2 us -> 19.3 us
    all_to_all x1 -> x0, blocking collectives: 13.9 us -> none  [per_device(): lax.all_to_all(second_copies, 'dp', 0, 0, tiled=True, axis_index_groups=far)]
    ppermute x0 -> x9, starting transfers between devices: none -> 7.66 us  [exchange(): lax.ppermute(value, 'dp', to(step))]
    pallas_call x9 -> x12, Pallas kernels: 44.8 us -> 50.5 us  [call(): pl.pallas_call(kernel, in_specs=in_specs, out_specs=out_specs, out_shape=...]
    all_to_all x1 -> x0, starting transfers between devices: 3.51 us -> none  [per_device(): lax.all_to_all(right_copies, 'dp', 0, 0, tiled=True, axis_index_groups=near)]
    ppermute x0 -> x9, waiting for transfers between devices: none -> 2.52 us  [exchange(): lax.ppermute(value, 'dp', to(step))]
    all_to_all x1 -> x0, waiting for transfers between devices: 1.89 us -> none  [per_device(): lax.all_to_all(right_copies, 'dp', 0, 0, tiled=True, axis_index_groups=near)]
    all_to_all x1, blocking collectives: 18.5 us -> 17.1 us  [per_device(): left = lax.all_to_all(left_copies, 'dp', 0, 0, tiled=True)]
  transfers between devices with their start and end apart: 4 -> 12, of which waited for: 2 -> 4; matrix products, arithmetic and copies ran while one was open for 0% -> 0% of each run, Pallas kernels for 29% -> 37%
where the time goes in v5:
time: 99 us; the launch traced here: 98.3 us
  Pallas kernels  50.5 us (51%)
  starting transfers between devices  19.3 us (19%)
  blocking collectives  17.1 us (17%)
  waiting for transfers between devices  10.4 us (11%)
    pallas_call x12, Pallas kernels, call(): pl.pallas_call(kernel, in_specs=in_specs, out_specs=out_specs, out_shape=...  50.5 us
    all_to_all x1, blocking collectives, per_device(): left = lax.all_to_all(left_copies, 'dp', 0, 0, tiled=True)  17.1 us
    all_to_all x1, starting transfers between devices, per_device(): gathered = lax.all_to_all(left_parts, 'dp', 0, 0, tiled=True)  11.5 us
    all_to_all x1, waiting for transfers between devices, per_device(): gathered = lax.all_to_all(left_parts, 'dp', 0, 0, tiled=True)  7.92 us
    ppermute x9, starting transfers between devices, exchange(): lax.ppermute(value, 'dp', to(step))  7.66 us
    ppermute x9, waiting for transfers between devices, exchange(): lax.ppermute(value, 'dp', to(step))  2.52 us
  transfers between devices with their start and end apart: 12, of which 4 were waited for; matrix products, arithmetic and copies ran while one was open for 0% of the time, Pallas kernels for 37%

profile of v5, /device:TPU:0, one launch (start us, length us, event | category | flops | bytes accessed | tf_op | source)
XLA Modules:
  0.0 98.3 jit_solution(6051708836336203830)
XLA Ops:
  0.6 0.1 collective-permute-start
  0.7 7.9 %shard_map.85 = (f32[32,8192]{1,0:T(8,128)S(1)}, bf16[96,256]{1,0:T(8,128)(2,1)S(1)}) custom-call(f32[32,512]{1,0:T(8,128)} %bitcast.1, bf16[512,512]{1,0:T(8,128)(2,1)} %og.9, bf16[256,8192]{1,0:T(8,128)(2,1)} %acts.5, bf16[8192,512]{1,0:T(8,128)(2,1)} %error.5), custom_call_target="tpu_custom_call" | custom-call | flops 1207959552 | bytes 13631488 | tf_op jit(solution)/shard_map/pallas_call | solution.py:52
  8.7 0.0 copy-start
  8.7 0.0 collective-permute-done.acts
  8.7 2.2 %shard_map.86 = (bf16[64,32,128]{2,1,0:T(8,128)(2,1)}, bf16[256,8192]{1,0:T(8,128)(2,1)}, f32[8,128]{1,0:T(8,128)S(1)}) custom-call(bf16[96,256]{1,0:T(8,128)(2,1)S(1)} %get-tuple-element.23.pq3, bf16[256,8192]{1,0:T(8,128)(2,1)S(1)} %collective-permute-done.acts, f32[32,8192]{1,0:T(8,128)S(1)} %get-tuple-element.24.part), custom_call_target="tpu_custom_call" | custom-call | flops 402653184 | bytes 6291456 | tf_op jit(solution)/shard_map/pallas_call | solution.py:52
  10.9 11.5 %all-to-all-start = ((bf16[64,32,128]{2,1,0:T(8,128)(2,1)}), bf16[64,32,128]{2,1,0:T(8,128)(2,1)S(1)}, u32[]{:S(2)}, u32[]{:S(2)}) async-start(bf16[64,32,128]{2,1,0:T(8,128)(2,1)} %get-tuple-element.25), calls=%async_computation | async-start | bytes 1048576 | tf_op jit(solution)/shard_map/all_to_all | solution.py:376
  22.5 6.1 %shard_map.87 = (bf16[256,8192]{1,0:T(8,128)(2,1)}, f32[8,128]{1,0:T(8,128)S(1)}) custom-call(bf16[512,512]{1,0:T(8,128)(2,1)S(1)} %copy-done, bf16[8192,512]{1,0:T(8,128)(2,1)} %weight.5, f32[8,128]{1,0:T(8,128)S(1)} %get-tuple-element.26.after), custom_call_target="tpu_custom_call" | custom-call | flops 2147483648 | bytes 13631488 | tf_op jit(solution)/shard_map/pallas_call | solution.py:52
  28.5 7.9 %all-to-all-done.parts = bf16[64,32,128]{2,1,0:T(8,128)(2,1)S(1)} async-done(((bf16[64,32,128]{2,1,0:T(8,128)(2,1)}), bf16[64,32,128]{2,1,0:T(8,128)(2,1)S(1)}, u32[]{:S(2)}, u32[]{:S(2)}) %all-to-all-start) | async-done | bytes 524320 | tf_op jit(solution)/shard_map/all_to_all | solution.py:376
  36.5 0.1 shard_map.88
  36.6 17.1 %all_to_all.10.left.after = bf16[64,32,128]{2,1,0:T(8,128)(2,1)S(1)} all-to-all(bf16[64,32,128]{2,1,0:T(8,128)(2,1)S(1)} %shard_map.88), channel_id=1, replica_groups=mesh['dp'=64,'tensor'=2] {'dp'}, dimensions={0} | all-to-all | bytes 1048576 | tf_op jit(solution)/shard_map/all_to_all | solution.py:402
  53.7 0.0 collective-permute-start.7
  53.7 7.8 %shard_map.89 = (f32[32,512]{1,0:T(8,128)S(1)}, f32[32,32]{1,0:T(8,128)S(1)}, bf16[32,8192]{1,0:T(8,128)(2,1)}) custom-call(bf16[512,512]{1,0:T(8,128)(2,1)S(1)} %copy-done, bf16[64,32,128]{2,1,0:T(8,128)(2,1)S(1)} %all_to_all.10.left.after, bf16[256,8192]{1,0:T(8,128)(2,1)} %acts.5, bf16[256,8192]{1,0:T(8,128)(2,1)} %get-tuple-element.28.acts_oth, ...), custom_call_target="tpu_custom_call" | custom-call | flops 536870912 | bytes 17825792 | tf_op jit(solution)/shard_map/pallas_call | solution.py:52
  61.5 1.0 collective-permute-start.3
  62.5 1.7 %collective-permute-start.2 = (f32[32,512]{1,0:T(8,128)S(1)}, f32[32,512]{1,0:T(8,128)S(1)}, u32[]{:S(2)}, u32[]{:S(2)}) collective-permute-start(f32[32,512]{1,0:T(8,128)S(1)} %get-tuple-element.29.first), channel_id=1, source_target_pairs={{0,4},{2,6},{4,0},{6,2},{8,12},{10,14},{12,8},{14,10},{16,20},{18,... | collective-permute-start | bytes 196616 | tf_op jit(solution)/shard_map/ppermute | solution.py:313
  64.2 6.0 %shard_map.90.after.metric = f32[32,32]{1,0:T(8,128)S(1)} custom-call(f32[32,32]{1,0:T(8,128)S(1)} %get-tuple-element.30.gram), custom_call_target="tpu_custom_call" | custom-call | flops 1073741824 | bytes 8192 | tf_op jit(solution)/shard_map/pallas_call | solution.py:52
  70.2 0.0 collective-permute-done.3.fourth
  70.2 0.0 collective-permute-done.2.third
  70.3 0.7 collective-permute-start.6
  71.0 2.1 %collective-permute-start.5 = (f32[32,512]{1,0:T(8,128)S(1)}, f32[32,512]{1,0:T(8,128)S(1)}, u32[]{:S(2)}, u32[]{:S(2)}) collective-permute-start(f32[32,512]{1,0:T(8,128)S(1)} %get-tuple-element.31.first), channel_id=1, source_target_pairs={{0,16},{2,18},{4,20},{6,22},{8,24},{10,26},{12,28},{14,30},{16,0},... | collective-permute-start | bytes 196616 | tf_op jit(solution)/shard_map/ppermute | solution.py:313
  73.0 0.0 collective-permute-done.7.received
  73.0 4.0 %shard_map.93 = (bf16[256,8192]{1,0:T(8,128)(2,1)}, f32[8,128]{1,0:T(8,128)S(1)}) custom-call(bf16[512,512]{1,0:T(8,128)(2,1)S(1)} %copy-done, bf16[8192,512]{1,0:T(8,128)(2,1)} %weight.5, bf16[256,8192]{1,0:T(8,128)(2,1)S(1)} %collective-permute-done.7.received, f32[8,128]{1,0:T(8,128)S(1)} %get-tuple-element.33.after), custom_call_target="tpu_custom_call" | custom-call | flops 1073741824 | bytes 8388608 | tf_op jit(solution)/shard_map/pallas_call | solution.py:52
  77.1 0.0 collective-permute-done.6.fourth
  77.1 0.0 collective-permute-done.5.third
  77.1 1.4 %collective-permute-done.4.second = f32[32,512]{1,0:T(8,128)S(1)} collective-permute-done((f32[32,512]{1,0:T(8,128)S(1)}, f32[32,512]{1,0:T(8,128)S(1)}, u32[]{:S(2)}, u32[]{:S(2)}) %collective-permute-start.4) | collective-permute-done | bytes 65568 | tf_op jit(solution)/shard_map/ppermute | solution.py:313
  78.5 0.8 collective-permute-start.10
  79.3 1.1 %collective-permute-start.9 = (f32[32,512]{1,0:T(8,128)S(1)}, f32[32,512]{1,0:T(8,128)S(1)}, u32[]{:S(2)}, u32[]{:S(2)}) collective-permute-start(f32[32,512]{1,0:T(8,128)S(1)} %get-tuple-element.35.first), channel_id=1, source_target_pairs={{0,64},{2,66},{4,68},{6,70},{8,72},{10,74},{12,76},{14,78},{16,80}... | collective-permute-start | bytes 196616 | tf_op jit(solution)/shard_map/ppermute | solution.py:313
  80.5 0.3 collective-permute-start.8
  80.7 4.1 %shard_map.95 = (bf16[256,8192]{1,0:T(8,128)(2,1)}, f32[8,128]{1,0:T(8,128)S(1)}) custom-call(bf16[512,512]{1,0:T(8,128)(2,1)S(1)} %copy-done, bf16[8192,512]{1,0:T(8,128)(2,1)} %weight.5, bf16[256,8192]{1,0:T(8,128)(2,1)S(1)} %collective-permute-done.7.received, f32[8,128]{1,0:T(8,128)S(1)} %get-tuple-element.37.after, ...), custom_call_target="tpu_custom_call", output_to_operand_aliasing={{0}: (4, {})} | custom-call | flops 1073741824 | bytes 8388608 | tf_op jit(solution)/shard_map/pallas_call | solution.py:52
  84.8 0.0 collective-permute-done.10.fourth
  84.9 0.3 collective-permute-done.9.third
  85.1 0.8 collective-permute-done.8.second
  85.9 12.2 %shard_map.96 = (bf16[8192,512]{1,0:T(8,128)(2,1)}, bf16[128,512]{1,0:T(8,128)(2,1)}) custom-call(f32[32,512]{1,0:T(8,128)S(1)} %get-tuple-element.35.first, f32[32,512]{1,0:T(8,128)S(1)} %collective-permute-done.8.second, f32[32,512]{1,0:T(8,128)S(1)} %collective-permute-done.9.third, f32[32,512]{1,0:T(8,128)S(1)} %collective-permute-done.10.fourth, ...), custom_call_target="tpu_custom_call" | custom-call | flops 5100273664 | bytes 26214400 | tf_op jit(solution)/shard_map/pallas_call | solution.py:52
  (11 shorter events, 0.1 us)
Async XLA Ops:
  0.6 8.1 %collective-permute-start = (bf16[256,8192]{1,0:T(8,128)(2,1)}, bf16[256,8192]{1,0:T(8,128)(2,1)S(1)}, u32[]{:S(2)}, u32[]{:S(2)}) collective-permute-start(bf16[256,8192]{1,0:T(8,128)(2,1)} %acts.5), channel_id=1, source_target_pairs={{0,1},{1,0},{2,3},{3,2},{4,5},{5,4},{6,7},{7,6},{8,9},{9,8},{10,11... | collective-permute-start | bytes 12582920 | tf_op jit(solution)/shard_map/ppermute | solution.py:347
  8.7 13.8 %copy-start = (bf16[512,512]{1,0:T(8,128)(2,1)S(1)}, bf16[512,512]{1,0:T(8,128)(2,1)}, u32[]{:S(2)}) copy-start(bf16[512,512]{1,0:T(8,128)(2,1)} %og.9) | copy-start | bytes 1572868
  10.9 25.5 %all-to-all-start = ((bf16[64,32,128]{2,1,0:T(8,128)(2,1)}), bf16[64,32,128]{2,1,0:T(8,128)(2,1)S(1)}, u32[]{:S(2)}, u32[]{:S(2)}) async-start(bf16[64,32,128]{2,1,0:T(8,128)(2,1)} %get-tuple-element.25), calls=%async_computation | async-start | bytes 1048576 | tf_op jit(solution)/shard_map/all_to_all | solution.py:376
  53.7 19.3 %collective-permute-start.7 = (bf16[256,8192]{1,0:T(8,128)(2,1)}, bf16[256,8192]{1,0:T(8,128)(2,1)S(1)}, u32[]{:S(2)}, u32[]{:S(2)}) collective-permute-start(bf16[256,8192]{1,0:T(8,128)(2,1)} %shard_map.92), channel_id=1, source_target_pairs={{0,1},{1,0},{2,3},{3,2},{4,5},{5,4},{6,7},{7,6},{8,9},{9,8},{10,11... | collective-permute-start | bytes 12582920 | tf_op jit(solution)/shard_map/ppermute | solution.py:413
  61.5 8.7 %collective-permute-start.3 = (f32[32,512]{1,0:T(8,128)S(1)}, f32[32,512]{1,0:T(8,128)S(1)}, u32[]{:S(2)}, u32[]{:S(2)}) collective-permute-start(f32[32,512]{1,0:T(8,128)S(1)} %get-tuple-element.29.first), channel_id=1, source_target_pairs={{0,6},{2,0},{4,2},{6,4},{8,14},{10,8},{12,10},{14,12},{16,22},{18,... | collective-permute-start | bytes 196616 | tf_op jit(solution)/shard_map/ppermute | solution.py:313
  62.5 7.8 %collective-permute-start.2 = (f32[32,512]{1,0:T(8,128)S(1)}, f32[32,512]{1,0:T(8,128)S(1)}, u32[]{:S(2)}, u32[]{:S(2)}) collective-permute-start(f32[32,512]{1,0:T(8,128)S(1)} %get-tuple-element.29.first), channel_id=1, source_target_pairs={{0,4},{2,6},{4,0},{6,2},{8,12},{10,14},{12,8},{14,10},{16,20},{18,... | collective-permute-start | bytes 196616 | tf_op jit(solution)/shard_map/ppermute | solution.py:313
  64.2 6.0 %collective-permute-start.1 = (f32[32,512]{1,0:T(8,128)S(1)}, f32[32,512]{1,0:T(8,128)S(1)}, u32[]{:S(2)}, u32[]{:S(2)}) collective-permute-start(f32[32,512]{1,0:T(8,128)S(1)} %get-tuple-element.29.first), channel_id=1, source_target_pairs={{0,2},{2,4},{4,6},{6,0},{8,10},{10,12},{12,14},{14,8},{16,18},{18,... | collective-permute-start | bytes 196616 | tf_op jit(solution)/shard_map/ppermute | solution.py:313
  70.3 6.8 %collective-permute-start.6 = (f32[32,512]{1,0:T(8,128)S(1)}, f32[32,512]{1,0:T(8,128)S(1)}, u32[]{:S(2)}, u32[]{:S(2)}) collective-permute-start(f32[32,512]{1,0:T(8,128)S(1)} %get-tuple-element.31.first), channel_id=1, source_target_pairs={{0,24},{2,26},{4,28},{6,30},{8,0},{10,2},{12,4},{14,6},{16,8},{18,... | collective-permute-start | bytes 196616 | tf_op jit(solution)/shard_map/ppermute | solution.py:313
  71.0 6.1 %collective-permute-start.5 = (f32[32,512]{1,0:T(8,128)S(1)}, f32[32,512]{1,0:T(8,128)S(1)}, u32[]{:S(2)}, u32[]{:S(2)}) collective-permute-start(f32[32,512]{1,0:T(8,128)S(1)} %get-tuple-element.31.first), channel_id=1, source_target_pairs={{0,16},{2,18},{4,20},{6,22},{8,24},{10,26},{12,28},{14,30},{16,0},... | collective-permute-start | bytes 196616 | tf_op jit(solution)/shard_map/ppermute | solution.py:313
  73.0 5.5 %collective-permute-start.4 = (f32[32,512]{1,0:T(8,128)S(1)}, f32[32,512]{1,0:T(8,128)S(1)}, u32[]{:S(2)}, u32[]{:S(2)}) collective-permute-start(f32[32,512]{1,0:T(8,128)S(1)} %get-tuple-element.31.first), channel_id=1, source_target_pairs={{0,8},{2,10},{4,12},{6,14},{8,16},{10,18},{12,20},{14,22},{16,24},... | collective-permute-start | bytes 196616 | tf_op jit(solution)/shard_map/ppermute | solution.py:313
  78.5 6.3 %collective-permute-start.10 = (f32[32,512]{1,0:T(8,128)S(1)}, f32[32,512]{1,0:T(8,128)S(1)}, u32[]{:S(2)}, u32[]{:S(2)}) collective-permute-start(f32[32,512]{1,0:T(8,128)S(1)} %get-tuple-element.35.first), channel_id=1, source_target_pairs={{0,96},{2,98},{4,100},{6,102},{8,104},{10,106},{12,108},{14,110},{... | collective-permute-start | bytes 196616 | tf_op jit(solution)/shard_map/ppermute | solution.py:313
  79.3 5.8 %collective-permute-start.9 = (f32[32,512]{1,0:T(8,128)S(1)}, f32[32,512]{1,0:T(8,128)S(1)}, u32[]{:S(2)}, u32[]{:S(2)}) collective-permute-start(f32[32,512]{1,0:T(8,128)S(1)} %get-tuple-element.35.first), channel_id=1, source_target_pairs={{0,64},{2,66},{4,68},{6,70},{8,72},{10,74},{12,76},{14,78},{16,80}... | collective-permute-start | bytes 196616 | tf_op jit(solution)/shard_map/ppermute | solution.py:313
  80.5 5.5 %collective-permute-start.8 = (f32[32,512]{1,0:T(8,128)S(1)}, f32[32,512]{1,0:T(8,128)S(1)}, u32[]{:S(2)}, u32[]{:S(2)}) collective-permute-start(f32[32,512]{1,0:T(8,128)S(1)} %get-tuple-element.35.first), channel_id=1, source_target_pairs={{0,32},{2,34},{4,36},{6,38},{8,40},{10,42},{12,44},{14,46},{16,48}... | collective-permute-start | bytes 196616 | tf_op jit(solution)/shard_map/ppermute | solution.py:313
  80.7 5.2 %copy-start.1 = (bf16[32,8192]{1,0:T(8,128)(2,1)S(1)}, bf16[32,8192]{1,0:T(8,128)(2,1)}, u32[]{:S(2)}) copy-start(bf16[32,8192]{1,0:T(8,128)(2,1)} %get-tuple-element.36.left_rows) | copy-start | bytes 1572868
  80.7 5.2 %copy-start.2 = (bf16[128,512]{1,0:T(8,128)(2,1)S(1)}, bf16[128,512]{1,0:T(8,128)(2,1)}, u32[]{:S(2)}) copy-start(bf16[128,512]{1,0:T(8,128)(2,1)} %momentum.1) | copy-start | bytes 393220

commit v6 on v5

--- a/solution.py
+++ b/solution.py
@@ -40,6 +40,16 @@
     middle = rest.astype(BF16)
     low = (rest - middle.astype(F32)).astype(BF16)
     return jnp.concatenate([high, middle, low], axis=axis)
+
+
+def split2(x):
+    high = x.astype(BF16)
+    return jnp.concatenate([high, (x - high.astype(F32)).astype(BF16)], axis=0)
+
+
+def sum2(x):
+    rows = x.shape[0] // 2
+    return x[:rows] + x[rows:]
 
 
 def sum3(x):
@@ -56,7 +66,7 @@
         out_shape=out_shape,
         scratch_shapes=list(scratch),
         input_output_aliases=aliases,
-        compiler_params=pltpu.CompilerParams(vmem_limit_bytes=48 * MIB),
+        compiler_params=pltpu.CompilerParams(vmem_limit_bytes=32 * MIB),
         cost_estimate=pl.CostEstimate(flops=flops, bytes_accessed=moved, transcendentals=0),
     )(*args)
 
@@ -115,7 +125,7 @@
     scale, q_hbm, og_hbm, acts, error, part, pq_oth, q, og, acts_here, error_here, sems, small_sems
 ):
     half, width = acts.shape
-    rows = blocks(width)
+    rows = blocks(BLOCK, BLOCK // 2) + blocks(width)[1:]
     q_copy = pltpu.make_async_copy(q_hbm, q, small_sems.at[0])
     og_copy = pltpu.make_async_copy(og_hbm, og, small_sems.at[1])
     q_copy.start()
@@ -123,25 +133,25 @@
     reader = Reader(reads, sems, ahead=2)
     og_copy.start()
     q_copy.wait()
-    q3 = split3(q[...])
+    q2 = split2(q[...])
     for i, at in enumerate(rows):
         reader.wait(i)
-        by_error = sum3(dot(error_here[at, :], q3, NT).T)
+        by_error = sum2(dot(error_here[at, :], q2, NT).T)
         if i == 0:
             og_copy.wait()
             og_own, og_oth = halves(og, half)
-            pq3 = split3(sum3(dot(q3, og_own, NT)) * scale)
-            pq_oth[...] = split3(sum3(dot(q3, og_oth, NT)) * scale)
-        part[:, at] = by_error + sum3(dot(pq3, acts_here[:, at]))
-
-
-def left_kernel(pq3, acts, part, left, acts_kept, token, here, sems):
+            pq2 = split2(sum2(dot(q2, og_own, NT)) * scale)
+            pq_oth[...] = split2(sum2(dot(q2, og_oth, NT)) * scale)
+        part[:, at] = by_error + sum2(dot(pq2, acts_here[:, at]))
+
+
+def left_kernel(pq2, acts, part, left, acts_kept, token, here, sems):
     token[...] = jnp.zeros_like(token)
     rows = blocks(acts.shape[1])
     copies = [pltpu.make_async_copy(acts, acts_kept, sems.at[len(rows)])]
     copies[0].start()
     for i, at in enumerate(rows):
-        total = part[:, at] + sum3(dot(pq3[...], acts[:, at]))
+        total = part[:, at] + sum2(dot(pq2[...], acts[:, at]))
         count = BLOCK // CHUNK
         chunks = slice(i * count, (i + 1) * count)
         for j in range(count):
@@ -170,12 +180,24 @@
 
 
 def input_own_kernel(part, og, weight, received, after, *refs):
-    out, token, weight_here, slots, sems, out_sems = refs[part:]
+    ahead = []
+    if part == 0:
+        out, token, weight_here, slots, sems, out_sems = refs
+    else:
+        _, acts, acts_oth, error, out, token, stack, first_error, weight_here, slots, sems, out_sems, ahead_sems = refs
+        pairs = [
+            (acts.at[:, :BLOCK], stack.at[: acts.shape[0], :]),
+            (acts_oth.at[:, :BLOCK], stack.at[acts.shape[0] :, :]),
+            (error.at[:BLOCK, :], first_error),
+        ]
+        ahead = [pltpu.make_async_copy(source, target, ahead_sems.at[i]) for i, (source, target) in enumerate(pairs)]
     token[...] = jnp.zeros_like(token)
     half, width = received.shape
     rows = blocks(width)
     rows = rows[: len(rows) // 2] if part == 0 else rows[len(rows) // 2 :]
     reader = Reader([[(weight.at[at, :], weight_here.at[at, :])] for at in rows], sems)
+    for copy in ahead:
+        copy.start()
     own, _ = halves(og, half)
     writer = Writer(slots, out_sems)
     for i, at in enumerate(rows):
@@ -183,6 +205,8 @@
         product = dot(own, weight_here[at, :], NT).astype(BF16)
         writer.put((product.astype(F32) + received[:, at].astype(F32)).astype(BF16), out.at[:, at])
     writer.finish()
+    for copy in ahead:
+        copy.wait()
 
 
 def gram_schmidt_kernel(gram, metric):
@@ -258,7 +282,7 @@
 
 
 def final_kernel(
-    scale, inverse_replicas, first, second, third, fourth, metric, og, left_rows, momentum, after, acts, acts_oth, error,
+    scale, inverse_replicas, first, second, third, fourth, metric, og, left_rows, momentum, first_stack, first_error, acts, acts_oth, error,
     new_error, new_momentum, stack, rest, error_here, slots, sems, out_sems,
 ):
     tokens, cols = og.shape
@@ -272,7 +296,7 @@
                 (acts_oth.at[:, at], stack.at[half:tokens, at]),
                 (error.at[at, :], error_here.at[at, :]),
             ]
-            for at in rows
+            for at in rows[1:]
         ],
         sems,
     )
@@ -285,9 +309,14 @@
     rest[tokens:] = split3(exact_dot(metric[...], total))
     writer = Writer(slots, out_sems)
     for i, at in enumerate(rows):
-        reader.wait(i)
-        product = dot(stack[:, at], rest[...], TN)
-        writer.put((product * scale + error_here[at, :].astype(F32)).astype(BF16), new_error.at[at, :])
+        if i == 0:
+            product = dot(first_stack[...], rest[:tokens], TN) + dot(stack[tokens:, at], rest[tokens:], TN)
+            base = first_error[...]
+        else:
+            reader.wait(i - 1)
+            product = dot(stack[:, at], rest[...], TN)
+            base = error_here[at, :]
+        writer.put((product * scale + base.astype(F32)).astype(BF16), new_error.at[at, :])
     count = momentum.shape[0]
     mine = pl.ds(pl.multiple_of(lax.axis_index("dp") * count, count), count)
     approx = dot(stack[tokens:, mine], rest[tokens:], TN) * -scale
@@ -323,13 +352,14 @@
             moved=MIB // 4,
         )
 
-    def input_own(part, after, *first_part):
+    def input_own(part, after, *more):
         return call(
             functools.partial(input_own_kernel, part),
-            [VMEM, HBM, VMEM, VMEM] + [HBM] * part,
-            [HBM, VMEM],
-            [pltpu.HBM((half, width), BF16), TOKEN],
-            (out_grad, weight, received, after, *first_part),
+            [VMEM, HBM, VMEM, VMEM] + [HBM] * len(more),
+            [HBM, VMEM] + [VMEM] * (2 * part),
+            [pltpu.HBM((half, width), BF16), TOKEN]
+            + [shape((tokens, BLOCK), BF16), shape((BLOCK, cols), BF16)] * part,
+            (out_grad, weight, received, after, *more),
             flops=tokens * cols * width // 2,
             moved=8 * MIB,
             scratch=[
@@ -337,7 +367,8 @@
                 pltpu.VMEM((4, half, BLOCK), BF16),
                 dma((n_blocks, 1)),
                 dma((4,)),
-            ],
+            ]
+            + [dma((3,))] * part,
             aliases={4: 0} if part else {},
         )
 
@@ -350,7 +381,7 @@
         functools.partial(left_own_kernel, scale),
         [HBM, HBM, HBM, HBM],
         [VMEM] * 2,
-        [shape((rank, width), F32), shape((3 * rank, half), BF16)],
+        [shape((rank, width), F32), shape((2 * rank, half), BF16)],
         (q_init.T, out_grad, acts, error),
         flops=2 * 96 * width * 768,
         moved=13 * MIB,
@@ -359,7 +390,7 @@
             pltpu.VMEM((tokens, cols), BF16),
             pltpu.VMEM((half, width), BF16),
             pltpu.VMEM((width, cols), BF16),
-            dma((n_blocks, 2)),
+            dma((n_blocks + 1, 2)),
             dma((2,)),
         ],
     )
@@ -431,13 +462,13 @@
     input_grad, input_done = input_own(0, right_done)
     right, right_done = right_sum(rows, input_done)
     rows = exchange(right, side * side)
-    input_grad, input_done = input_own(1, right_done, input_grad)
+    input_grad, _, first_stack, first_error = input_own(1, right_done, input_grad, acts, acts_oth, error)
     new_error, new_momentum = call(
         functools.partial(final_kernel, scale, 1.0 / replicas),
-        [VMEM] * (side + 5) + [HBM] * 3,
+        [VMEM] * (side + 6) + [HBM] * 3,
         [HBM, VMEM],
         [pltpu.HBM((width, cols), BF16), shape(momentum.shape, BF16)],
-        (*rows, metric, out_grad, left_rows, momentum, input_done, acts, acts_oth, error),
+        (*rows, metric, out_grad, left_rows, momentum, first_stack, first_error, acts, acts_oth, error),
         flops=2 * (tokens + 3 * rank) * width * cols,
         moved=25 * MIB,
         scratch=[

time: 99 us -> 98 us (0.990)
  transfers between devices with their start and end apart: 12 -> 12, of which waited for: 4 -> 3; matrix products, arithmetic and copies ran while one was open for 0% -> 0% of each run, Pallas kernels for 37% -> 38%
where the time goes in v6:
time: 98 us; the launch traced here: 97.1 us
  Pallas kernels  50.3 us (51%)
  starting transfers between devices  19.3 us (20%)
  blocking collectives  17.1 us (17%)
  waiting for transfers between devices  9.48 us (10%)
    pallas_call x12, Pallas kernels, call(): pl.pallas_call(kernel, in_specs=in_specs, out_specs=out_specs, out_shape=...  50.3 us
    all_to_all x1, blocking collectives, per_device(): left = lax.all_to_all(left_copies, 'dp', 0, 0, tiled=True)  17.1 us
    all_to_all x1, starting transfers between devices, per_device(): gathered = lax.all_to_all(left_parts, 'dp', 0, 0, tiled=True)  11.5 us
    all_to_all x1, waiting for transfers between devices, per_device(): gathered = lax.all_to_all(left_parts, 'dp', 0, 0, tiled=True)  7.92 us
    ppermute x9, starting transfers between devices, exchange(): lax.ppermute(value, 'dp', to(step))  7.66 us
  transfers between devices with their start and end apart: 12, of which 3 were waited for; matrix products, arithmetic and copies ran while one was open for 0% of the time, Pallas kernels for 38%

profile of v6, /device:TPU:0, one launch (start us, length us, event | category | flops | bytes accessed | tf_op | source)
XLA Modules:
  0.0 97.1 jit_solution(16585763289045361733)
XLA Ops:
  0.6 0.1 collective-permute-start
  0.7 7.8 %shard_map.85 = (f32[32,8192]{1,0:T(8,128)S(1)}, bf16[64,256]{1,0:T(8,128)(2,1)S(1)}) custom-call(f32[32,512]{1,0:T(8,128)} %bitcast.1, bf16[512,512]{1,0:T(8,128)(2,1)} %og.9, bf16[256,8192]{1,0:T(8,128)(2,1)} %acts.5, bf16[8192,512]{1,0:T(8,128)(2,1)} %error.5), custom_call_target="tpu_custom_call" | custom-call | flops 1207959552 | bytes 13631488 | tf_op jit(solution)/shard_map/pallas_call | solution.py:62
  8.6 0.0 copy-start
  8.6 0.0 collective-permute-done.acts
  8.6 2.2 %shard_map.86 = (bf16[64,32,128]{2,1,0:T(8,128)(2,1)}, bf16[256,8192]{1,0:T(8,128)(2,1)}, f32[8,128]{1,0:T(8,128)S(1)}) custom-call(bf16[64,256]{1,0:T(8,128)(2,1)S(1)} %get-tuple-element.24.pq2, bf16[256,8192]{1,0:T(8,128)(2,1)S(1)} %collective-permute-done.acts, f32[32,8192]{1,0:T(8,128)S(1)} %get-tuple-element.25.part), custom_call_target="tpu_custom_call" | custom-call | flops 402653184 | bytes 6291456 | tf_op jit(solution)/shard_map/pallas_call | solution.py:62
  10.8 11.5 %all-to-all-start = ((bf16[64,32,128]{2,1,0:T(8,128)(2,1)}), bf16[64,32,128]{2,1,0:T(8,128)(2,1)S(1)}, u32[]{:S(2)}, u32[]{:S(2)}) async-start(bf16[64,32,128]{2,1,0:T(8,128)(2,1)} %get-tuple-element.26), calls=%async_computation | async-start | bytes 1048576 | tf_op jit(solution)/shard_map/all_to_all | solution.py:407
  22.4 6.1 %shard_map.87 = (bf16[256,8192]{1,0:T(8,128)(2,1)}, f32[8,128]{1,0:T(8,128)S(1)}) custom-call(bf16[512,512]{1,0:T(8,128)(2,1)S(1)} %copy-done, bf16[8192,512]{1,0:T(8,128)(2,1)} %weight.5, f32[8,128]{1,0:T(8,128)S(1)} %get-tuple-element.27.after), custom_call_target="tpu_custom_call" | custom-call | flops 2147483648 | bytes 13631488 | tf_op jit(solution)/shard_map/pallas_call | solution.py:62
  28.4 7.9 %all-to-all-done.parts = bf16[64,32,128]{2,1,0:T(8,128)(2,1)S(1)} async-done(((bf16[64,32,128]{2,1,0:T(8,128)(2,1)}), bf16[64,32,128]{2,1,0:T(8,128)(2,1)S(1)}, u32[]{:S(2)}, u32[]{:S(2)}) %all-to-all-start) | async-done | bytes 524320 | tf_op jit(solution)/shard_map/all_to_all | solution.py:407
  36.4 0.1 shard_map.88
  36.5 17.1 %all_to_all.10.left.after = bf16[64,32,128]{2,1,0:T(8,128)(2,1)S(1)} all-to-all(bf16[64,32,128]{2,1,0:T(8,128)(2,1)S(1)} %shard_map.88), channel_id=1, replica_groups=mesh['dp'=64,'tensor'=2] {'dp'}, dimensions={0} | all-to-all | bytes 1048576 | tf_op jit(solution)/shard_map/all_to_all | solution.py:433
  53.6 0.0 collective-permute-start.7
  53.6 7.8 %shard_map.89 = (f32[32,512]{1,0:T(8,128)S(1)}, f32[32,32]{1,0:T(8,128)S(1)}, bf16[32,8192]{1,0:T(8,128)(2,1)}) custom-call(bf16[512,512]{1,0:T(8,128)(2,1)S(1)} %copy-done, bf16[64,32,128]{2,1,0:T(8,128)(2,1)S(1)} %all_to_all.10.left.after, bf16[256,8192]{1,0:T(8,128)(2,1)} %acts.5, bf16[256,8192]{1,0:T(8,128)(2,1)} %get-tuple-element.29.acts_oth.refs_2_, ...), custom_call_target="tpu_custom_call" | custom-call | flops 536870912 | bytes 17825792 | tf_op jit(solution)/shard_map/pallas_call | solution.py:62
  61.4 1.0 collective-permute-start.3
  62.4 1.7 %collective-permute-start.2 = (f32[32,512]{1,0:T(8,128)S(1)}, f32[32,512]{1,0:T(8,128)S(1)}, u32[]{:S(2)}, u32[]{:S(2)}) collective-permute-start(f32[32,512]{1,0:T(8,128)S(1)} %get-tuple-element.30.first), channel_id=1, source_target_pairs={{0,4},{2,6},{4,0},{6,2},{8,12},{10,14},{12,8},{14,10},{16,20},{18,... | collective-permute-start | bytes 196616 | tf_op jit(solution)/shard_map/ppermute | solution.py:342
  64.1 0.0 collective-permute-start.1
  64.1 6.0 %shard_map.90.after.metric = f32[32,32]{1,0:T(8,128)S(1)} custom-call(f32[32,32]{1,0:T(8,128)S(1)} %get-tuple-element.31.gram), custom_call_target="tpu_custom_call" | custom-call | flops 1073741824 | bytes 8192 | tf_op jit(solution)/shard_map/pallas_call | solution.py:62
  70.1 0.0 collective-permute-done.3.fourth
  70.1 0.0 collective-permute-done.2.third
  70.2 0.0 collective-permute-done.1.second
  70.2 0.7 collective-permute-start.6
  70.9 2.1 %collective-permute-start.5 = (f32[32,512]{1,0:T(8,128)S(1)}, f32[32,512]{1,0:T(8,128)S(1)}, u32[]{:S(2)}, u32[]{:S(2)}) collective-permute-start(f32[32,512]{1,0:T(8,128)S(1)} %get-tuple-element.32.first), channel_id=1, source_target_pairs={{0,16},{2,18},{4,20},{6,22},{8,24},{10,26},{12,28},{14,30},{16,0},... | collective-permute-start | bytes 196616 | tf_op jit(solution)/shard_map/ppermute | solution.py:342
  72.9 0.0 collective-permute-done.7.received
  72.9 4.0 %shard_map.93 = (bf16[256,8192]{1,0:T(8,128)(2,1)}, f32[8,128]{1,0:T(8,128)S(1)}) custom-call(bf16[512,512]{1,0:T(8,128)(2,1)S(1)} %copy-done, bf16[8192,512]{1,0:T(8,128)(2,1)} %weight.5, bf16[256,8192]{1,0:T(8,128)(2,1)S(1)} %collective-permute-done.7.received, f32[8,128]{1,0:T(8,128)S(1)} %get-tuple-element.34.after), custom_call_target="tpu_custom_call" | custom-call | flops 1073741824 | bytes 8388608 | tf_op jit(solution)/shard_map/pallas_call | solution.py:62
  77.0 0.0 collective-permute-done.6.fourth
  77.0 1.4 %collective-permute-done.4.second = f32[32,512]{1,0:T(8,128)S(1)} collective-permute-done((f32[32,512]{1,0:T(8,128)S(1)}, f32[32,512]{1,0:T(8,128)S(1)}, u32[]{:S(2)}, u32[]{:S(2)}) %collective-permute-start.4) | collective-permute-done | bytes 65568 | tf_op jit(solution)/shard_map/ppermute | solution.py:342
  78.4 0.8 collective-permute-start.10
  79.2 1.1 %collective-permute-start.9 = (f32[32,512]{1,0:T(8,128)S(1)}, f32[32,512]{1,0:T(8,128)S(1)}, u32[]{:S(2)}, u32[]{:S(2)}) collective-permute-start(f32[32,512]{1,0:T(8,128)S(1)} %get-tuple-element.36.first), channel_id=1, source_target_pairs={{0,64},{2,66},{4,68},{6,70},{8,72},{10,74},{12,76},{14,78},{16,80}... | collective-permute-start | bytes 196616 | tf_op jit(solution)/shard_map/ppermute | solution.py:342
  80.4 0.3 collective-permute-start.8
  80.6 5.1 %shard_map.95 = (bf16[256,8192]{1,0:T(8,128)(2,1)}, f32[8,128]{1,0:T(8,128)}, bf16[512,1024]{1,0:T(8,128)(2,1)S(1)}, bf16[1024,512]{1,0:T(8,128)(2,1)S(1)}) custom-call(bf16[512,512]{1,0:T(8,128)(2,1)S(1)} %copy-done, bf16[8192,512]{1,0:T(8,128)(2,1)} %weight.5, ...), custom_call_target="tpu_custom_call", output_to_operand_aliasing={{0}: (4, {})} | custom-call | flops 1073741824 | bytes 8388608 | tf_op jit(solution)/shard_map/pallas_call | solution.py:62
  85.7 0.0 collective-permute-done.10.fourth
  85.7 0.1 collective-permute-done.8.second
  85.8 11.1 %shard_map.96 = (bf16[8192,512]{1,0:T(8,128)(2,1)}, bf16[128,512]{1,0:T(8,128)(2,1)}) custom-call(f32[32,512]{1,0:T(8,128)S(1)} %get-tuple-element.36.first, f32[32,512]{1,0:T(8,128)S(1)} %collective-permute-done.8.second, f32[32,512]{1,0:T(8,128)S(1)} %collective-permute-done.9.third, f32[32,512]{1,0:T(8,128)S(1)} %collective-permute-done.10.fourth, ...), custom_call_target="tpu_custom_call" | custom-call | flops 5100273664 | bytes 26214400 | tf_op jit(solution)/shard_map/pallas_call | solution.py:62
  (11 shorter events, 0.1 us)
Async XLA Ops:
  0.6 8.0 %collective-permute-start = (bf16[256,8192]{1,0:T(8,128)(2,1)}, bf16[256,8192]{1,0:T(8,128)(2,1)S(1)}, u32[]{:S(2)}, u32[]{:S(2)}) collective-permute-start(bf16[256,8192]{1,0:T(8,128)(2,1)} %acts.5), channel_id=1, source_target_pairs={{0,1},{1,0},{2,3},{3,2},{4,5},{5,4},{6,7},{7,6},{8,9},{9,8},{10,11... | collective-permute-start | bytes 12582920 | tf_op jit(solution)/shard_map/ppermute | solution.py:378
  8.6 13.8 %copy-start = (bf16[512,512]{1,0:T(8,128)(2,1)S(1)}, bf16[512,512]{1,0:T(8,128)(2,1)}, u32[]{:S(2)}) copy-start(bf16[512,512]{1,0:T(8,128)(2,1)} %og.9) | copy-start | bytes 1572868
  10.8 25.5 %all-to-all-start = ((bf16[64,32,128]{2,1,0:T(8,128)(2,1)}), bf16[64,32,128]{2,1,0:T(8,128)(2,1)S(1)}, u32[]{:S(2)}, u32[]{:S(2)}) async-start(bf16[64,32,128]{2,1,0:T(8,128)(2,1)} %get-tuple-element.26), calls=%async_computation | async-start | bytes 1048576 | tf_op jit(solution)/shard_map/all_to_all | solution.py:407
  53.6 19.3 %collective-permute-start.7 = (bf16[256,8192]{1,0:T(8,128)(2,1)}, bf16[256,8192]{1,0:T(8,128)(2,1)S(1)}, u32[]{:S(2)}, u32[]{:S(2)}) collective-permute-start(bf16[256,8192]{1,0:T(8,128)(2,1)} %shard_map.92), channel_id=1, source_target_pairs={{0,1},{1,0},{2,3},{3,2},{4,5},{5,4},{6,7},{7,6},{8,9},{9,8},{10,11... | collective-permute-start | bytes 12582920 | tf_op jit(solution)/shard_map/ppermute | solution.py:444
  61.4 8.7 %collective-permute-start.3 = (f32[32,512]{1,0:T(8,128)S(1)}, f32[32,512]{1,0:T(8,128)S(1)}, u32[]{:S(2)}, u32[]{:S(2)}) collective-permute-start(f32[32,512]{1,0:T(8,128)S(1)} %get-tuple-element.30.first), channel_id=1, source_target_pairs={{0,6},{2,0},{4,2},{6,4},{8,14},{10,8},{12,10},{14,12},{16,22},{18,... | collective-permute-start | bytes 196616 | tf_op jit(solution)/shard_map/ppermute | solution.py:342
  62.4 7.8 %collective-permute-start.2 = (f32[32,512]{1,0:T(8,128)S(1)}, f32[32,512]{1,0:T(8,128)S(1)}, u32[]{:S(2)}, u32[]{:S(2)}) collective-permute-start(f32[32,512]{1,0:T(8,128)S(1)} %get-tuple-element.30.first), channel_id=1, source_target_pairs={{0,4},{2,6},{4,0},{6,2},{8,12},{10,14},{12,8},{14,10},{16,20},{18,... | collective-permute-start | bytes 196616 | tf_op jit(solution)/shard_map/ppermute | solution.py:342
  64.1 6.0 %collective-permute-start.1 = (f32[32,512]{1,0:T(8,128)S(1)}, f32[32,512]{1,0:T(8,128)S(1)}, u32[]{:S(2)}, u32[]{:S(2)}) collective-permute-start(f32[32,512]{1,0:T(8,128)S(1)} %get-tuple-element.30.first), channel_id=1, source_target_pairs={{0,2},{2,4},{4,6},{6,0},{8,10},{10,12},{12,14},{14,8},{16,18},{18,... | collective-permute-start | bytes 196616 | tf_op jit(solution)/shard_map/ppermute | solution.py:342
  70.2 6.8 %collective-permute-start.6 = (f32[32,512]{1,0:T(8,128)S(1)}, f32[32,512]{1,0:T(8,128)S(1)}, u32[]{:S(2)}, u32[]{:S(2)}) collective-permute-start(f32[32,512]{1,0:T(8,128)S(1)} %get-tuple-element.32.first), channel_id=1, source_target_pairs={{0,24},{2,26},{4,28},{6,30},{8,0},{10,2},{12,4},{14,6},{16,8},{18,... | collective-permute-start | bytes 196616 | tf_op jit(solution)/shard_map/ppermute | solution.py:342
  70.9 6.1 %collective-permute-start.5 = (f32[32,512]{1,0:T(8,128)S(1)}, f32[32,512]{1,0:T(8,128)S(1)}, u32[]{:S(2)}, u32[]{:S(2)}) collective-permute-start(f32[32,512]{1,0:T(8,128)S(1)} %get-tuple-element.32.first), channel_id=1, source_target_pairs={{0,16},{2,18},{4,20},{6,22},{8,24},{10,26},{12,28},{14,30},{16,0},... | collective-permute-start | bytes 196616 | tf_op jit(solution)/shard_map/ppermute | solution.py:342
  72.9 5.5 %collective-permute-start.4 = (f32[32,512]{1,0:T(8,128)S(1)}, f32[32,512]{1,0:T(8,128)S(1)}, u32[]{:S(2)}, u32[]{:S(2)}) collective-permute-start(f32[32,512]{1,0:T(8,128)S(1)} %get-tuple-element.32.first), channel_id=1, source_target_pairs={{0,8},{2,10},{4,12},{6,14},{8,16},{10,18},{12,20},{14,22},{16,24},... | collective-permute-start | bytes 196616 | tf_op jit(solution)/shard_map/ppermute | solution.py:342
  78.4 7.3 %collective-permute-start.10 = (f32[32,512]{1,0:T(8,128)S(1)}, f32[32,512]{1,0:T(8,128)S(1)}, u32[]{:S(2)}, u32[]{:S(2)}) collective-permute-start(f32[32,512]{1,0:T(8,128)S(1)} %get-tuple-element.36.first), channel_id=1, source_target_pairs={{0,96},{2,98},{4,100},{6,102},{8,104},{10,106},{12,108},{14,110},{... | collective-permute-start | bytes 196616 | tf_op jit(solution)/shard_map/ppermute | solution.py:342
  79.2 6.5 %collective-permute-start.9 = (f32[32,512]{1,0:T(8,128)S(1)}, f32[32,512]{1,0:T(8,128)S(1)}, u32[]{:S(2)}, u32[]{:S(2)}) collective-permute-start(f32[32,512]{1,0:T(8,128)S(1)} %get-tuple-element.36.first), channel_id=1, source_target_pairs={{0,64},{2,66},{4,68},{6,70},{8,72},{10,74},{12,76},{14,78},{16,80}... | collective-permute-start | bytes 196616 | tf_op jit(solution)/shard_map/ppermute | solution.py:342
  80.4 5.5 %collective-permute-start.8 = (f32[32,512]{1,0:T(8,128)S(1)}, f32[32,512]{1,0:T(8,128)S(1)}, u32[]{:S(2)}, u32[]{:S(2)}) collective-permute-start(f32[32,512]{1,0:T(8,128)S(1)} %get-tuple-element.36.first), channel_id=1, source_target_pairs={{0,32},{2,34},{4,36},{6,38},{8,40},{10,42},{12,44},{14,46},{16,48}... | collective-permute-start | bytes 196616 | tf_op jit(solution)/shard_map/ppermute | solution.py:342
  80.6 5.2 %copy-start.1 = (bf16[32,8192]{1,0:T(8,128)(2,1)S(1)}, bf16[32,8192]{1,0:T(8,128)(2,1)}, u32[]{:S(2)}) copy-start(bf16[32,8192]{1,0:T(8,128)(2,1)} %get-tuple-element.37.left_rows) | copy-start | bytes 1572868
  80.6 5.2 %copy-start.2 = (bf16[128,512]{1,0:T(8,128)(2,1)S(1)}, bf16[128,512]{1,0:T(8,128)(2,1)}, u32[]{:S(2)}) copy-start(bf16[128,512]{1,0:T(8,128)(2,1)} %momentum.1) | copy-start | bytes 393220

commit v7 on v6

--- a/solution.py
+++ b/solution.py
@@ -182,7 +182,7 @@
 def input_own_kernel(part, og, weight, received, after, *refs):
     ahead = []
     if part == 0:
-        out, token, weight_here, slots, sems, out_sems = refs
+        gram, coeffs, products, out, token, metric, weight_here, slots, sems, out_sems = refs
     else:
         _, acts, acts_oth, error, out, token, stack, first_error, weight_here, slots, sems, out_sems, ahead_sems = refs
         pairs = [
@@ -199,6 +199,10 @@
     for copy in ahead:
         copy.start()
     own, _ = halves(og, half)
+    if part == 0:
+        rank = gram.shape[0]
+        full, _ = gram_schmidt(gram[...], range(rank * 3 // 4, rank), coeffs[...], products[...])
+        metric[...] = exact_dot(full, full, NT)
     writer = Writer(slots, out_sems)
     for i, at in enumerate(rows):
         reader.wait(i)
@@ -209,10 +213,9 @@
         copy.wait()
 
 
-def gram_schmidt_kernel(gram, metric):
-    for coeffs in gram_schmidt(gram[...]):
-        pass
-    metric[...] = exact_dot(coeffs, coeffs, NT)
+def gram_schmidt_kernel(gram, coeffs, products):
+    zeros = jnp.zeros(gram.shape, F32)
+    coeffs[...], products[...] = gram_schmidt(gram[...], range(gram.shape[0] * 3 // 4), zeros, zeros)
 
 
 def left_sum_kernel(parts, after, out):
@@ -258,13 +261,11 @@
     left_copy.wait()
 
 
-def gram_schmidt(g):
+def gram_schmidt(g, steps, coeffs, products):
     width = g.shape[0]
     rows = lax.broadcasted_iota(jnp.int32, (width, width), 0)
     columns = lax.broadcasted_iota(jnp.int32, (width, width), 1)
-    coeffs = jnp.zeros((width, width), F32)
-    products = jnp.zeros((width, width), F32)
-    for k in range(width):
+    for k in steps:
         along = products[k : k + 1]
         unit = (rows[:, :1] == k).astype(F32)
         v = unit - jnp.sum(along * coeffs, axis=1, keepdims=True)
@@ -273,7 +274,7 @@
         inverse = lax.rsqrt(square + 1e-06)
         coeffs = jnp.where(columns == k, v * inverse, coeffs)
         products = jnp.where(columns == k, inner * inverse, products)
-        yield coeffs
+    return coeffs, products
 
 
 def right_sum_kernel(first, second, third, fourth, after, out, token):
@@ -355,10 +356,10 @@
     def input_own(part, after, *more):
         return call(
             functools.partial(input_own_kernel, part),
-            [VMEM, HBM, VMEM, VMEM] + [HBM] * len(more),
-            [HBM, VMEM] + [VMEM] * (2 * part),
+            [VMEM, HBM, VMEM, VMEM] + [HBM if part else VMEM] * len(more),
+            [HBM, VMEM] + [VMEM] * (1 + part),
             [pltpu.HBM((half, width), BF16), TOKEN]
-            + [shape((tokens, BLOCK), BF16), shape((BLOCK, cols), BF16)] * part,
+            + ([shape((tokens, BLOCK), BF16), shape((BLOCK, cols), BF16)] if part else [shape((rank, rank), F32)]),
             (out_grad, weight, received, after, *more),
             flops=tokens * cols * width // 2,
             moved=8 * MIB,
@@ -454,12 +455,12 @@
         scratch=[pltpu.VMEM((tokens + rank, width), BF16), pltpu.VMEM((width, cols), BF16), dma((2 * n_blocks, 3)), dma((1,))],
     )
     rows = exchange(right, 1)
-    metric = call(
-        gram_schmidt_kernel, [VMEM], VMEM, shape((rank, rank), F32), (gram,), flops=MIB * 1024, moved=8192
-    )
-    right, right_done = right_sum(rows, metric)
+    coeffs, products = call(
+        gram_schmidt_kernel, [VMEM], [VMEM] * 2, [shape((rank, rank), F32)] * 2, (gram,), flops=MIB * 1024, moved=8192
+    )
+    right, right_done = right_sum(rows, coeffs)
     rows = exchange(right, side)
-    input_grad, input_done = input_own(0, right_done)
+    input_grad, input_done, metric = input_own(0, right_done, gram, coeffs, products)
     right, right_done = right_sum(rows, input_done)
     rows = exchange(right, side * side)
     input_grad, _, first_stack, first_error = input_own(1, right_done, input_grad, acts, acts_oth, error)

time: 98 us -> 97.2 us (level)
  Pallas kernels: 50.3 us -> 49.1 us
    pallas_call x12, Pallas kernels: 50.3 us -> 49.1 us  [call(): pl.pallas_call(kernel, in_specs=in_specs, out_specs=out_specs, out_shape=...]
  transfers between devices with their start and end apart: 12 -> 12, of which waited for: 3 -> 3; matrix products, arithmetic and copies ran while one was open for 0% -> 0% of each run, Pallas kernels for 38% -> 37%
where the time goes in v7:
time: 97.2 us; the launch traced here: 96.9 us
  Pallas kernels  49.1 us (51%)
  starting transfers between devices  19.7 us (20%)
  blocking collectives  17.1 us (18%)
  waiting for transfers between devices  9.95 us (10%)
  between operations  0.99 us (1%)
    pallas_call x12, Pallas kernels, call(): pl.pallas_call(kernel, in_specs=in_specs, out_specs=out_specs, out_shape=...  49.1 us
    all_to_all x1, blocking collectives, per_device(): left = lax.all_to_all(left_copies, 'dp', 0, 0, tiled=True)  17.1 us
    all_to_all x1, starting transfers between devices, per_device(): gathered = lax.all_to_all(left_parts, 'dp', 0, 0, tiled=True)  11.5 us
    ppermute x9, starting transfers between devices, exchange(): lax.ppermute(value, 'dp', to(step))  8.11 us
    all_to_all x1, waiting for transfers between devices, per_device(): gathered = lax.all_to_all(left_parts, 'dp', 0, 0, tiled=True)  7.92 us
    ppermute x9, waiting for transfers between devices, exchange(): lax.ppermute(value, 'dp', to(step))  2.03 us
  transfers between devices with their start and end apart: 12, of which 3 were waited for; matrix products, arithmetic and copies ran while one was open for 0% of the time, Pallas kernels for 37%

profile of v7, /device:TPU:0, one launch (start us, length us, event | category | flops | bytes accessed | tf_op | source)
XLA Modules:
  0.0 96.9 jit_solution(15972569787446105534)
XLA Ops:
  0.6 0.1 collective-permute-start
  0.7 7.8 %shard_map.85 = (f32[32,8192]{1,0:T(8,128)S(1)}, bf16[64,256]{1,0:T(8,128)(2,1)S(1)}) custom-call(f32[32,512]{1,0:T(8,128)} %bitcast.1, bf16[512,512]{1,0:T(8,128)(2,1)} %og.9, bf16[256,8192]{1,0:T(8,128)(2,1)} %acts.5, bf16[8192,512]{1,0:T(8,128)(2,1)} %error.5), custom_call_target="tpu_custom_call" | custom-call | flops 1207959552 | bytes 13631488 | tf_op jit(solution)/shard_map/pallas_call | solution.py:62
  8.6 0.0 copy-start
  8.6 2.2 %shard_map.86 = (bf16[64,32,128]{2,1,0:T(8,128)(2,1)}, bf16[256,8192]{1,0:T(8,128)(2,1)}, f32[8,128]{1,0:T(8,128)S(1)}) custom-call(bf16[64,256]{1,0:T(8,128)(2,1)S(1)} %get-tuple-element.27.pq2, bf16[256,8192]{1,0:T(8,128)(2,1)S(1)} %collective-permute-done.acts, f32[32,8192]{1,0:T(8,128)S(1)} %get-tuple-element.28.part), custom_call_target="tpu_custom_call" | custom-call | flops 402653184 | bytes 6291456 | tf_op jit(solution)/shard_map/pallas_call | solution.py:62
  10.8 11.5 %all-to-all-start = ((bf16[64,32,128]{2,1,0:T(8,128)(2,1)}), bf16[64,32,128]{2,1,0:T(8,128)(2,1)S(1)}, u32[]{:S(2)}, u32[]{:S(2)}) async-start(bf16[64,32,128]{2,1,0:T(8,128)(2,1)} %get-tuple-element.29), calls=%async_computation | async-start | bytes 1048576 | tf_op jit(solution)/shard_map/all_to_all | solution.py:408
  22.4 6.1 %shard_map.87 = (bf16[256,8192]{1,0:T(8,128)(2,1)}, f32[8,128]{1,0:T(8,128)S(1)}) custom-call(bf16[512,512]{1,0:T(8,128)(2,1)S(1)} %copy-done, bf16[8192,512]{1,0:T(8,128)(2,1)} %weight.5, f32[8,128]{1,0:T(8,128)S(1)} %get-tuple-element.30.after), custom_call_target="tpu_custom_call" | custom-call | flops 2147483648 | bytes 13631488 | tf_op jit(solution)/shard_map/pallas_call | solution.py:62
  28.4 7.9 %all-to-all-done.parts = bf16[64,32,128]{2,1,0:T(8,128)(2,1)S(1)} async-done(((bf16[64,32,128]{2,1,0:T(8,128)(2,1)}), bf16[64,32,128]{2,1,0:T(8,128)(2,1)S(1)}, u32[]{:S(2)}, u32[]{:S(2)}) %all-to-all-start) | async-done | bytes 524320 | tf_op jit(solution)/shard_map/all_to_all | solution.py:408
  36.4 0.1 shard_map.88
  36.5 17.1 %all_to_all.10.left.after = bf16[64,32,128]{2,1,0:T(8,128)(2,1)S(1)} all-to-all(bf16[64,32,128]{2,1,0:T(8,128)(2,1)S(1)} %shard_map.88), channel_id=1, replica_groups=mesh['dp'=64,'tensor'=2] {'dp'}, dimensions={0} | all-to-all | bytes 1048576 | tf_op jit(solution)/shard_map/all_to_all | solution.py:434
  53.6 0.0 collective-permute-start.7
  53.6 7.8 %shard_map.89 = (f32[32,512]{1,0:T(8,128)S(1)}, f32[32,32]{1,0:T(8,128)S(1)}, bf16[32,8192]{1,0:T(8,128)(2,1)}) custom-call(bf16[512,512]{1,0:T(8,128)(2,1)S(1)} %copy-done, bf16[64,32,128]{2,1,0:T(8,128)(2,1)S(1)} %all_to_all.10.left.after, bf16[256,8192]{1,0:T(8,128)(2,1)} %acts.5, bf16[256,8192]{1,0:T(8,128)(2,1)} %get-tuple-element.32.acts_oth.refs_2_, ...), custom_call_target="tpu_custom_call" | custom-call | flops 536870912 | bytes 17825792 | tf_op jit(solution)/shard_map/pallas_call | solution.py:62
  61.4 1.0 collective-permute-start.3
  62.4 1.7 %collective-permute-start.2 = (f32[32,512]{1,0:T(8,128)S(1)}, f32[32,512]{1,0:T(8,128)S(1)}, u32[]{:S(2)}, u32[]{:S(2)}) collective-permute-start(f32[32,512]{1,0:T(8,128)S(1)} %get-tuple-element.33.first), channel_id=1, source_target_pairs={{0,4},{2,6},{4,0},{6,2},{8,12},{10,14},{12,8},{14,10},{16,20},{18,... | collective-permute-start | bytes 196616 | tf_op jit(solution)/shard_map/ppermute | solution.py:343
  64.1 0.0 collective-permute-start.1
  64.1 4.4 %shard_map.90 = (f32[32,32]{1,0:T(8,128)S(1)}, f32[32,32]{1,0:T(8,128)S(1)}) custom-call(f32[32,32]{1,0:T(8,128)S(1)} %get-tuple-element.34.gram.refs_0_), custom_call_target="tpu_custom_call" | custom-call | flops 1073741824 | bytes 8192 | tf_op jit(solution)/shard_map/pallas_call | solution.py:62
  68.6 0.0 collective-permute-done.3.fourth
  68.6 0.0 collective-permute-done.2.third
  68.6 1.0 %collective-permute-done.1.second = f32[32,512]{1,0:T(8,128)S(1)} collective-permute-done((f32[32,512]{1,0:T(8,128)S(1)}, f32[32,512]{1,0:T(8,128)S(1)}, u32[]{:S(2)}, u32[]{:S(2)}) %collective-permute-start.1) | collective-permute-done | bytes 65568 | tf_op jit(solution)/shard_map/ppermute | solution.py:343
  69.6 1.1 %collective-permute-start.6 = (f32[32,512]{1,0:T(8,128)S(1)}, f32[32,512]{1,0:T(8,128)S(1)}, u32[]{:S(2)}, u32[]{:S(2)}) collective-permute-start(f32[32,512]{1,0:T(8,128)S(1)} %get-tuple-element.36.first), channel_id=1, source_target_pairs={{0,24},{2,26},{4,28},{6,30},{8,0},{10,2},{12,4},{14,6},{16,8},{18,... | collective-permute-start | bytes 196616 | tf_op jit(solution)/shard_map/ppermute | solution.py:343
  70.8 1.6 %collective-permute-start.5 = (f32[32,512]{1,0:T(8,128)S(1)}, f32[32,512]{1,0:T(8,128)S(1)}, u32[]{:S(2)}, u32[]{:S(2)}) collective-permute-start(f32[32,512]{1,0:T(8,128)S(1)} %get-tuple-element.36.first), channel_id=1, source_target_pairs={{0,16},{2,18},{4,20},{6,22},{8,24},{10,26},{12,28},{14,30},{16,0},... | collective-permute-start | bytes 196616 | tf_op jit(solution)/shard_map/ppermute | solution.py:343
  72.4 0.0 collective-permute-start.4
  72.4 0.0 collective-permute-done.7.received
  72.4 4.4 %shard_map.93 = (bf16[256,8192]{1,0:T(8,128)(2,1)}, f32[8,128]{1,0:T(8,128)S(1)}, f32[32,32]{1,0:T(8,128)S(1)}) custom-call(bf16[512,512]{1,0:T(8,128)(2,1)S(1)} %copy-done, bf16[8192,512]{1,0:T(8,128)(2,1)} %weight.5, bf16[256,8192]{1,0:T(8,128)(2,1)S(1)} %collective-permute-done.7.received, f32[8,128]{1,0:T(8,128)S(1)} %get-tuple-element.38.after, ...), custom_call_target="tpu_custom_call" | custom-call | flops 1073741824 | bytes 8388608 | tf_op jit(solution)/shard_map/pallas_call | solution.py:62
  76.8 0.0 collective-permute-done.6.fourth
  76.8 0.0 collective-permute-done.5.third
  76.8 1.0 %collective-permute-done.4.second = f32[32,512]{1,0:T(8,128)S(1)} collective-permute-done((f32[32,512]{1,0:T(8,128)S(1)}, f32[32,512]{1,0:T(8,128)S(1)}, u32[]{:S(2)}, u32[]{:S(2)}) %collective-permute-start.4) | collective-permute-done | bytes 65568 | tf_op jit(solution)/shard_map/ppermute | solution.py:343
  77.9 0.8 collective-permute-start.10
  78.7 1.4 %collective-permute-start.9 = (f32[32,512]{1,0:T(8,128)S(1)}, f32[32,512]{1,0:T(8,128)S(1)}, u32[]{:S(2)}, u32[]{:S(2)}) collective-permute-start(f32[32,512]{1,0:T(8,128)S(1)} %get-tuple-element.41.first), channel_id=1, source_target_pairs={{0,64},{2,66},{4,68},{6,70},{8,72},{10,74},{12,76},{14,78},{16,80}... | collective-permute-start | bytes 196616 | tf_op jit(solution)/shard_map/ppermute | solution.py:343
  80.1 0.5 collective-permute-start.8
  80.5 5.1 %shard_map.95 = (bf16[256,8192]{1,0:T(8,128)(2,1)}, f32[8,128]{1,0:T(8,128)}, bf16[512,1024]{1,0:T(8,128)(2,1)S(1)}, bf16[1024,512]{1,0:T(8,128)(2,1)S(1)}) custom-call(bf16[512,512]{1,0:T(8,128)(2,1)S(1)} %copy-done, bf16[8192,512]{1,0:T(8,128)(2,1)} %weight.5, ...), custom_call_target="tpu_custom_call", output_to_operand_aliasing={{0}: (4, {})} | custom-call | flops 1073741824 | bytes 8388608 | tf_op jit(solution)/shard_map/pallas_call | solution.py:62
  85.6 0.0 collective-permute-done.10.fourth
  85.7 11.1 %shard_map.96 = (bf16[8192,512]{1,0:T(8,128)(2,1)}, bf16[128,512]{1,0:T(8,128)(2,1)}) custom-call(f32[32,512]{1,0:T(8,128)S(1)} %get-tuple-element.41.first, f32[32,512]{1,0:T(8,128)S(1)} %collective-permute-done.8.second, f32[32,512]{1,0:T(8,128)S(1)} %collective-permute-done.9.third, f32[32,512]{1,0:T(8,128)S(1)} %collective-permute-done.10.fourth, ...), custom_call_target="tpu_custom_call" | custom-call | flops 5100273664 | bytes 26214400 | tf_op jit(solution)/shard_map/pallas_call | solution.py:62
  (11 shorter events, 0.1 us)
Async XLA Ops:
  0.6 8.0 %collective-permute-start = (bf16[256,8192]{1,0:T(8,128)(2,1)}, bf16[256,8192]{1,0:T(8,128)(2,1)S(1)}, u32[]{:S(2)}, u32[]{:S(2)}) collective-permute-start(bf16[256,8192]{1,0:T(8,128)(2,1)} %acts.5), channel_id=1, source_target_pairs={{0,1},{1,0},{2,3},{3,2},{4,5},{5,4},{6,7},{7,6},{8,9},{9,8},{10,11... | collective-permute-start | bytes 12582920 | tf_op jit(solution)/shard_map/ppermute | solution.py:379
  8.6 13.8 %copy-start = (bf16[512,512]{1,0:T(8,128)(2,1)S(1)}, bf16[512,512]{1,0:T(8,128)(2,1)}, u32[]{:S(2)}) copy-start(bf16[512,512]{1,0:T(8,128)(2,1)} %og.9) | copy-start | bytes 1572868
  10.8 25.5 %all-to-all-start = ((bf16[64,32,128]{2,1,0:T(8,128)(2,1)}), bf16[64,32,128]{2,1,0:T(8,128)(2,1)S(1)}, u32[]{:S(2)}, u32[]{:S(2)}) async-start(bf16[64,32,128]{2,1,0:T(8,128)(2,1)} %get-tuple-element.29), calls=%async_computation | async-start | bytes 1048576 | tf_op jit(solution)/shard_map/all_to_all | solution.py:408
  53.6 18.8 %collective-permute-start.7 = (bf16[256,8192]{1,0:T(8,128)(2,1)}, bf16[256,8192]{1,0:T(8,128)(2,1)S(1)}, u32[]{:S(2)}, u32[]{:S(2)}) collective-permute-start(bf16[256,8192]{1,0:T(8,128)(2,1)} %shard_map.92), channel_id=1, source_target_pairs={{0,1},{1,0},{2,3},{3,2},{4,5},{5,4},{6,7},{7,6},{8,9},{9,8},{10,11... | collective-permute-start | bytes 12582920 | tf_op jit(solution)/shard_map/ppermute | solution.py:445
  61.4 7.2 %collective-permute-start.3 = (f32[32,512]{1,0:T(8,128)S(1)}, f32[32,512]{1,0:T(8,128)S(1)}, u32[]{:S(2)}, u32[]{:S(2)}) collective-permute-start(f32[32,512]{1,0:T(8,128)S(1)} %get-tuple-element.33.first), channel_id=1, source_target_pairs={{0,6},{2,0},{4,2},{6,4},{8,14},{10,8},{12,10},{14,12},{16,22},{18,... | collective-permute-start | bytes 196616 | tf_op jit(solution)/shard_map/ppermute | solution.py:343
  62.4 6.2 %collective-permute-start.2 = (f32[32,512]{1,0:T(8,128)S(1)}, f32[32,512]{1,0:T(8,128)S(1)}, u32[]{:S(2)}, u32[]{:S(2)}) collective-permute-start(f32[32,512]{1,0:T(8,128)S(1)} %get-tuple-element.33.first), channel_id=1, source_target_pairs={{0,4},{2,6},{4,0},{6,2},{8,12},{10,14},{12,8},{14,10},{16,20},{18,... | collective-permute-start | bytes 196616 | tf_op jit(solution)/shard_map/ppermute | solution.py:343
  64.1 5.5 %collective-permute-start.1 = (f32[32,512]{1,0:T(8,128)S(1)}, f32[32,512]{1,0:T(8,128)S(1)}, u32[]{:S(2)}, u32[]{:S(2)}) collective-permute-start(f32[32,512]{1,0:T(8,128)S(1)} %get-tuple-element.33.first), channel_id=1, source_target_pairs={{0,2},{2,4},{4,6},{6,0},{8,10},{10,12},{12,14},{14,8},{16,18},{18,... | collective-permute-start | bytes 196616 | tf_op jit(solution)/shard_map/ppermute | solution.py:343
  69.6 7.2 %collective-permute-start.6 = (f32[32,512]{1,0:T(8,128)S(1)}, f32[32,512]{1,0:T(8,128)S(1)}, u32[]{:S(2)}, u32[]{:S(2)}) collective-permute-start(f32[32,512]{1,0:T(8,128)S(1)} %get-tuple-element.36.first), channel_id=1, source_target_pairs={{0,24},{2,26},{4,28},{6,30},{8,0},{10,2},{12,4},{14,6},{16,8},{18,... | collective-permute-start | bytes 196616 | tf_op jit(solution)/shard_map/ppermute | solution.py:343
  70.8 6.1 %collective-permute-start.5 = (f32[32,512]{1,0:T(8,128)S(1)}, f32[32,512]{1,0:T(8,128)S(1)}, u32[]{:S(2)}, u32[]{:S(2)}) collective-permute-start(f32[32,512]{1,0:T(8,128)S(1)} %get-tuple-element.36.first), channel_id=1, source_target_pairs={{0,16},{2,18},{4,20},{6,22},{8,24},{10,26},{12,28},{14,30},{16,0},... | collective-permute-start | bytes 196616 | tf_op jit(solution)/shard_map/ppermute | solution.py:343
  72.4 5.5 %collective-permute-start.4 = (f32[32,512]{1,0:T(8,128)S(1)}, f32[32,512]{1,0:T(8,128)S(1)}, u32[]{:S(2)}, u32[]{:S(2)}) collective-permute-start(f32[32,512]{1,0:T(8,128)S(1)} %get-tuple-element.36.first), channel_id=1, source_target_pairs={{0,8},{2,10},{4,12},{6,14},{8,16},{10,18},{12,20},{14,22},{16,24},... | collective-permute-start | bytes 196616 | tf_op jit(solution)/shard_map/ppermute | solution.py:343
  77.9 7.7 %collective-permute-start.10 = (f32[32,512]{1,0:T(8,128)S(1)}, f32[32,512]{1,0:T(8,128)S(1)}, u32[]{:S(2)}, u32[]{:S(2)}) collective-permute-start(f32[32,512]{1,0:T(8,128)S(1)} %get-tuple-element.41.first), channel_id=1, source_target_pairs={{0,96},{2,98},{4,100},{6,102},{8,104},{10,106},{12,108},{14,110},{... | collective-permute-start | bytes 196616 | tf_op jit(solution)/shard_map/ppermute | solution.py:343
  78.7 6.9 %collective-permute-start.9 = (f32[32,512]{1,0:T(8,128)S(1)}, f32[32,512]{1,0:T(8,128)S(1)}, u32[]{:S(2)}, u32[]{:S(2)}) collective-permute-start(f32[32,512]{1,0:T(8,128)S(1)} %get-tuple-element.41.first), channel_id=1, source_target_pairs={{0,64},{2,66},{4,68},{6,70},{8,72},{10,74},{12,76},{14,78},{16,80}... | collective-permute-start | bytes 196616 | tf_op jit(solution)/shard_map/ppermute | solution.py:343
  80.1 5.6 %collective-permute-start.8 = (f32[32,512]{1,0:T(8,128)S(1)}, f32[32,512]{1,0:T(8,128)S(1)}, u32[]{:S(2)}, u32[]{:S(2)}) collective-permute-start(f32[32,512]{1,0:T(8,128)S(1)} %get-tuple-element.41.first), channel_id=1, source_target_pairs={{0,32},{2,34},{4,36},{6,38},{8,40},{10,42},{12,44},{14,46},{16,48}... | collective-permute-start | bytes 196616 | tf_op jit(solution)/shard_map/ppermute | solution.py:343
  80.5 5.1 %copy-start.1 = (bf16[32,8192]{1,0:T(8,128)(2,1)S(1)}, bf16[32,8192]{1,0:T(8,128)(2,1)}, u32[]{:S(2)}) copy-start(bf16[32,8192]{1,0:T(8,128)(2,1)} %get-tuple-element.43.left_rows) | copy-start | bytes 1572868
  80.5 5.1 %copy-start.2 = (bf16[128,512]{1,0:T(8,128)(2,1)S(1)}, bf16[128,512]{1,0:T(8,128)(2,1)}, u32[]{:S(2)}) copy-start(bf16[128,512]{1,0:T(8,128)(2,1)} %momentum.1) | copy-start | bytes 393220
